TPU v7x, 256 devices: a whole 4x4x8 slice. The times are simulated.
256 devices in a mesh: batch: 32 (over x, z_lo, core), field: 8 (over y, z_hi).
Axes of the slice: x: 4, y: 4, z: 8 (z_hi: 2, z_lo: 4; z = z_hi * 4 + z_lo), core: 2. Of those that a mesh axis runs over, the one named last changes fastest.
Arguments:
- emb_tables: bfloat16 [256, 8192, 128], P(('field', 'batch')), may hold values from -3 to 3
- bag_ids: int32 [256, 6144, 8], P(('field', 'batch')), may hold values from 0 to 8191
- bag_lengths: int32 [256, 6144], P(('field', 'batch')), may hold values from 1 to 8
- table_widths: int32 [256], P(('field', 'batch')), may hold values from 16 to 128
- projection: bfloat16 [256, 128, 64], P('field'), may hold values from -0.5 to 0.5
- cross_u: bfloat16 [2, 512, 16384], P(None, 'batch', 'field'), may hold values from -0.25 to 0.25
- cross_v: bfloat16 [2, 512, 16384], P(None, 'batch', 'field'), may hold values from -0.046875 to 0.046875
- cross_bias: float32 [2, 16384], P(None, 'field'), may hold values from -3 to 3
- cotangent: bfloat16 [6144, 16384], P('batch', 'field'), may hold values from -6 to 6
Outputs:
- crossed: bfloat16 [6144, 16384], P('batch', 'field')
- grad_u: float32 [2, 512, 16384], P(None, 'batch', 'field')
- grad_v: float32 [2, 512, 16384], P(None, 'batch', 'field')
- grad_bias: float32 [2, 16384], P(None, ('field', 'batch'))
- grad_projection: float32 [256, 128, 64], P(('field', 'batch'))
- grad_pooled: bfloat16 [256, 6144, 128], P(('field', 'batch'))
All inputs are finite; a program needn't handle non-finite values.
Results may differ from a plain program's by a relative error of at most 0.039.
Values may be sent and summed in bfloat16 or wider, within the bound.
No kernel may reach another device: no remote copies, remote signals or barrier semaphores. Data moves between devices by JAX's collectives and lax.ppermute only.
A program may use at most 128 MiB of HBM per device.

v0:
```python
import jax
import jax.numpy as jnp
from jax import lax
from jax.sharding import PartitionSpec as P


def pool_bags(table_shard, bag_ids, bag_lengths, within):
    sample_count = bag_ids.shape[1]
    emb_width = table_shard.shape[2]
    summed = jnp.zeros((sample_count, emb_width), jnp.float32)
    for bag_place in range(bag_ids.shape[2]):
        looked_up = jnp.take(table_shard[0], bag_ids[0, :, bag_place], axis=0)
        active = (bag_lengths[0] > bag_place)[:, None]
        summed = summed + jnp.where(active, looked_up.astype(jnp.float32), 0.0)
    pooled_list = [jnp.where(within[0], summed, 0.0).astype(jnp.bfloat16)]
    return jnp.stack(pooled_list)


def field_total(partial_value):
    return lax.psum(partial_value.astype(jnp.bfloat16), "field").astype(jnp.float32)


def contract_rows(left_side, right_side):
    return lax.dot_general(
        left_side, right_side, (((0,), (0,)), ((), ())), preferred_element_type=jnp.float32
    )


def contract_cols(left_side, right_side):
    return lax.dot_general(
        left_side, right_side, (((1,), (1,)), ((), ())), preferred_element_type=jnp.float32
    )


def on_device(
    emb_tables,
    bag_ids,
    bag_lengths,
    table_widths,
    projection,
    cross_u,
    cross_v,
    cross_bias,
    cotangent,
):
    batch_count = lax.axis_size("batch")
    local_tables = emb_tables.shape[0]
    emb_width = emb_tables.shape[2]
    proj_width = projection.shape[2]
    samples = cotangent.shape[0]
    feature_width = cotangent.shape[1]
    field_tables = batch_count * local_tables
    layer_count = cross_u.shape[0]
    columns = lax.broadcasted_iota(jnp.int32, (1, 1, emb_width), 2)
    within = columns < table_widths[:, None, None]
    pooled = pool_bags(emb_tables, bag_ids, bag_lengths, within)
    outgoing = pooled.reshape(local_tables, batch_count, samples * emb_width)
    arrived = lax.all_to_all(outgoing, "batch", split_axis=1, concat_axis=0, tiled=True)
    received = arrived.reshape(field_tables, samples, emb_width)
    table_rows = jnp.einsum(
        "tse,tep->tsp", received, projection, preferred_element_type=jnp.float32
    ).astype(jnp.bfloat16)
    initial = jnp.transpose(table_rows, (1, 0, 2)).reshape(samples, feature_width)
    initial_wide = initial.astype(jnp.float32)
    current = initial
    layer_inputs = []
    rank_lows = []
    hiddens = []
    weights = []
    for layer_index in range(layer_count):
        full_u, full_v = (
            lax.all_gather(cross_u[layer_index], "batch", axis=0, tiled=True),
            lax.all_gather(cross_v[layer_index], "batch", axis=0, tiled=True),
        )
        rank_low = field_total(contract_cols(current, full_v)).astype(jnp.bfloat16)
        hidden = (
            jnp.dot(rank_low, full_u, preferred_element_type=jnp.float32)
            + cross_bias[layer_index][None, :]
        )
        layer_inputs.append(current)
        rank_lows.append(rank_low)
        hiddens.append(hidden)
        weights.append((full_u, full_v))
        current = (initial_wide * hidden + current.astype(jnp.float32)).astype(jnp.bfloat16)
    upstream = cotangent.astype(jnp.float32)
    base_grad = jnp.zeros_like(upstream)
    terms_list = []
    for layer_index in reversed(range(layer_count)):
        full_u, full_v = weights[layer_index]
        hidden_grad = (upstream * initial_wide).astype(jnp.bfloat16)
        base_grad = base_grad + upstream * hiddens[layer_index]
        u_term = contract_rows(rank_lows[layer_index], hidden_grad)
        bias_term = jnp.sum(hidden_grad, axis=0, dtype=jnp.float32)
        rank_grad = field_total(contract_cols(hidden_grad, full_u)).astype(jnp.bfloat16)
        v_term = contract_rows(rank_grad, layer_inputs[layer_index])
        upstream = upstream + jnp.dot(rank_grad, full_v, preferred_element_type=jnp.float32)
        terms_list.append(
            (
                lax.psum_scatter(
                    u_term.astype(jnp.bfloat16), "batch", scatter_dimension=0, tiled=True
                ).astype(jnp.float32),
                lax.psum_scatter(
                    v_term.astype(jnp.bfloat16), "batch", scatter_dimension=0, tiled=True
                ).astype(jnp.float32),
                lax.psum_scatter(
                    bias_term.astype(jnp.bfloat16), "batch", scatter_dimension=0, tiled=True
                ).astype(jnp.float32),
            )
        )
    terms_list = terms_list[::-1]
    stack_u = jnp.stack([member[0] for member in terms_list])
    stack_v = jnp.stack([member[1] for member in terms_list])
    stack_bias = jnp.stack([member[2] for member in terms_list])
    input_grad = (upstream + base_grad).astype(jnp.bfloat16)
    grad_rows = jnp.transpose(input_grad.reshape(samples, field_tables, proj_width), (1, 0, 2))
    sent_back = jnp.einsum(
        "tsp,tep->tse", grad_rows, projection, preferred_element_type=jnp.float32
    ).astype(jnp.bfloat16)
    returned = lax.all_to_all(
        sent_back.reshape(field_tables, 1, samples * emb_width),
        "batch",
        split_axis=0,
        concat_axis=1,
        tiled=True,
    )
    grad_pooled = jnp.where(
        within, returned.reshape(local_tables, batch_count * samples, emb_width), 0.0
    )
    proj_term = jnp.einsum("tse,tsp->tep", received, grad_rows, preferred_element_type=jnp.float32)
    grad_projection = lax.psum_scatter(
        proj_term.astype(jnp.bfloat16), "batch", scatter_dimension=0, tiled=True
    ).astype(jnp.float32)
    return (current, stack_u, stack_v, stack_bias, grad_projection, grad_pooled)


def solution(mesh):
    return jax.shard_map(
        on_device,
        mesh=mesh,
        in_specs=(
            P(("field", "batch"), None, None),
            P(("field", "batch"), None, None),
            P(("field", "batch"), None),
            P(("field", "batch")),
            P("field", None, None),
            P(None, "batch", "field"),
            P(None, "batch", "field"),
            P(None, "field"),
            P("batch", "field"),
        ),
        out_specs=(
            P("batch", "field"),
            P(None, "batch", "field"),
            P(None, "batch", "field"),
            P(None, ("field", "batch")),
            P(("field", "batch"), None, None),
            P(("field", "batch"), None, None),
        ),
        check_vma=False,
    )
```

profile of v0, /device:TPU:1, one launch (start us, length us, event | category | flops | bytes accessed | tf_op | source)
XLA Modules:
  0.0 1337.2 jit_solution(7361567453015076011)
XLA Ops:
  7.2 1.7 fusion.46
  9.0 1.5 fusion.47
  10.5 2.0 fusion.45
  12.6 22.3 %gather_fusion.7 = bf16[6144,128]{1,0:T(8,128)(2,1)} fusion(bf16[8192,128]{1,0:T(8,128)(2,1)S(1)} %bitcast.94, s32[6144]{0:T(1024)S(1)} %fusion.39), kind=kCustom, calls=%fused_computation.7.clone | custom fusion | bytes 3170304 | tf_op jit(solution)/shard_map/jit(_take)/gather | solution.py:12
  34.9 22.1 %gather_fusion.6 = bf16[6144,128]{1,0:T(8,128)(2,1)} fusion(bf16[8192,128]{1,0:T(8,128)(2,1)S(1)} %bitcast.93, s32[6144]{0:T(1024)S(1)} %fusion.38), kind=kCustom, calls=%fused_computation.6.clone | custom fusion | bytes 3170304 | tf_op jit(solution)/shard_map/jit(_take)/gather | solution.py:12
  56.9 22.0 %gather_fusion.5 = bf16[6144,128]{1,0:T(8,128)(2,1)} fusion(bf16[8192,128]{1,0:T(8,128)(2,1)S(1)} %bitcast.92, s32[6144]{0:T(1024)S(1)} %fusion.37), kind=kCustom, calls=%fused_computation.5.clone | custom fusion | bytes 3170304 | tf_op jit(solution)/shard_map/jit(_take)/gather | solution.py:12
  79.0 22.0 %gather_fusion.4 = bf16[6144,128]{1,0:T(8,128)(2,1)} fusion(bf16[8192,128]{1,0:T(8,128)(2,1)S(1)} %bitcast.91, s32[6144]{0:T(1024)S(1)} %fusion.36), kind=kCustom, calls=%fused_computation.4.clone | custom fusion | bytes 3170304 | tf_op jit(solution)/shard_map/jit(_take)/gather | solution.py:12
  101.0 22.1 %gather_fusion.3 = bf16[6144,128]{1,0:T(8,128)(2,1)} fusion(bf16[8192,128]{1,0:T(8,128)(2,1)S(1)} %bitcast.90, s32[6144]{0:T(1024)S(1)} %fusion.35), kind=kCustom, calls=%fused_computation.3.clone | custom fusion | bytes 3170304 | tf_op jit(solution)/shard_map/jit(_take)/gather | solution.py:12
  123.1 22.1 %gather_fusion.2 = bf16[6144,128]{1,0:T(8,128)(2,1)} fusion(bf16[8192,128]{1,0:T(8,128)(2,1)S(1)} %bitcast.89, s32[6144]{0:T(1024)S(1)} %fusion.34), kind=kCustom, calls=%fused_computation.2.clone | custom fusion | bytes 3170304 | tf_op jit(solution)/shard_map/jit(_take)/gather | solution.py:12
  145.2 22.1 %gather_fusion.1 = bf16[6144,128]{1,0:T(8,128)(2,1)} fusion(bf16[8192,128]{1,0:T(8,128)(2,1)S(1)} %bitcast.88, s32[6144]{0:T(1024)S(1)} %fusion.33), kind=kCustom, calls=%fused_computation.1.clone | custom fusion | bytes 3170304 | tf_op jit(solution)/shard_map/jit(_take)/gather | solution.py:12
  167.3 22.1 %gather_fusion = bf16[6144,128]{1,0:T(8,128)(2,1)} fusion(bf16[8192,128]{1,0:T(8,128)(2,1)S(1)} %bitcast.87, s32[6144]{0:T(1024)S(1)} %fusion.32), kind=kCustom, calls=%fused_computation.clone | custom fusion | bytes 3170304 | tf_op jit(solution)/shard_map/jit(_take)/gather | solution.py:12
  190.7 17.8 %select_convert_fusion = bf16[6144,128]{1,0:T(8,128)(2,1)} fusion(bf16[6144,128]{1,0:T(8,128)(2,1)} %gather_fusion.7, bf16[6144,128]{1,0:T(8,128)(2,1)} %gather_fusion.6, bf16[6144,128]{1,0:T(8,128)(2,1)} %gather_fusion.5, bf16[6144,128]{1,0:T(8,128)(2,1)} %gather_fusion.4, bf16[6144,128]{1,0:T(8,128)(2,1)} %gather_fusion.3, ...), kind=kLoop, calls=%fused_computation.13 | loop fusion | flops 25952256 | bytes 14254208 | tf_op jit(solution)/shard_map/convert_element_type | solution.py:15
  208.5 7.5 reshape_stack.4
  216.5 11.4 reduce.21
  227.9 3.3 reshape.253
  231.2 10.1 all-to-all-start
  241.3 0.7 all-gather.11.cloned.1.call-update
  242.0 42.0 %all-to-all-done = bf16[32,2,12288]{2,1,0:T(2,128)(2,1)} async-done(((bf16[32,2,12288]{2,1,0:T(2,128)(2,1)}), bf16[32,2,12288]{2,1,0:T(2,128)(2,1)}, u32[]{:S(2)}, u32[]{:S(2)}) %all-to-all-start) | async-done | bytes 1572896 | tf_op jit(solution)/shard_map/all_to_all | solution.py:58
  284.0 8.6 reshape.254
  292.6 10.4 bitcast_reduce_fusion
  303.0 1.8 copy.27
  304.9 2.2 convolution_convert_fusion.5
  307.0 1.6 copy.24
  308.7 3.5 fusion.20
  312.2 3.1 fusion.29
  316.1 102.5 %all-reduce.10.cloned.1.call-done = (bf16[192,512]{1,0:T(8,128)(2,1)}, bf16[192,512]{1,0:T(8,128)(2,1)}) async-done(((bf16[192,512]{1,0:T(8,128)(2,1)}, bf16[192,512]{1,0:T(8,128)(2,1)}), (bf16[192,512]{1,0:T(8,128)(2,1)}, bf16[192,512]{1,0:T(8,128)(2,1)})) %all-reduce.10.cloned.1.call-update) | async-done | bytes 393232 | tf_op jit(solution)/shard_map/psum | solution.py:20
  418.6 3.8 fusion.15
  422.5 59.3 %all-gather.13.cloned.1.call-done = bf16[1,512,2048]{2,1,0:T(8,128)(2,1)} async-done(((bf16[1,16,2048]{2,1,0:T(8,128)(2,1)}), bf16[1,512,2048]{2,1,0:T(8,128)(2,1)}) %all-gather.13.cloned.1.call-update) | async-done | bytes 2097168 | tf_op jit(solution)/shard_map/all_gather | solution.py:73
  481.8 3.5 fusion.26
  485.3 2.0 fusion.43
  487.4 0.9 copy-done.7
  488.2 1.5 fusion.23
  489.8 102.6 %all-reduce.8.cloned.1.call-done = (bf16[192,512]{1,0:T(8,128)(2,1)}, bf16[192,512]{1,0:T(8,128)(2,1)}) async-done(((bf16[192,512]{1,0:T(8,128)(2,1)}, bf16[192,512]{1,0:T(8,128)(2,1)}), (bf16[192,512]{1,0:T(8,128)(2,1)}, bf16[192,512]{1,0:T(8,128)(2,1)})) %all-reduce.8.cloned.1.call-update) | async-done | bytes 393232 | tf_op jit(solution)/shard_map/psum | solution.py:20
  592.5 3.6 fusion.17
  596.1 1.8 fusion.1
  597.9 2.2 copy.25
  600.1 2.8 convolution_convert_fusion.6
  602.9 3.2 convolution_convert_fusion.3
  606.2 0.9 copy-done.14
  607.1 2.1 convolution_convert_fusion.2
  609.2 1.1 copy-done.3
  610.3 2.1 convolution_convert_fusion
  612.4 1.2 copy-done.4
  613.7 1.8 convolution_convert_fusion.4
  615.5 7.5 reshape.240
  623.0 11.4 reduce.22
  634.4 3.2 reshape.255
  637.6 10.8 all-to-all-start.1
  648.4 3.3 convolution_convert_fusion.1
  651.8 0.6 copy-done.20
  652.4 0.6 dynamic-slice
  653.7 87.6 %all-reduce.2 = (bf16[2048]{0:T(1024)(128)(2,1)S(1)}, bf16[2048]{0:T(1024)(128)(2,1)S(1)}) all-reduce(bf16[2048]{0:T(1024)(128)(2,1)S(1)} %get-tuple-element.23, bf16[2048]{0:T(1024)(128)(2,1)S(1)} %get-tuple-element.21), channel_id=11, replica_groups=mesh['batch'=32,'field'=8] {'batch'}, use_global_device_ids=true, to_apply=%region_11.13.clone | all-reduce | flops 4096 | bytes 16384
  742.1 2.0 reduce-scatter.14.cloned.1.call-done
  744.0 1.3 convert_element_type.140
  745.4 8.2 reshape.256
  753.6 10.8 reduce.11
  764.4 2.9 reshape.147
  767.3 2.7 broadcast_select_fusion
  769.9 120.4 %reduce-scatter.6.cloned.1.call-done = bf16[16,2048]{1,0:T(8,128)(2,1)} async-done(((bf16[512,2048]{1,0:T(8,128)(2,1)}), bf16[16,2048]{1,0:T(8,128)(2,1)}) %reduce-scatter.6.cloned.1.call-update) | async-done | bytes 65552 | tf_op jit(solution)/shard_map/reduce_scatter | solution.py:99
  890.3 145.6 %reduce-scatter.8.cloned.1.call-done = bf16[16,2048]{1,0:T(8,128)(2,1)} async-done(((bf16[512,2048]{1,0:T(8,128)(2,1)}), bf16[16,2048]{1,0:T(8,128)(2,1)}) %reduce-scatter.8.cloned.1.call-update) | async-done | bytes 65552 | tf_op jit(solution)/shard_map/reduce_scatter | solution.py:99
  1035.9 1.6 maximum_convert_fusion
  1037.5 144.9 %reduce-scatter.12.cloned.1.call-done = bf16[16,2048]{1,0:T(8,128)(2,1)} async-done(((bf16[512,2048]{1,0:T(8,128)(2,1)}), bf16[16,2048]{1,0:T(8,128)(2,1)}) %reduce-scatter.12.cloned.1.call-update) | async-done | bytes 65552 | tf_op jit(solution)/shard_map/reduce_scatter | solution.py:102
  1182.4 146.2 %reduce-scatter.10.cloned.1.call-done = bf16[16,2048]{1,0:T(8,128)(2,1)} async-done(((bf16[512,2048]{1,0:T(8,128)(2,1)}), bf16[16,2048]{1,0:T(8,128)(2,1)}) %reduce-scatter.10.cloned.1.call-update) | async-done | bytes 65552 | tf_op jit(solution)/shard_map/reduce_scatter | solution.py:102
  1328.7 1.6 maximum_convert_fusion.1
  (81 shorter events, 3.4 us)
Async XLA Ops:
  7.2 5.5 copy-start
  7.2 301.5 %all-gather.9.cloned.1.call-start = ((), (), s32[]{:S(2)}) async-start(), calls=%async_computation.12 | async-start | bytes 2162688 | tf_op jit(solution)/shard_map/all_gather | solution.py:73
  8.9 303.3 %all-gather.15.cloned.1.call-start = ((), (), s32[]{:S(2)}) async-start(), calls=%async_computation.15 | async-start | bytes 2162688 | tf_op jit(solution)/shard_map/all_gather | solution.py:72
  167.3 22.7 %copy-start.18 = (s32[1,6144]{1,0:T(1,128)S(1)}, s32[1,6144]{1,0:T(1,128)}, u32[]{:S(2)}) copy-start(s32[1,6144]{1,0:T(1,128)} %param.13) | copy-start | bytes 73732
  231.2 52.8 %all-to-all-start = ((bf16[32,2,12288]{2,1,0:T(2,128)(2,1)}), bf16[32,2,12288]{2,1,0:T(2,128)(2,1)}, u32[]{:S(2)}, u32[]{:S(2)}) async-start(bf16[32,2,12288]{2,1,0:T(2,128)(2,1)} %reshape.253), calls=%async_computation | async-start | bytes 3145728 | tf_op jit(solution)/shard_map/all_to_all | solution.py:58
  241.3 74.8 %all-gather.11.cloned.1.call-start = ((), (), s32[]{:S(2)}) async-start(), calls=%async_computation.13 | async-start | bytes 2162688 | tf_op jit(solution)/shard_map/all_gather | solution.py:72
  242.0 176.6 %all-reduce.10.cloned.1.call-start = ((), (), s32[]{:S(2)}) async-start(), calls=%async_computation.17 | async-start | bytes 786432 | tf_op jit(solution)/shard_map/psum | solution.py:20
  303.0 1.8 copy-start.11
  308.7 3.6 copy-start.2
  312.2 3.8 copy-start.19
  315.4 166.4 %all-gather.13.cloned.1.call-start = ((), (), s32[]{:S(2)}) async-start(), calls=%async_computation.14 | async-start | bytes 2162688 | tf_op jit(solution)/shard_map/all_gather | solution.py:73
  316.0 276.5 %all-reduce.8.cloned.1.call-start = ((), (), s32[]{:S(2)}) async-start(), calls=%async_computation.16 | async-start | bytes 786432 | tf_op jit(solution)/shard_map/psum | solution.py:20
  422.5 62.9 %copy-start.13 = (bf16[192,512]{1,0:T(8,128)(2,1)S(1)}, bf16[192,512]{1,0:T(8,128)(2,1)}, u32[]{:S(2)}) copy-start(bf16[192,512]{1,0:T(8,128)(2,1)} %get-tuple-element.20) | copy-start | bytes 589828
  481.8 3.5 copy-start.6
  485.3 2.9 copy-start.5
  487.4 0.9 copy-start.7
  489.8 254.2 %reduce-scatter.14.cloned.1.call-start = ((), (), s32[]{:S(2)}) async-start(), calls=%async_computation.11 | async-start | bytes 540672 | tf_op jit(solution)/shard_map/reduce_scatter | solution.py:130
  592.5 3.6 copy-start.8
  592.5 3.6 copy-start.9
  592.5 3.6 copy-start.10
  592.5 3.6 copy-start.16
  600.1 2.9 copy-start.15
  602.9 287.4 %reduce-scatter.6.cloned.1.call-start = ((), (), s32[]{:S(2)}) async-start(), calls=%async_computation.7 | async-start | bytes 2162688 | tf_op jit(solution)/shard_map/reduce_scatter | solution.py:99
  606.2 0.9 copy-start.14
  606.2 429.7 %reduce-scatter.8.cloned.1.call-start = ((), (), s32[]{:S(2)}) async-start(), calls=%async_computation.8 | async-start | bytes 2162688 | tf_op jit(solution)/shard_map/reduce_scatter | solution.py:99
  609.1 1.1 copy-start.3
  609.2 573.3 %reduce-scatter.12.cloned.1.call-start = ((), (), s32[]{:S(2)}) async-start(), calls=%async_computation.10 | async-start | bytes 2162688 | tf_op jit(solution)/shard_map/reduce_scatter | solution.py:102
  612.3 1.2 copy-start.4
  612.3 1.4 copy-start.12
  637.6 10.8 copy-start.17
  637.6 107.8 %all-to-all-start.1 = ((bf16[32,2,12288]{2,1,0:T(2,128)(2,1)}), bf16[32,2,12288]{2,1,0:T(2,128)(2,1)}, u32[]{:S(2)}, u32[]{:S(2)}) async-start(bf16[32,2,12288]{2,1,0:T(2,128)(2,1)} %reshape.255), calls=%async_computation.6 | async-start | bytes 3145728 | tf_op jit(solution)/shard_map/all_to_all | solution.py:119
  648.4 680.3 %reduce-scatter.10.cloned.1.call-start = ((), (), s32[]{:S(2)}) async-start(), calls=%async_computation.9 | async-start | bytes 2162688 | tf_op jit(solution)/shard_map/reduce_scatter | solution.py:102
  651.8 0.7 copy-start.20
  764.4 565.9 %copy-start.1 = (bf16[1,8192,128]{2,1,0:T(8,128)(2,1)S(1)}, bf16[1,8192,128]{2,1,0:T(8,128)(2,1)}, u32[]{:S(2)}) copy-start(bf16[1,8192,128]{2,1,0:T(8,128)(2,1)} %param.11) | copy-start | bytes 6291460
Sparse Core Ops, SparseCore 0:
  10.4 64.3 all-gather.8
  77.2 59.1 all-gather.14
  244.0 65.9 all-gather.10
  315.5 103.0 all-reduce.9
  421.1 60.7 all-gather.12
  489.9 102.4 all-reduce.7
  603.0 140.9 reduce-scatter.13
  746.7 143.5 reduce-scatter.5
  892.8 143.0 reduce-scatter.7
  1038.4 143.9 reduce-scatter.11
  1185.0 143.6 reduce-scatter.9
where the time goes:
time: 1350 us; the launch traced here: 1340 us
  waiting for transfers between devices  867 us (64%)
  local copies, waits for them, and re-layouts  245 us (18%)
  blocking collectives  87.6 us (6%)
  other arithmetic  59.9 us (4%)
  matrix products  40.3 us (3%)
  starting transfers between devices  21.3 us (2%)
  between operations  15.9 us (1%)
    reduce_scatter x2, waiting for transfers between devices, on_device(): lax.psum_scatter(v_term.astype(jnp.bfloat16), 'batch', scatter_dimension=...  291 us
    reduce_scatter x2, waiting for transfers between devices, on_device(): lax.psum_scatter(u_term.astype(jnp.bfloat16), 'batch', scatter_dimension=...  266 us
    psum x2, waiting for transfers between devices, field_total(): lax.psum(partial_value.astype(jnp.bfloat16), 'field').astype(jnp.float32)  205 us
    gather x8, local copies, waits for them, and re-layouts, pool_bags(): looked_up = jnp.take(table_shard[0], bag_ids[0, :, bag_place], axis=0)  177 us
    unnamed x1, blocking collectives  87.6 us
    all_gather x2, waiting for transfers between devices, on_device(): lax.all_gather(cross_v[layer_index], 'batch', axis=0, tiled=True)  59.4 us
    all_to_all x1, waiting for transfers between devices, on_device(): lax.all_to_all(outgoing, 'batch', split_axis=1, concat_axis=0, tiled=True)  42 us
    unnamed x49, local copies, waits for them, and re-layouts  31 us
  transfers between devices with their start and end apart: 13, of which 9 were waited for; matrix products, arithmetic and copies ran while one was open for 24% of the time, Pallas kernels for 0%

commit v1 on v0

v1 whole, which is shorter than its diff:
```python
import functools

import jax
import jax.numpy as jnp
from jax import lax
from jax.experimental import pallas as pl
from jax.experimental.pallas import tpu as pltpu
from jax.sharding import PartitionSpec as P

BF16 = jnp.bfloat16
F32 = jnp.float32
MIB = 2**20

X_SIZE, Z_SIZE, CORES = 4, 4, 2
Y_SIZE, HALVES = 4, 2

ROWS, EMB, PROJ, BAG = 8192, 128, 64, 8
SAMPLES, FEATURES, RANK = 192, 2048, 512
FIELD_TABLES = 32
HALF = SAMPLES // 2
SHARE = RANK // FIELD_TABLES
TOKENS = SAMPLES * FIELD_TABLES
BACK_ROWS = HALF + 16
FEATURE_BLOCK = 256
POOL_CHUNK = 768
POOL_UNROLL = 32
QUARTER = 2 * SAMPLES // Y_SIZE

AT_BATCH, AT_X, AT_Z, AT_CORE, AT_Y, AT_WIDTH = range(6)
U0, U1, V0, V1 = range(4)


def params():
    return pltpu.CompilerParams(vmem_limit_bytes=48 * MIB)


def cost(flops, moved):
    return pl.CostEstimate(flops=flops, bytes_accessed=moved, transcendentals=0)


def dot(left, right, left_dim, right_dim):
    return lax.dot_general(
        left, right, (((left_dim,), (right_dim,)), ((), ())), preferred_element_type=F32
    )


def masked_projection(proj_ref, width):
    columns = lax.broadcasted_iota(jnp.int32, (PROJ, EMB), 1)
    return jnp.where(columns < width, proj_ref[0].astype(F32), 0.0).astype(BF16)


def pool_kernel(at, ids, table, proj, pooled, sent, wide_table, summed):
    @pl.when(pl.program_id(0) == 0)
    def _():
        within = lax.broadcasted_iota(jnp.int32, (256, EMB), 1) < at[AT_WIDTH]

        @pl.loop(0, ROWS // 256)
        def _(part):
            rows = pl.ds(pl.multiple_of(part * 256, 256), 256)
            wide_table[rows, :] = jnp.where(within, table[rows, :].astype(F32), 0.0)

        wide_table[ROWS : ROWS + 8, :] = jnp.zeros((8, EMB), F32)

    groups = 128 // POOL_UNROLL

    @pl.loop(0, POOL_CHUNK // POOL_UNROLL)
    def _(group):
        first = group * POOL_UNROLL
        base = (group // groups) * (128 * BAG) + (group % groups) * POOL_UNROLL
        for step in range(POOL_UNROLL):
            rows = [wide_table[pl.ds(ids[base + (place * 128 + step)], 1), :] for place in range(BAG)]
            summed[pl.ds(first + step, 1), :] = (
                (rows[0] + rows[1]) + (rows[2] + rows[3])
            ) + ((rows[4] + rows[5]) + (rows[6] + rows[7]))

    low = summed[...].astype(BF16)
    pooled[...] = low
    factor = proj[0]
    none = jnp.zeros_like(factor)
    both = jnp.concatenate(
        [jnp.concatenate([factor, none], axis=1), jnp.concatenate([none, factor], axis=1)], axis=0
    )
    for block in range(POOL_CHUNK // SAMPLES):
        start = block * SAMPLES
        pair = jnp.concatenate(
            [low[start : start + HALF], low[start + HALF : start + SAMPLES]], axis=1
        )
        sent[block] = dot(pair, both, 1, 1).astype(BF16)


def pool(at, ids, table, proj):
    blocks = POOL_CHUNK // SAMPLES
    return pl.pallas_call(
        pool_kernel,
        grid_spec=pltpu.PrefetchScalarGridSpec(
            num_scalar_prefetch=1,
            grid=(TOKENS // POOL_CHUNK,),
            in_specs=[
                pl.BlockSpec((POOL_CHUNK * BAG,), lambda i, at: (i,), memory_space=pltpu.SMEM),
                pl.BlockSpec((ROWS, EMB), lambda i, at: (0, 0)),
                pl.BlockSpec((1, PROJ, EMB), lambda i, at: (at[AT_BATCH], 0, 0)),
            ],
            out_specs=[
                pl.BlockSpec((POOL_CHUNK, EMB), lambda i, at: (i, 0)),
                pl.BlockSpec((blocks, HALF, EMB), lambda i, at: (i, 0, 0)),
            ],
            scratch_shapes=[pltpu.VMEM((ROWS + 8, EMB), F32), pltpu.VMEM((POOL_CHUNK, EMB), F32)],
        ),
        out_shape=[
            jax.ShapeDtypeStruct((TOKENS, EMB), BF16),
            jax.ShapeDtypeStruct((FIELD_TABLES, HALF, EMB), BF16),
        ],
        compiler_params=params(),
        cost_estimate=cost(2 * 10**9, 100 * MIB),
    )(at, ids, table, proj)


def write_quarters(at, total, parts):
    for shift, part in enumerate(parts):
        place = lax.rem(at[AT_Y] + shift, Y_SIZE)
        part[...] = total[pl.ds(pl.multiple_of(place * QUARTER, QUARTER), QUARTER), :].astype(BF16)


def read_quarters(at, parts, whole):
    for shift, part in enumerate(parts):
        place = lax.rem(at[AT_Y] + Y_SIZE - shift, Y_SIZE)
        whole[pl.ds(pl.multiple_of(place * QUARTER, QUARTER), QUARTER), :] = part[...]


def weight(ref):
    return ref[...].reshape(RANK, FEATURE_BLOCK)


def first_kernel(at, recv, cot, v0, u1, x0_out, hg_out, bias_out, *rest):
    parts, total = rest[:4], rest[4]
    step = pl.program_id(0)
    columns = []
    for pair in range(FEATURE_BLOCK // EMB):
        left, right = recv[2 * pair], recv[2 * pair + 1]
        top = jnp.concatenate([left[:, :PROJ], right[:, :PROJ]], axis=1)
        bottom = jnp.concatenate([left[:, PROJ:], right[:, PROJ:]], axis=1)
        columns.append(jnp.concatenate([top, bottom], axis=0))
    x0 = jnp.concatenate(columns, axis=1)
    hg = (cot[...].astype(F32) * x0.astype(F32)).astype(BF16)
    x0_out[...] = x0
    hg_out[...] = hg
    bias_out[...] = jnp.sum(hg.astype(F32), axis=0, keepdims=True)
    rank = dot(x0, weight(v0), 1, 1)
    rank_grad = dot(hg, weight(u1), 1, 1)

    @pl.when(step == 0)
    def _():
        total[:SAMPLES, :] = rank
        total[SAMPLES:, :] = rank_grad

    @pl.when(step > 0)
    def _():
        total[:SAMPLES, :] += rank
        total[SAMPLES:, :] += rank_grad

    @pl.when(step == pl.num_programs(0) - 1)
    def _():
        write_quarters(at, total, parts)


def feature_spec(rows):
    return pl.BlockSpec((rows, FEATURE_BLOCK), lambda j, at: (0, j))


def weight_spec(which):
    return pl.BlockSpec(
        (FIELD_TABLES, 1, SHARE, FEATURE_BLOCK), lambda j, at: (0, which, 0, j)
    )


def whole_spec(*shape):
    return pl.BlockSpec(shape, lambda j, at: (0,) * len(shape))


QUARTER_SPECS = [whole_spec(QUARTER, RANK) for _ in range(Y_SIZE)]
QUARTER_SHAPES = [jax.ShapeDtypeStruct((QUARTER, RANK), BF16) for _ in range(Y_SIZE)]
FEATURE_STEPS = FEATURES // FEATURE_BLOCK
TABLES_STEP = FEATURE_BLOCK // PROJ


def first(at, recv, cot, weights):
    return pl.pallas_call(
        first_kernel,
        grid_spec=pltpu.PrefetchScalarGridSpec(
            num_scalar_prefetch=1,
            grid=(FEATURE_STEPS,),
            in_specs=[
                pl.BlockSpec((TABLES_STEP, HALF, EMB), lambda j, at: (j, 0, 0)),
                feature_spec(SAMPLES),
                weight_spec(V0),
                weight_spec(U1),
            ],
            out_specs=[feature_spec(SAMPLES), feature_spec(SAMPLES), feature_spec(1)] + QUARTER_SPECS,
            scratch_shapes=[pltpu.VMEM((2 * SAMPLES, RANK), F32)],
        ),
        out_shape=[
            jax.ShapeDtypeStruct((SAMPLES, FEATURES), BF16),
            jax.ShapeDtypeStruct((SAMPLES, FEATURES), BF16),
            jax.ShapeDtypeStruct((1, FEATURES), F32),
        ]
        + QUARTER_SHAPES,
        compiler_params=params(),
        cost_estimate=cost(10**9, 8 * MIB),
    )(at, recv, cot, weights, weights)


def second_kernel(at, q0, q1, q2, q3, x0_ref, cot, u0_ref, v1_ref, bias, x1_out, hg_out, base_out, bias_out, *rest):
    parts, total, ranks = rest[:4], rest[4], rest[5]
    step = pl.program_id(0)

    @pl.when(step == 0)
    def _():
        read_quarters(at, (q0, q1, q2, q3), ranks)

    u0, v1 = weight(u0_ref), weight(v1_ref)
    x0 = x0_ref[...].astype(F32)
    hidden = dot(ranks[:SAMPLES, :], u0, 1, 0) + bias[0:1, :]
    upstream = cot[...].astype(F32) + dot(ranks[SAMPLES:, :], v1, 1, 0)
    x1 = (x0 * hidden + x0).astype(BF16)
    hg = (upstream * x0).astype(BF16)
    x1_out[...] = x1
    hg_out[...] = hg
    base_out[...] = upstream + upstream * hidden
    bias_out[...] = jnp.sum(hg.astype(F32), axis=0, keepdims=True)
    rank = dot(x1, v1, 1, 1)
    rank_grad = dot(hg, u0, 1, 1)

    @pl.when(step == 0)
    def _():
        total[:SAMPLES, :] = rank
        total[SAMPLES:, :] = rank_grad

    @pl.when(step > 0)
    def _():
        total[:SAMPLES, :] += rank
        total[SAMPLES:, :] += rank_grad

    @pl.when(step == pl.num_programs(0) - 1)
    def _():
        write_quarters(at, total, parts)


def second(at, quarters, x0, cot, weights, bias):
    return pl.pallas_call(
        second_kernel,
        grid_spec=pltpu.PrefetchScalarGridSpec(
            num_scalar_prefetch=1,
            grid=(FEATURE_STEPS,),
            in_specs=QUARTER_SPECS
            + [feature_spec(SAMPLES), feature_spec(SAMPLES), weight_spec(U0), weight_spec(V1), feature_spec(2)],
            out_specs=[feature_spec(SAMPLES), feature_spec(SAMPLES), feature_spec(SAMPLES), feature_spec(1)]
            + QUARTER_SPECS,
            scratch_shapes=[pltpu.VMEM((2 * SAMPLES, RANK), F32), pltpu.VMEM((2 * SAMPLES, RANK), BF16)],
        ),
        out_shape=[
            jax.ShapeDtypeStruct((SAMPLES, FEATURES), BF16),
            jax.ShapeDtypeStruct((SAMPLES, FEATURES), BF16),
            jax.ShapeDtypeStruct((SAMPLES, FEATURES), F32),
            jax.ShapeDtypeStruct((1, FEATURES), F32),
        ]
        + QUARTER_SHAPES,
        compiler_params=params(),
        cost_estimate=cost(2 * 10**9, 10 * MIB),
    )(at, *quarters, x0, cot, weights, weights, bias)


def third_kernel(at, q0, q1, q2, q3, x0_ref, x1_ref, cot, base, u1_ref, v0_ref, bias, sum0, sum1, crossed, back, ranks):
    @pl.when(pl.program_id(0) == 0)
    def _():
        read_quarters(at, (q0, q1, q2, q3), ranks)

    hidden = dot(ranks[:SAMPLES, :], weight(u1_ref), 1, 0) + bias[1:2, :]
    crossed[...] = (x0_ref[...].astype(F32) * hidden + x1_ref[...].astype(F32)).astype(BF16)
    grad = base[...] + dot(ranks[SAMPLES:, :], weight(v0_ref), 1, 0) + cot[...].astype(F32) * hidden
    grad = grad.astype(BF16)
    for table in range(TABLES_STEP):
        columns = slice(table * PROJ, (table + 1) * PROJ)
        back[table, :HALF, :] = jnp.concatenate([grad[:HALF, columns], grad[HALF:, columns]], axis=1)
        row = jnp.concatenate([sum0[:, columns], sum1[:, columns]], axis=1)
        first_row = lax.broadcasted_iota(jnp.int32, (16, EMB), 0) == 0
        back[table, HALF:, :] = jnp.where(first_row, row, 0.0).astype(BF16)


def third(at, quarters, x0, x1, cot, base, weights, bias, sum0, sum1):
    return pl.pallas_call(
        third_kernel,
        grid_spec=pltpu.PrefetchScalarGridSpec(
            num_scalar_prefetch=1,
            grid=(FEATURE_STEPS,),
            in_specs=QUARTER_SPECS
            + [feature_spec(SAMPLES)] * 4
            + [weight_spec(U1), weight_spec(V0), feature_spec(2), feature_spec(1), feature_spec(1)],
            out_specs=[
                feature_spec(SAMPLES),
                pl.BlockSpec((TABLES_STEP, BACK_ROWS, EMB), lambda j, at: (j, 0, 0)),
            ],
            scratch_shapes=[pltpu.VMEM((2 * SAMPLES, RANK), BF16)],
        ),
        out_shape=[
            jax.ShapeDtypeStruct((SAMPLES, FEATURES), BF16),
            jax.ShapeDtypeStruct((FIELD_TABLES, BACK_ROWS, EMB), BF16),
        ],
        compiler_params=params(),
        cost_estimate=cost(10**9, 10 * MIB),
    )(at, *quarters, x0, x1, cot, base, weights, weights, bias, sum0, sum1)


def terms_kernel(at, q0, q1, q2, q3, u_side, v_side, own, other, ranks):
    @pl.when(pl.program_id(0) == 0)
    def _():
        read_quarters(at, (q0, q1, q2, q3), ranks)

    is_first = at[AT_CORE] == 0
    for which, side in enumerate((u_side, v_side)):
        rows = ranks[which * SAMPLES : (which + 1) * SAMPLES, :]
        term = dot(rows, side[...], 0, 0).reshape(X_SIZE, Z_SIZE, CORES, SHARE, FEATURE_BLOCK)
        lower, upper = term[:, :, 0], term[:, :, 1]
        own[:, which] = jnp.where(is_first, lower, upper).astype(BF16)
        other[:, which] = jnp.where(is_first, upper, lower).astype(BF16)


GRAD_SHAPE = (X_SIZE, 2, Z_SIZE, SHARE, FEATURES)


def terms(at, quarters, u_side, v_side):
    block = pl.BlockSpec((X_SIZE, 2, Z_SIZE, SHARE, FEATURE_BLOCK), lambda j, at: (0, 0, 0, 0, j))
    return pl.pallas_call(
        terms_kernel,
        grid_spec=pltpu.PrefetchScalarGridSpec(
            num_scalar_prefetch=1,
            grid=(FEATURE_STEPS,),
            in_specs=QUARTER_SPECS + [feature_spec(SAMPLES)] * 2,
            out_specs=[block, block],
            scratch_shapes=[pltpu.VMEM((2 * SAMPLES, RANK), BF16)],
        ),
        out_shape=[jax.ShapeDtypeStruct(GRAD_SHAPE, BF16)] * 2,
        compiler_params=params(),
        cost_estimate=cost(10**9, 6 * MIB),
    )(at, *quarters, u_side, v_side)


def core_sum_kernel(at, *refs):
    for shift in range(X_SIZE):
        mine, theirs, out = refs[shift], refs[X_SIZE + shift], refs[2 * X_SIZE + shift]
        out[...] = (mine[0].astype(F32) + theirs[0].astype(F32)).astype(BF16)


def core_sum(at, own, arrived):
    width = 512

    def spec(shift):
        return pl.BlockSpec(
            (1, 2, Z_SIZE, SHARE, width),
            lambda j, at: (lax.rem(at[AT_X] + shift, X_SIZE), 0, 0, 0, j),
        )

    specs = [spec(shift) for shift in range(X_SIZE)]
    out_spec = pl.BlockSpec((2, Z_SIZE, SHARE, width), lambda j, at: (0, 0, 0, j))
    return pl.pallas_call(
        core_sum_kernel,
        grid_spec=pltpu.PrefetchScalarGridSpec(
            num_scalar_prefetch=1,
            grid=(FEATURES // width,),
            in_specs=specs + specs,
            out_specs=[out_spec] * X_SIZE,
        ),
        out_shape=[jax.ShapeDtypeStruct(GRAD_SHAPE[1:], BF16)] * X_SIZE,
        compiler_params=params(),
        cost_estimate=cost(10**6, 6 * MIB),
    )(at, *([own] * X_SIZE), *([arrived] * X_SIZE))


def x_sum_kernel(at, a, b, c, d, *rest):
    outs, total = rest[:Z_SIZE], rest[Z_SIZE]
    total[...] = (a[...].astype(F32) + b[...].astype(F32)) + (c[...].astype(F32) + d[...].astype(F32))
    for shift, out in enumerate(outs):
        place = lax.rem(at[AT_Z] + shift, Z_SIZE)
        out[...] = total[:, pl.ds(place, 1)].reshape(out.shape).astype(BF16)


def x_sum(at, blocks):
    width = 1024
    in_spec = pl.BlockSpec((2, Z_SIZE, SHARE, width), lambda j, at: (0, 0, 0, j))
    out_spec = pl.BlockSpec((2, SHARE, width), lambda j, at: (0, 0, j))
    return pl.pallas_call(
        x_sum_kernel,
        grid_spec=pltpu.PrefetchScalarGridSpec(
            num_scalar_prefetch=1,
            grid=(FEATURES // width,),
            in_specs=[in_spec] * X_SIZE,
            out_specs=[out_spec] * Z_SIZE,
            scratch_shapes=[pltpu.VMEM((2, Z_SIZE, SHARE, width), F32)],
        ),
        out_shape=[jax.ShapeDtypeStruct((2, SHARE, FEATURES), BF16)] * Z_SIZE,
        compiler_params=params(),
        cost_estimate=cost(10**6, 3 * MIB),
    )(at, *blocks)


def z_sum_kernel(*refs):
    early, late, (grad_u, grad_v) = refs[:Z_SIZE], refs[Z_SIZE : 2 * Z_SIZE], refs[2 * Z_SIZE :]

    def total(blocks, which):
        a, b, c, d = (block[which].astype(F32) for block in blocks)
        return (a + b) + (c + d)

    grad_u[0] = total(early, 0)
    grad_v[1] = total(early, 1)
    grad_u[1] = total(late, 0)
    grad_v[0] = total(late, 1)


def z_sum(early, late):
    return pl.pallas_call(
        z_sum_kernel,
        out_shape=[jax.ShapeDtypeStruct((2, SHARE, FEATURES), F32)] * 2,
        compiler_params=params(),
        cost_estimate=cost(10**6, 2 * MIB),
    )(*early, *late)


def last_kernel(at, back, pooled, proj, grad_pooled, grad_proj, grad_bias):
    step = pl.program_id(0)
    factor = masked_projection(proj, at[AT_WIDTH])
    none = jnp.zeros_like(factor)
    both = jnp.concatenate(
        [jnp.concatenate([factor, none], axis=1), jnp.concatenate([none, factor], axis=1)], axis=0
    )
    total = jnp.zeros((PROJ, EMB), F32)
    bias = jnp.zeros((1, EMB), F32)
    for block in range(back.shape[0]):
        grads = back[block, :HALF, :]
        start = block * SAMPLES
        out = dot(grads, both, 1, 0).astype(BF16)
        grad_pooled[start : start + HALF, :] = out[:, :EMB]
        grad_pooled[start + HALF : start + SAMPLES, :] = out[:, EMB:]
        upper = dot(grads, pooled[start : start + HALF, :], 0, 0)
        lower = dot(grads, pooled[start + HALF : start + SAMPLES, :], 0, 0)
        total += upper[:PROJ] + lower[PROJ:]
        bias += back[block, HALF:, :].astype(F32)[:1]

    @pl.when(step == 0)
    def _():
        grad_proj[...] = total
        grad_bias[...] = bias

    @pl.when(step > 0)
    def _():
        grad_proj[...] += total
        grad_bias[...] += bias


def last(at, back, pooled, proj):
    blocks = 8
    return pl.pallas_call(
        last_kernel,
        grid_spec=pltpu.PrefetchScalarGridSpec(
            num_scalar_prefetch=1,
            grid=(FIELD_TABLES // blocks,),
            in_specs=[
                pl.BlockSpec((blocks, BACK_ROWS, EMB), lambda i, at: (i, 0, 0)),
                pl.BlockSpec((blocks * SAMPLES, EMB), lambda i, at: (i, 0)),
                pl.BlockSpec((1, PROJ, EMB), lambda i, at: (at[AT_BATCH], 0, 0)),
            ],
            out_specs=[
                pl.BlockSpec((blocks * SAMPLES, EMB), lambda i, at: (i, 0)),
                whole_spec(PROJ, EMB),
                whole_spec(1, EMB),
            ],
        ),
        out_shape=[
            jax.ShapeDtypeStruct((TOKENS, EMB), BF16),
            jax.ShapeDtypeStruct((PROJ, EMB), F32),
            jax.ShapeDtypeStruct((1, EMB), F32),
        ],
        compiler_params=params(),
        cost_estimate=cost(10**9, 5 * MIB),
    )(at, back, pooled, proj)


def batch_moves(move):
    pairs = []
    for source in range(X_SIZE * Z_SIZE * CORES):
        x, z, core = source // (Z_SIZE * CORES), source // CORES % Z_SIZE, source % CORES
        x, z, core = move(x, z, core)
        pairs.append((source, (x * Z_SIZE + z) * CORES + core))
    return pairs


def field_moves(move):
    pairs = []
    for source in range(Y_SIZE * HALVES):
        y, half = move(source // HALVES, source % HALVES)
        pairs.append((source, y * HALVES + half))
    return pairs


CORE_SWAP = batch_moves(lambda x, z, core: (x, z, 1 - core))
X_MOVES = [batch_moves(lambda x, z, core, s=s: ((x + s) % X_SIZE, z, core)) for s in range(X_SIZE)]
Z_MOVES = [batch_moves(lambda x, z, core, s=s: (x, (z + s) % Z_SIZE, core)) for s in range(Z_SIZE)]
Y_MOVES = [field_moves(lambda y, half, s=s: ((y + s) % Y_SIZE, half)) for s in range(Y_SIZE)]
HALF_SWAP = field_moves(lambda y, half: (y, 1 - half))


def exchange(parts, axis, moves):
    return [parts[0]] + [lax.ppermute(parts[s], axis, moves[s]) for s in range(1, len(parts))]


def low_sum(parts):
    wide = [part.astype(F32) for part in parts]
    total = wide[0]
    for part in wide[1:]:
        total = total + part
    return total.astype(BF16)


def field_total(parts):
    partial = low_sum(exchange(parts, "field", Y_MOVES))
    whole = low_sum([partial, lax.ppermute(partial, "field", HALF_SWAP)])
    return exchange([whole] * Y_SIZE, "field", Y_MOVES)


def scatter_sum(at, own, other):
    blocks = core_sum(at, own, lax.ppermute(other, "batch", CORE_SWAP))
    blocks = x_sum(at, exchange(blocks, "batch", X_MOVES))
    return exchange(blocks, "batch", Z_MOVES)


def on_device(
    emb_tables, bag_ids, bag_lengths, table_widths, projection, cross_u, cross_v, cross_bias, cotangent
):
    batch = lax.axis_index("batch")
    field = lax.axis_index("field")
    at = jnp.stack(
        [batch, batch // (Z_SIZE * CORES), batch // CORES % Z_SIZE, batch % CORES, field // HALVES, table_widths[0]]
    ).astype(jnp.int32)
    shard = jnp.concatenate([cross_u, cross_v], axis=0)
    weights = lax.all_gather(shard, "batch", axis=0, tiled=True)
    weights = weights.reshape(FIELD_TABLES, 4, SHARE, FEATURES)
    proj = jnp.transpose(projection, (0, 2, 1))

    places = lax.broadcasted_iota(jnp.int32, (BAG, TOKENS), 0)
    ids = jnp.where(places < bag_lengths, bag_ids[0].T, ROWS)
    ids = ids.reshape(BAG, TOKENS // 128, 128).transpose(1, 0, 2).reshape(-1)
    pooled, sent = pool(at, ids, emb_tables[0], proj)
    recv = lax.all_to_all(sent, "batch", split_axis=0, concat_axis=0, tiled=True)

    x0, hg1, sum1, *parts = first(at, recv, cotangent, weights)
    quarters_a = field_total(parts)
    x1, hg0, base, sum0, *parts = second(at, quarters_a, x0, cotangent, weights, cross_bias)
    own_a, other_a = terms(at, quarters_a, hg0, x1)
    quarters_b = field_total(parts)
    early = scatter_sum(at, own_a, other_a)
    crossed, back = third(
        at, quarters_b, x0, x1, cotangent, base, weights, cross_bias, sum0, sum1
    )
    returned = lax.all_to_all(back, "batch", split_axis=0, concat_axis=0, tiled=True)
    own_b, other_b = terms(at, quarters_b, hg1, x0)
    late = scatter_sum(at, own_b, other_b)
    grad_u, grad_v = z_sum(early, late)
    grad_pooled, grad_proj, grad_bias = last(at, returned, pooled, proj)
    return (
        crossed,
        grad_u,
        grad_v,
        grad_bias.reshape(2, PROJ),
        grad_proj.T[None],
        grad_pooled[None],
    )


def solution(mesh):
    return jax.shard_map(
        on_device,
        mesh=mesh,
        in_specs=(
            P(("field", "batch"), None, None),
            P(("field", "batch"), None, None),
            P(("field", "batch"), None),
            P(("field", "batch")),
            P("field", None, None),
            P(None, "batch", "field"),
            P(None, "batch", "field"),
            P(None, "field"),
            P("batch", "field"),
        ),
        out_specs=(
            P("batch", "field"),
            P(None, "batch", "field"),
            P(None, "batch", "field"),
            P(None, ("field", "batch")),
            P(("field", "batch"), None, None),
            P(("field", "batch"), None, None),
        ),
        check_vma=False,
    )
```

time: 1350 us -> 271 us (0.20)
  waiting for transfers between devices: 867 us -> 59.4 us
  local copies, waits for them, and re-layouts: 245 us -> 8.65 us
  Pallas kernels: 0 us -> 95.3 us
  other arithmetic: 59.9 us -> 3.47 us
  blocking collectives: 87.6 us -> 35.2 us
  matrix products: 40.3 us -> 0 us
  starting transfers between devices: 21.3 us -> 52.9 us
    reduce_scatter x5 -> x0, waiting for transfers between devices: 559 us -> none  [the longest x2 291 us: on_device(): lax.psum_scatter(v_term.astype(jnp.bfloat16), 'batch', scatter_dimension=...]
    psum x2 -> x0, waiting for transfers between devices: 205 us -> none  [field_total(): lax.psum(partial_value.astype(jnp.bfloat16), 'field').astype(jnp.float32)]
    gather x8 -> x0, local copies, waits for them, and re-layouts: 177 us -> none  [pool_bags(): looked_up = jnp.take(table_shard[0], bag_ids[0, :, bag_place], axis=0)]
    pallas_call x0 -> x12, Pallas kernels: none -> 95.3 us  [the longest x1 45.3 us: pool(): pl.pallas_call(pool_kernel, grid_spec=pltpu.PrefetchScalarGridSpec(num_sc...]
    unnamed x1 -> x0, blocking collectives: 87.6 us -> none
    all_gather x4 -> x1, waiting for transfers between devices: 59.4 us -> 0.01 us  [on_device(): weights = lax.all_gather(shard, 'batch', axis=0, tiled=True)]
    ppermute x0 -> x28, waiting for transfers between devices: none -> 59.4 us  [the longest x24 52.2 us: exchange(): lax.ppermute(parts[s], axis, moves[s])]
    ppermute x0 -> x28, starting transfers between devices: none -> 44.8 us  [the longest x24 32 us: exchange(): lax.ppermute(parts[s], axis, moves[s])]
  transfers between devices with their start and end apart: 13 -> 30, of which waited for: 9 -> 14; matrix products, arithmetic and copies ran while one was open for 24% -> 1% of each run, Pallas kernels for 0% -> 29%
where the time goes in v1:
time: 271 us; the launch traced here: 270 us
  Pallas kernels  95.3 us (35%)
  waiting for transfers between devices  59.4 us (22%)
  starting transfers between devices  52.9 us (20%)
  blocking collectives  35.2 us (13%)
  between operations  14.9 us (5%)
  local copies, waits for them, and re-layouts  8.65 us (3%)
  other arithmetic  3.47 us (1%)
    ppermute x24, waiting for transfers between devices, exchange(): lax.ppermute(parts[s], axis, moves[s])  52.2 us
    pallas_call x1, Pallas kernels, pool(): pl.pallas_call(pool_kernel, grid_spec=pltpu.PrefetchScalarGridSpec(num_sc...  45.3 us
    all_to_all x1, blocking collectives, on_device(): lax.all_to_all(sent, 'batch', split_axis=0, concat_axis=0, tiled=True)  35.2 us
    ppermute x24, starting transfers between devices, exchange(): lax.ppermute(parts[s], axis, moves[s])  32 us
    pallas_call x2, Pallas kernels, terms(): pl.pallas_call(terms_kernel, grid_spec=pltpu.PrefetchScalarGridSpec(num_s...  11.4 us
    ppermute x2, starting transfers between devices, field_total(): whole = low_sum([partial, lax.ppermute(partial, 'field', HALF_SWAP)])  8.63 us
    pallas_call x1, Pallas kernels, second(): pl.pallas_call(second_kernel, grid_spec=pltpu.PrefetchScalarGridSpec(num_...  8.2 us
    all_to_all x1, starting transfers between devices, on_device(): lax.all_to_all(back, 'batch', split_axis=0, concat_axis=0, tiled=True)  8.05 us
  transfers between devices with their start and end apart: 30, of which 14 were waited for; matrix products, arithmetic and copies ran while one was open for 1% of the time, Pallas kernels for 29%

profile of v1, /device:TPU:1, one launch (start us, length us, event | category | flops | bytes accessed | tf_op | source)
XLA Modules:
  0.0 269.9 jit_solution(9804136595435489094)
XLA Ops:
  7.2 1.7 pad_maximum_fusion
  9.7 1.0 fusion.ids
  10.7 1.6 copy-done.5
  12.3 1.0 copy-done.6
  13.3 45.3 %shard_map.136 = (bf16[6144,128]{1,0:T(8,128)(2,1)S(1)}, bf16[32,96,128]{2,1,0:T(8,128)(2,1)S(1)}) custom-call(s32[6]{0:T(128)S(1)} %stack.23.at, s32[49152]{0:T(1024)S(1)} %fusion.ids, bf16[8192,128]{1,0:T(8,128)(2,1)S(1)} %bitcast.25, bf16[32,64,128]{2,1,0:T(8,128)(2,1)S(1)} %bitcast.26), custom_call_target="tpu_custom_call" | custom-call | flops 2000000000 | bytes 104857600 | tf_op jit(solution)/shard_map/pallas_call | solution.py:93
  58.6 1.1 copy-done.8
  59.7 35.2 %all_to_all.10.recv = bf16[32,96,128]{2,1,0:T(8,128)(2,1)S(1)} all-to-all(bf16[32,96,128]{2,1,0:T(8,128)(2,1)S(1)} %get-tuple-element.50), channel_id=1, replica_groups=mesh['batch'=32,'field'=8] {'batch'}, dimensions={0} | all-to-all | bytes 1572864 | tf_op jit(solution)/shard_map/all_to_all | solution.py:551
  95.0 7.2 %shard_map.137 = (bf16[192,2048]{1,0:T(8,128)(2,1)S(1)}, bf16[192,2048]{1,0:T(8,128)(2,1)S(1)}, f32[1,2048]{1,0:T(1,128)S(1)}, bf16[96,512]{1,0:T(8,128)(2,1)S(1...) custom-call(s32[6]{0:T(128)S(1)} %stack.23.at, ...), custom_call_target="tpu_custom_call" | custom-call | flops 1000000000 | bytes 8388608 | tf_op jit(solution)/shard_map/pallas_call | solution.py:187
  102.1 2.6 collective-permute-start.2
  104.7 0.5 collective-permute-start.1
  105.2 0.6 collective-permute-start
  105.8 2.5 collective-permute-done.2
  108.4 2.3 collective-permute-done.1
  110.7 1.6 collective-permute-done
  112.3 4.2 %collective-permute-start.3 = (bf16[96,512]{1,0:T(8,128)(2,1)S(1)}, bf16[96,512]{1,0:T(8,128)(2,1)S(1)}, u32[]{:S(2)}, u32[]{:S(2)}) collective-permute-start(bf16[96,512]{1,0:T(8,128)(2,1)S(1)} %add_convert_fusion.3), channel_id=1, source_target_pairs={{0,1},{1,0},{2,3},{3,2},{4,5},{5,4},{6,7},{7,6},{8,9},{9,8},{10,11... | collective-permute-start | bytes 294920 | tf_op jit(solution)/shard_map/ppermute | solution.py:524
  116.5 3.8 %collective-permute-done.3 = bf16[96,512]{1,0:T(8,128)(2,1)S(1)} collective-permute-done((bf16[96,512]{1,0:T(8,128)(2,1)S(1)}, bf16[96,512]{1,0:T(8,128)(2,1)S(1)}, u32[]{:S(2)}, u32[]{:S(2)}) %collective-permute-start.3) | collective-permute-done | bytes 98336 | tf_op jit(solution)/shard_map/ppermute | solution.py:524
  120.4 1.7 collective-permute-start.5
  122.2 0.9 collective-permute-start.6
  123.1 2.6 collective-permute-done.4.q1
  125.8 1.1 collective-permute-done.5.q2
  127.1 8.2 %shard_map.138 = (bf16[192,2048]{1,0:T(8,128)(2,1)S(1)}, bf16[192,2048]{1,0:T(8,128)(2,1)S(1)}, f32[192,2048]{1,0:T(8,128)S(1)}, f32[1,2048]{1,0:T(1,128)S(1)}, ...) custom-call(s32[6]{0:T(128)S(1)} %stack.23.at, ...), custom_call_target="tpu_custom_call" | custom-call | flops 2000000000 | bytes 10485760 | tf_op jit(solution)/shard_map/pallas_call | solution.py:249
  135.3 1.8 collective-permute-start.9
  137.1 1.2 collective-permute-start.8
  138.3 5.7 %shard_map.140 = (bf16[4,2,4,16,2048]{4,3,2,1,0:T(8,128)(2,1)S(1)}, bf16[4,2,4,16,2048]{4,3,2,1,0:T(8,128)(2,1)}) custom-call(s32[6]{0:T(128)S(1)} %stack.23.at, bf16[96,512]{1,0:T(8,128)(2,1)S(1)} %add_convert_fusion.2.q0, bf16[96,512]{1,0:T(8,128)(2,1)S(1)} %collective-permute-done.4.q1, bf16[96,512]{1,0:T(8,128)(2,1)S(1)} %collective-permute-done.5.q2, ...), custom_call_target="tpu_custom_call" | custom-call | flops 1000000000 | bytes 6291456 | tf_op jit(solution)/shard_map/pallas_call | solution.py:332
  144.0 2.9 %collective-permute-start.14 = (bf16[4,2,4,16,2048]{4,3,2,1,0:T(8,128)(2,1)}, bf16[4,2,4,16,2048]{4,3,2,1,0:T(8,128)(2,1)}, u32[]{:S(2)}, u32[]{:S(2)}) collective-permute-start(bf16[4,2,4,16,2048]{4,3,2,1,0:T(8,128)(2,1)} %get-tuple-element.67), channel_id=1, source_target_pairs={{0,8},{8,0},{16,24},{24,16},{32,40},{40,32},{48,56},{56,48},{64,72... | collective-permute-start | bytes 6291464 | tf_op jit(solution)/shard_map/ppermute | solution.py:529
  146.9 4.4 %collective-permute-start.10 = (bf16[96,512]{1,0:T(8,128)(2,1)S(1)}, bf16[96,512]{1,0:T(8,128)(2,1)S(1)}, u32[]{:S(2)}, u32[]{:S(2)}) collective-permute-start(bf16[96,512]{1,0:T(8,128)(2,1)S(1)} %add_convert_fusion.1), channel_id=1, source_target_pairs={{0,1},{1,0},{2,3},{3,2},{4,5},{5,4},{6,7},{7,6},{8,9},{9,8},{10,11... | collective-permute-start | bytes 294920 | tf_op jit(solution)/shard_map/ppermute | solution.py:524
  151.4 3.4 %collective-permute-done.10 = bf16[96,512]{1,0:T(8,128)(2,1)S(1)} collective-permute-done((bf16[96,512]{1,0:T(8,128)(2,1)S(1)}, bf16[96,512]{1,0:T(8,128)(2,1)S(1)}, u32[]{:S(2)}, u32[]{:S(2)}) %collective-permute-start.10) | collective-permute-done | bytes 98336 | tf_op jit(solution)/shard_map/ppermute | solution.py:524
  154.8 2.9 %collective-permute-start.11 = (bf16[96,512]{1,0:T(8,128)(2,1)S(1)}, bf16[96,512]{1,0:T(8,128)(2,1)S(1)}, u32[]{:S(2)}, u32[]{:S(2)}) collective-permute-start(bf16[96,512]{1,0:T(8,128)(2,1)S(1)} %add_convert_fusion.q0), channel_id=1, source_target_pairs={{0,2},{1,3},{2,4},{3,5},{4,6},{5,7},{6,0},{7,1},{8,10},{9,11},{10,... | collective-permute-start | bytes 294920 | tf_op jit(solution)/shard_map/ppermute | solution.py:511
  157.7 1.5 collective-permute-start.12
  159.3 0.9 collective-permute-start.13
  160.2 3.8 %collective-permute-done.12.q2 = bf16[96,512]{1,0:T(8,128)(2,1)S(1)} collective-permute-done((bf16[96,512]{1,0:T(8,128)(2,1)S(1)}, bf16[96,512]{1,0:T(8,128)(2,1)S(1)}, u32[]{:S(2)}, u32[]{:S(2)}) %collective-permute-start.12) | collective-permute-done | bytes 98336 | tf_op jit(solution)/shard_map/ppermute | solution.py:511
  164.0 5.7 %shard_map.143 = (bf16[4,2,4,16,2048]{4,3,2,1,0:T(8,128)(2,1)S(1)}, bf16[4,2,4,16,2048]{4,3,2,1,0:T(8,128)(2,1)}) custom-call(s32[6]{0:T(128)S(1)} %stack.23.at, bf16[96,512]{1,0:T(8,128)(2,1)S(1)} %add_convert_fusion.q0, bf16[96,512]{1,0:T(8,128)(2,1)S(1)} %collective-permute-done.11.q1, bf16[96,512]{1,0:T(8,128)(2,1)S(1)} %collective-permute-done.12.q2, ...), custom_call_target="tpu_custom_call" | custom-call | flops 1000000000 | bytes 6291456 | tf_op jit(solution)/shard_map/pallas_call | solution.py:332
  169.7 1.3 copy-done
  171.0 1.3 collective-permute-start.21
  172.3 7.8 %shard_map.139 = (bf16[192,2048]{1,0:T(8,128)(2,1)}, bf16[32,112,128]{2,1,0:T(8,128)(2,1)S(1)}) custom-call(s32[6]{0:T(128)S(1)} %stack.23.at, bf16[96,512]{1,0:T(8,128)(2,1)S(1)} %add_convert_fusion.q0, bf16[96,512]{1,0:T(8,128)(2,1)S(1)} %collective-permute-done.11.q1, bf16[96,512]{1,0:T(8,128)(2,1)S(1)} %collective-permute-done.12.q2, ...), custom_call_target="tpu_custom_call" | custom-call | flops 1000000000 | bytes 10485760 | tf_op jit(solution)/shard_map/pallas_call | solution.py:290
  180.1 0.9 copy-done.3
  181.0 8.0 %all-to-all-start.1 = ((bf16[32,112,128]{2,1,0:T(8,128)(2,1)}), bf16[32,112,128]{2,1,0:T(8,128)(2,1)}, u32[]{:S(2)}, u32[]{:S(2)}) async-start(bf16[32,112,128]{2,1,0:T(8,128)(2,1)} %copy-done.3), calls=%async_computation.1 | async-start | bytes 1835008 | tf_op jit(solution)/shard_map/all_to_all | solution.py:562
  189.1 3.7 %shard_map.141 = (bf16[2,4,16,2048]{3,2,1,0:T(8,128)(2,1)S(1)}, bf16[2,4,16,2048]{3,2,1,0:T(8,128)(2,1)S(1)}, bf16[2,4,16,2048]{3,2,1,0:T(8,128)(2,1)S(1)}, bf16[2,4,16,2048]{3,2,1,0:T(8,128)(2,1)S(1)}) custom-call(s32[6]{0:T(128)S(1)} %stack.23.at, bf16[4,2,4,16,2048]{4,3,2,1,0:T(8,128)(2,1)S(1)} %get-tuple-element.66.refs_0_.refs_1_.refs_2_.refs_3_, ...), custom_call_target="tpu_custom_call" | custom-call | flops 1000000 | bytes 6291456 | tf_op jit(solution)/shard_map/pallas_call | solution.py:364
  192.7 1.5 collective-permute-start.15
  194.2 2.4 collective-permute-start.16
  196.6 1.1 collective-permute-start.17
  197.8 3.7 %shard_map.144 = (bf16[2,4,16,2048]{3,2,1,0:T(8,128)(2,1)S(1)}, bf16[2,4,16,2048]{3,2,1,0:T(8,128)(2,1)S(1)}, bf16[2,4,16,2048]{3,2,1,0:T(8,128)(2,1)S(1)}, bf16[2,4,16,2048]{3,2,1,0:T(8,128)(2,1)S(1)}) custom-call(s32[6]{0:T(128)S(1)} %stack.23.at, bf16[4,2,4,16,2048]{4,3,2,1,0:T(8,128)(2,1)S(1)} %copy-done.1, bf16[4,2,4,16,2048]{4,3,2,1,0:T(8,128)(2,1)S(1)} %copy-done.1, ...), custom_call_target="tpu_custom_call" | custom-call | flops 1000000 | bytes 6291456 | tf_op jit(solution)/shard_map/pallas_call | solution.py:364
  201.4 0.4 collective-permute-start.22
  201.8 0.9 collective-permute-start.23
  202.7 10.7 %collective-permute-done.15.b = bf16[2,4,16,2048]{3,2,1,0:T(8,128)(2,1)S(1)} collective-permute-done((bf16[2,4,16,2048]{3,2,1,0:T(8,128)(2,1)S(1)}, bf16[2,4,16,2048]{3,2,1,0:T(8,128)(2,1)S(1)}, u32[]{:S(2)}, u32[]{:S(2)}) %collective-permute-start.15) | collective-permute-done | bytes 524320 | tf_op jit(solution)/shard_map/ppermute | solution.py:511
  213.4 0.6 collective-permute-start.24
  214.0 11.5 %collective-permute-done.16.c = bf16[2,4,16,2048]{3,2,1,0:T(8,128)(2,1)S(1)} collective-permute-done((bf16[2,4,16,2048]{3,2,1,0:T(8,128)(2,1)S(1)}, bf16[2,4,16,2048]{3,2,1,0:T(8,128)(2,1)S(1)}, u32[]{:S(2)}, u32[]{:S(2)}) %collective-permute-start.16) | collective-permute-done | bytes 524320 | tf_op jit(solution)/shard_map/ppermute | solution.py:511
  225.5 1.3 shard_map.142
  226.7 1.2 collective-permute-start.18
  228.0 1.8 collective-permute-start.19
  229.8 6.5 %collective-permute-done.22.b = bf16[2,4,16,2048]{3,2,1,0:T(8,128)(2,1)S(1)} collective-permute-done((bf16[2,4,16,2048]{3,2,1,0:T(8,128)(2,1)S(1)}, bf16[2,4,16,2048]{3,2,1,0:T(8,128)(2,1)S(1)}, u32[]{:S(2)}, u32[]{:S(2)}) %collective-permute-start.22) | collective-permute-done | bytes 524320 | tf_op jit(solution)/shard_map/ppermute | solution.py:511
  236.4 3.3 %collective-permute-start.20 = (bf16[2,16,2048]{2,1,0:T(8,128)(2,1)S(1)}, bf16[2,16,2048]{2,1,0:T(8,128)(2,1)S(1)}, u32[]{:S(2)}, u32[]{:S(2)}) collective-permute-start(bf16[2,16,2048]{2,1,0:T(8,128)(2,1)S(1)} %get-tuple-element.75), channel_id=1, source_target_pairs={{0,48},{8,56},{16,0},{24,8},{32,16},{40,24},{48,32},{56,40},{64,11... | collective-permute-start | bytes 393224 | tf_op jit(solution)/shard_map/ppermute | solution.py:511
  239.6 8.3 %collective-permute-done.23.c = bf16[2,4,16,2048]{3,2,1,0:T(8,128)(2,1)S(1)} collective-permute-done((bf16[2,4,16,2048]{3,2,1,0:T(8,128)(2,1)S(1)}, bf16[2,4,16,2048]{3,2,1,0:T(8,128)(2,1)S(1)}, u32[]{:S(2)}, u32[]{:S(2)}) %collective-permute-start.23) | collective-permute-done | bytes 524320 | tf_op jit(solution)/shard_map/ppermute | solution.py:511
  247.9 1.3 shard_map.145
  249.2 1.2 collective-permute-start.25
  250.5 1.8 collective-permute-start.26
  252.3 0.9 collective-permute-start.27
  253.2 1.4 copy-done.9
  254.6 4.8 %shard_map.147 = (bf16[6144,128]{1,0:T(8,128)(2,1)}, f32[64,128]{1,0:T(8,128)}, f32[1,128]{1,0:T(1,128)S(1)}) custom-call(s32[6]{0:T(128)S(1)} %stack.23.at, bf16[32,112,128]{2,1,0:T(8,128)(2,1)} %all-to-all-done.1.back, bf16[6144,128]{1,0:T(8,128)(2,1)S(1)} %copy-done.9, bf16[32,64,128]{2,1,0:T(8,128)(2,1)S(1)} %bitcast.27), custom_call_target="tpu_custom_call" | custom-call | flops 1000000000 | bytes 5242880 | tf_op jit(solution)/shard_map/pallas_call | solution.py:460
  259.4 0.5 broadcast.8
  259.9 0.7 reduce.3
  260.6 0.6 reshape.27
  261.2 0.9 collective-permute-done.26.refs_6_
  262.1 0.9 shard_map.146
  (40 shorter events, 0.7 us)
Async XLA Ops:
  7.2 87.8 %all-gather.2.cloned.1.call-start = ((), (), s32[]{:S(2)}) async-start(), calls=%async_computation.2 | async-start | bytes 8650752 | tf_op jit(solution)/shard_map/all_gather | solution.py:543
  10.7 1.6 copy-start.5
  12.3 1.0 copy-start.6
  58.6 1.1 copy-start.8
  59.7 35.2 %copy-start.2 = (bf16[192,2048]{1,0:T(8,128)(2,1)S(1)}, bf16[192,2048]{1,0:T(8,128)(2,1)}, u32[]{:S(2)}) copy-start(bf16[192,2048]{1,0:T(8,128)(2,1)} %cot.5) | copy-start | bytes 2359300
  95.0 32.1 %copy-start.4 = (f32[2,2048]{1,0:T(2,128)S(1)}, f32[2,2048]{1,0:T(2,128)}, u32[]{:S(2)}) copy-start(f32[2,2048]{1,0:T(2,128)} %bias.3) | copy-start | bytes 49156
  102.1 6.2 %collective-permute-start.2 = (bf16[96,512]{1,0:T(8,128)(2,1)S(1)}, bf16[96,512]{1,0:T(8,128)(2,1)S(1)}, u32[]{:S(2)}, u32[]{:S(2)}) collective-permute-start(bf16[96,512]{1,0:T(8,128)(2,1)S(1)} %get-tuple-element.54), channel_id=1, source_target_pairs={{0,6},{1,7},{2,0},{3,1},{4,2},{5,3},{6,4},{7,5},{8,14},{9,15},{10,... | collective-permute-start | bytes 294920 | tf_op jit(solution)/shard_map/ppermute | solution.py:511
  104.7 6.0 %collective-permute-start.1 = (bf16[96,512]{1,0:T(8,128)(2,1)S(1)}, bf16[96,512]{1,0:T(8,128)(2,1)S(1)}, u32[]{:S(2)}, u32[]{:S(2)}) collective-permute-start(bf16[96,512]{1,0:T(8,128)(2,1)S(1)} %get-tuple-element.53), channel_id=1, source_target_pairs={{0,4},{1,5},{2,6},{3,7},{4,0},{5,1},{6,2},{7,3},{8,12},{9,13},{10,... | collective-permute-start | bytes 294920 | tf_op jit(solution)/shard_map/ppermute | solution.py:511
  105.2 7.1 %collective-permute-start = (bf16[96,512]{1,0:T(8,128)(2,1)S(1)}, bf16[96,512]{1,0:T(8,128)(2,1)S(1)}, u32[]{:S(2)}, u32[]{:S(2)}) collective-permute-start(bf16[96,512]{1,0:T(8,128)(2,1)S(1)} %get-tuple-element.52), channel_id=1, source_target_pairs={{0,2},{1,3},{2,4},{3,5},{4,6},{5,7},{6,0},{7,1},{8,10},{9,11},{10,... | collective-permute-start | bytes 294920 | tf_op jit(solution)/shard_map/ppermute | solution.py:511
  112.3 8.0 %collective-permute-start.3 = (bf16[96,512]{1,0:T(8,128)(2,1)S(1)}, bf16[96,512]{1,0:T(8,128)(2,1)S(1)}, u32[]{:S(2)}, u32[]{:S(2)}) collective-permute-start(bf16[96,512]{1,0:T(8,128)(2,1)S(1)} %add_convert_fusion.3), channel_id=1, source_target_pairs={{0,1},{1,0},{2,3},{3,2},{4,5},{5,4},{6,7},{7,6},{8,9},{9,8},{10,11... | collective-permute-start | bytes 294920 | tf_op jit(solution)/shard_map/ppermute | solution.py:524
  120.3 5.4 %collective-permute-start.4 = (bf16[96,512]{1,0:T(8,128)(2,1)S(1)}, bf16[96,512]{1,0:T(8,128)(2,1)S(1)}, u32[]{:S(2)}, u32[]{:S(2)}) collective-permute-start(bf16[96,512]{1,0:T(8,128)(2,1)S(1)} %add_convert_fusion.2.q0), channel_id=1, source_target_pairs={{0,2},{1,3},{2,4},{3,5},{4,6},{5,7},{6,0},{7,1},{8,10},{9,11},{10,... | collective-permute-start | bytes 294920 | tf_op jit(solution)/shard_map/ppermute | solution.py:511
  120.4 6.4 %collective-permute-start.5 = (bf16[96,512]{1,0:T(8,128)(2,1)S(1)}, bf16[96,512]{1,0:T(8,128)(2,1)S(1)}, u32[]{:S(2)}, u32[]{:S(2)}) collective-permute-start(bf16[96,512]{1,0:T(8,128)(2,1)S(1)} %add_convert_fusion.2.q0), channel_id=1, source_target_pairs={{0,4},{1,5},{2,6},{3,7},{4,0},{5,1},{6,2},{7,3},{8,12},{9,13},{10,... | collective-permute-start | bytes 294920 | tf_op jit(solution)/shard_map/ppermute | solution.py:511
  122.2 4.9 %collective-permute-start.6 = (bf16[96,512]{1,0:T(8,128)(2,1)S(1)}, bf16[96,512]{1,0:T(8,128)(2,1)S(1)}, u32[]{:S(2)}, u32[]{:S(2)}) collective-permute-start(bf16[96,512]{1,0:T(8,128)(2,1)S(1)} %add_convert_fusion.2.q0), channel_id=1, source_target_pairs={{0,6},{1,7},{2,0},{3,1},{4,2},{5,3},{6,4},{7,5},{8,14},{9,15},{10,... | collective-permute-start | bytes 294920 | tf_op jit(solution)/shard_map/ppermute | solution.py:511
  135.3 11.6 %collective-permute-start.9 = (bf16[96,512]{1,0:T(8,128)(2,1)S(1)}, bf16[96,512]{1,0:T(8,128)(2,1)S(1)}, u32[]{:S(2)}, u32[]{:S(2)}) collective-permute-start(bf16[96,512]{1,0:T(8,128)(2,1)S(1)} %get-tuple-element.59), channel_id=1, source_target_pairs={{0,6},{1,7},{2,0},{3,1},{4,2},{5,3},{6,4},{7,5},{8,14},{9,15},{10,... | collective-permute-start | bytes 294920 | tf_op jit(solution)/shard_map/ppermute | solution.py:511
  137.1 9.7 %collective-permute-start.8 = (bf16[96,512]{1,0:T(8,128)(2,1)S(1)}, bf16[96,512]{1,0:T(8,128)(2,1)S(1)}, u32[]{:S(2)}, u32[]{:S(2)}) collective-permute-start(bf16[96,512]{1,0:T(8,128)(2,1)S(1)} %get-tuple-element.58), channel_id=1, source_target_pairs={{0,4},{1,5},{2,6},{3,7},{4,0},{5,1},{6,2},{7,3},{8,12},{9,13},{10,... | collective-permute-start | bytes 294920 | tf_op jit(solution)/shard_map/ppermute | solution.py:511
  138.3 8.6 %collective-permute-start.7 = (bf16[96,512]{1,0:T(8,128)(2,1)S(1)}, bf16[96,512]{1,0:T(8,128)(2,1)S(1)}, u32[]{:S(2)}, u32[]{:S(2)}) collective-permute-start(bf16[96,512]{1,0:T(8,128)(2,1)S(1)} %get-tuple-element.57), channel_id=1, source_target_pairs={{0,2},{1,3},{2,4},{3,5},{4,6},{5,7},{6,0},{7,1},{8,10},{9,11},{10,... | collective-permute-start | bytes 294920 | tf_op jit(solution)/shard_map/ppermute | solution.py:511
  144.0 45.1 %collective-permute-start.14 = (bf16[4,2,4,16,2048]{4,3,2,1,0:T(8,128)(2,1)}, bf16[4,2,4,16,2048]{4,3,2,1,0:T(8,128)(2,1)}, u32[]{:S(2)}, u32[]{:S(2)}) collective-permute-start(bf16[4,2,4,16,2048]{4,3,2,1,0:T(8,128)(2,1)} %get-tuple-element.67), channel_id=1, source_target_pairs={{0,8},{8,0},{16,24},{24,16},{32,40},{40,32},{48,56},{56,48},{64,72... | collective-permute-start | bytes 6291464 | tf_op jit(solution)/shard_map/ppermute | solution.py:529
  146.9 7.8 %collective-permute-start.10 = (bf16[96,512]{1,0:T(8,128)(2,1)S(1)}, bf16[96,512]{1,0:T(8,128)(2,1)S(1)}, u32[]{:S(2)}, u32[]{:S(2)}) collective-permute-start(bf16[96,512]{1,0:T(8,128)(2,1)S(1)} %add_convert_fusion.1), channel_id=1, source_target_pairs={{0,1},{1,0},{2,3},{3,2},{4,5},{5,4},{6,7},{7,6},{8,9},{9,8},{10,11... | collective-permute-start | bytes 294920 | tf_op jit(solution)/shard_map/ppermute | solution.py:524
  154.8 5.4 %collective-permute-start.11 = (bf16[96,512]{1,0:T(8,128)(2,1)S(1)}, bf16[96,512]{1,0:T(8,128)(2,1)S(1)}, u32[]{:S(2)}, u32[]{:S(2)}) collective-permute-start(bf16[96,512]{1,0:T(8,128)(2,1)S(1)} %add_convert_fusion.q0), channel_id=1, source_target_pairs={{0,2},{1,3},{2,4},{3,5},{4,6},{5,7},{6,0},{7,1},{8,10},{9,11},{10,... | collective-permute-start | bytes 294920 | tf_op jit(solution)/shard_map/ppermute | solution.py:511
  157.7 6.3 %collective-permute-start.12 = (bf16[96,512]{1,0:T(8,128)(2,1)S(1)}, bf16[96,512]{1,0:T(8,128)(2,1)S(1)}, u32[]{:S(2)}, u32[]{:S(2)}) collective-permute-start(bf16[96,512]{1,0:T(8,128)(2,1)S(1)} %add_convert_fusion.q0), channel_id=1, source_target_pairs={{0,4},{1,5},{2,6},{3,7},{4,0},{5,1},{6,2},{7,3},{8,12},{9,13},{10,... | collective-permute-start | bytes 294920 | tf_op jit(solution)/shard_map/ppermute | solution.py:511
  159.3 4.8 %collective-permute-start.13 = (bf16[96,512]{1,0:T(8,128)(2,1)S(1)}, bf16[96,512]{1,0:T(8,128)(2,1)S(1)}, u32[]{:S(2)}, u32[]{:S(2)}) collective-permute-start(bf16[96,512]{1,0:T(8,128)(2,1)S(1)} %add_convert_fusion.q0), channel_id=1, source_target_pairs={{0,6},{1,7},{2,0},{3,1},{4,2},{5,3},{6,4},{7,5},{8,14},{9,15},{10,... | collective-permute-start | bytes 294920 | tf_op jit(solution)/shard_map/ppermute | solution.py:511
  169.7 1.3 copy-start
  171.0 26.8 %collective-permute-start.21 = (bf16[4,2,4,16,2048]{4,3,2,1,0:T(8,128)(2,1)}, bf16[4,2,4,16,2048]{4,3,2,1,0:T(8,128)(2,1)}, u32[]{:S(2)}, u32[]{:S(2)}) collective-permute-start(bf16[4,2,4,16,2048]{4,3,2,1,0:T(8,128)(2,1)} %get-tuple-element.78), channel_id=1, source_target_pairs={{0,8},{8,0},{16,24},{24,16},{32,40},{40,32},{48,56},{56,48},{64,72... | collective-permute-start | bytes 6291464 | tf_op jit(solution)/shard_map/ppermute | solution.py:529
  180.1 0.9 copy-start.3
  181.0 72.2 %all-to-all-start.1 = ((bf16[32,112,128]{2,1,0:T(8,128)(2,1)}), bf16[32,112,128]{2,1,0:T(8,128)(2,1)}, u32[]{:S(2)}, u32[]{:S(2)}) async-start(bf16[32,112,128]{2,1,0:T(8,128)(2,1)} %copy-done.3), calls=%async_computation.1 | async-start | bytes 1835008 | tf_op jit(solution)/shard_map/all_to_all | solution.py:562
  189.1 8.7 %copy-start.1 = (bf16[4,2,4,16,2048]{4,3,2,1,0:T(8,128)(2,1)S(1)}, bf16[4,2,4,16,2048]{4,3,2,1,0:T(8,128)(2,1)}, u32[]{:S(2)}) copy-start(bf16[4,2,4,16,2048]{4,3,2,1,0:T(8,128)(2,1)} %copy-done) | copy-start | bytes 6291460
  192.7 20.6 %collective-permute-start.15 = (bf16[2,4,16,2048]{3,2,1,0:T(8,128)(2,1)S(1)}, bf16[2,4,16,2048]{3,2,1,0:T(8,128)(2,1)S(1)}, u32[]{:S(2)}, u32[]{:S(2)}) collective-permute-start(bf16[2,4,16,2048]{3,2,1,0:T(8,128)(2,1)S(1)} %get-tuple-element.69), channel_id=1, source_target_pairs={{0,64},{8,72},{16,80},{24,88},{32,96},{40,104},{48,112},{56,120},{... | collective-permute-start | bytes 1572872 | tf_op jit(solution)/shard_map/ppermute | solution.py:511
  194.2 31.3 %collective-permute-start.16 = (bf16[2,4,16,2048]{3,2,1,0:T(8,128)(2,1)S(1)}, bf16[2,4,16,2048]{3,2,1,0:T(8,128)(2,1)S(1)}, u32[]{:S(2)}, u32[]{:S(2)}) collective-permute-start(bf16[2,4,16,2048]{3,2,1,0:T(8,128)(2,1)S(1)} %get-tuple-element.70), channel_id=1, source_target_pairs={{0,128},{8,136},{16,144},{24,152},{32,160},{40,168},{48,176},{56,1... | collective-permute-start | bytes 1572872 | tf_op jit(solution)/shard_map/ppermute | solution.py:511
  196.6 28.8 %collective-permute-start.17 = (bf16[2,4,16,2048]{3,2,1,0:T(8,128)(2,1)S(1)}, bf16[2,4,16,2048]{3,2,1,0:T(8,128)(2,1)S(1)}, u32[]{:S(2)}, u32[]{:S(2)}) collective-permute-start(bf16[2,4,16,2048]{3,2,1,0:T(8,128)(2,1)S(1)} %get-tuple-element.71), channel_id=1, source_target_pairs={{0,192},{8,200},{16,208},{24,216},{32,224},{40,232},{48,240},{56,2... | collective-permute-start | bytes 1572872 | tf_op jit(solution)/shard_map/ppermute | solution.py:511
  201.4 34.9 %collective-permute-start.22 = (bf16[2,4,16,2048]{3,2,1,0:T(8,128)(2,1)S(1)}, bf16[2,4,16,2048]{3,2,1,0:T(8,128)(2,1)S(1)}, u32[]{:S(2)}, u32[]{:S(2)}) collective-permute-start(bf16[2,4,16,2048]{3,2,1,0:T(8,128)(2,1)S(1)} %get-tuple-element.80), channel_id=1, source_target_pairs={{0,64},{8,72},{16,80},{24,88},{32,96},{40,104},{48,112},{56,120},{... | collective-permute-start | bytes 1572872 | tf_op jit(solution)/shard_map/ppermute | solution.py:511
  201.8 46.1 %collective-permute-start.23 = (bf16[2,4,16,2048]{3,2,1,0:T(8,128)(2,1)S(1)}, bf16[2,4,16,2048]{3,2,1,0:T(8,128)(2,1)S(1)}, u32[]{:S(2)}, u32[]{:S(2)}) collective-permute-start(bf16[2,4,16,2048]{3,2,1,0:T(8,128)(2,1)S(1)} %get-tuple-element.81), channel_id=1, source_target_pairs={{0,128},{8,136},{16,144},{24,152},{32,160},{40,168},{48,176},{56,1... | collective-permute-start | bytes 1572872 | tf_op jit(solution)/shard_map/ppermute | solution.py:511
  213.4 34.5 %collective-permute-start.24 = (bf16[2,4,16,2048]{3,2,1,0:T(8,128)(2,1)S(1)}, bf16[2,4,16,2048]{3,2,1,0:T(8,128)(2,1)S(1)}, u32[]{:S(2)}, u32[]{:S(2)}) collective-permute-start(bf16[2,4,16,2048]{3,2,1,0:T(8,128)(2,1)S(1)} %get-tuple-element.82), channel_id=1, source_target_pairs={{0,192},{8,200},{16,208},{24,216},{32,224},{40,232},{48,240},{56,2... | collective-permute-start | bytes 1572872 | tf_op jit(solution)/shard_map/ppermute | solution.py:511
  225.5 27.7 %copy-start.7 = (bf16[32,128,64]{1,2,0:T(8,128)(2,1)S(1)}, bf16[32,128,64]{1,2,0:T(8,128)(2,1)}, u32[]{:S(2)}) copy-start(bf16[32,128,64]{1,2,0:T(8,128)(2,1)} %param.13) | copy-start | bytes 1572868
  226.7 25.6 %collective-permute-start.18 = (bf16[2,16,2048]{2,1,0:T(8,128)(2,1)S(1)}, bf16[2,16,2048]{2,1,0:T(8,128)(2,1)S(1)}, u32[]{:S(2)}, u32[]{:S(2)}) collective-permute-start(bf16[2,16,2048]{2,1,0:T(8,128)(2,1)S(1)} %get-tuple-element.73), channel_id=1, source_target_pairs={{0,16},{8,24},{16,32},{24,40},{32,48},{40,56},{48,0},{56,8},{64,80... | collective-permute-start | bytes 393224 | tf_op jit(solution)/shard_map/ppermute | solution.py:511
  228.0 33.2 %collective-permute-start.19 = (bf16[2,16,2048]{2,1,0:T(8,128)(2,1)S(1)}, bf16[2,16,2048]{2,1,0:T(8,128)(2,1)S(1)}, u32[]{:S(2)}, u32[]{:S(2)}) collective-permute-start(bf16[2,16,2048]{2,1,0:T(8,128)(2,1)S(1)} %get-tuple-element.74), channel_id=1, source_target_pairs={{0,32},{8,40},{16,48},{24,56},{32,0},{40,8},{48,16},{56,24},{64,96... | collective-permute-start | bytes 393224 | tf_op jit(solution)/shard_map/ppermute | solution.py:511
  236.4 24.9 %collective-permute-start.20 = (bf16[2,16,2048]{2,1,0:T(8,128)(2,1)S(1)}, bf16[2,16,2048]{2,1,0:T(8,128)(2,1)S(1)}, u32[]{:S(2)}, u32[]{:S(2)}) collective-permute-start(bf16[2,16,2048]{2,1,0:T(8,128)(2,1)S(1)} %get-tuple-element.75), channel_id=1, source_target_pairs={{0,48},{8,56},{16,0},{24,8},{32,16},{40,24},{48,32},{56,40},{64,11... | collective-permute-start | bytes 393224 | tf_op jit(solution)/shard_map/ppermute | solution.py:511
  249.2 12.0 %collective-permute-start.25 = (bf16[2,16,2048]{2,1,0:T(8,128)(2,1)S(1)}, bf16[2,16,2048]{2,1,0:T(8,128)(2,1)S(1)}, u32[]{:S(2)}, u32[]{:S(2)}) collective-permute-start(bf16[2,16,2048]{2,1,0:T(8,128)(2,1)S(1)} %get-tuple-element.84), channel_id=1, source_target_pairs={{0,16},{8,24},{16,32},{24,40},{32,48},{40,56},{48,0},{56,8},{64,80... | collective-permute-start | bytes 393224 | tf_op jit(solution)/shard_map/ppermute | solution.py:511
  250.5 11.7 %collective-permute-start.26 = (bf16[2,16,2048]{2,1,0:T(8,128)(2,1)S(1)}, bf16[2,16,2048]{2,1,0:T(8,128)(2,1)S(1)}, u32[]{:S(2)}, u32[]{:S(2)}) collective-permute-start(bf16[2,16,2048]{2,1,0:T(8,128)(2,1)S(1)} %get-tuple-element.85), channel_id=1, source_target_pairs={{0,32},{8,40},{16,48},{24,56},{32,0},{40,8},{48,16},{56,24},{64,96... | collective-permute-start | bytes 393224 | tf_op jit(solution)/shard_map/ppermute | solution.py:511
  252.3 9.8 %collective-permute-start.27 = (bf16[2,16,2048]{2,1,0:T(8,128)(2,1)S(1)}, bf16[2,16,2048]{2,1,0:T(8,128)(2,1)S(1)}, u32[]{:S(2)}, u32[]{:S(2)}) collective-permute-start(bf16[2,16,2048]{2,1,0:T(8,128)(2,1)S(1)} %get-tuple-element.86), channel_id=1, source_target_pairs={{0,48},{8,56},{16,0},{24,8},{32,16},{40,24},{48,32},{56,40},{64,11... | collective-permute-start | bytes 393224 | tf_op jit(solution)/shard_map/ppermute | solution.py:511
  253.2 1.4 copy-start.9
Sparse Core Ops, SparseCore 0:
  10.4 82.6 all-gather.1

commit v2 on v1

v2 whole, which is shorter than its diff:
```python
import functools

import jax
import jax.numpy as jnp
from jax import lax
from jax.experimental import pallas as pl
from jax.experimental.pallas import tpu as pltpu
from jax.sharding import PartitionSpec as P

BF16 = jnp.bfloat16
F32 = jnp.float32
MIB = 2**20

X_SIZE, Z_SIZE, CORES = 4, 4, 2
Y_SIZE, HALVES = 4, 2

ROWS, EMB, PROJ, BAG = 8192, 128, 64, 8
SAMPLES, FEATURES, RANK = 192, 2048, 512
FIELD_TABLES = 32
HALF = SAMPLES // 2
SHARE = RANK // FIELD_TABLES
TOKENS = SAMPLES * FIELD_TABLES
BACK_ROWS = HALF + 16
FEATURE_BLOCK = 512
POOL_CHUNK = 1536
POOL_UNROLL = 64
QUARTER = 2 * SAMPLES // Y_SIZE

AT_BATCH, AT_X, AT_Z, AT_CORE, AT_Y, AT_WIDTH = range(6)
U0, U1, V0, V1 = range(4)


def params():
    return pltpu.CompilerParams(vmem_limit_bytes=32 * MIB)


def cost(moved):
    return pl.CostEstimate(flops=0, bytes_accessed=moved, transcendentals=0)


def dot(left, right, left_dim, right_dim):
    return lax.dot_general(
        left, right, (((left_dim,), (right_dim,)), ((), ())), preferred_element_type=F32
    )


def masked_projection(proj_ref, width):
    columns = lax.broadcasted_iota(jnp.int32, (PROJ, EMB), 1)
    return jnp.where(columns < width, proj_ref[0].astype(F32), 0.0).astype(BF16)


def pool_kernel(at, ids, table, proj, pooled, sent, wide_table, summed):
    @pl.when(pl.program_id(0) == 0)
    def _():
        within = lax.broadcasted_iota(jnp.int32, (256, EMB), 1) < at[AT_WIDTH]

        @pl.loop(0, ROWS // 256)
        def _(part):
            rows = pl.ds(pl.multiple_of(part * 256, 256), 256)
            wide_table[rows, :] = jnp.where(within, table[rows, :].astype(F32), 0.0)

        wide_table[ROWS : ROWS + 8, :] = jnp.zeros((8, EMB), F32)

    groups = 128 // POOL_UNROLL

    @pl.loop(0, POOL_CHUNK // POOL_UNROLL)
    def _(group):
        first = group * POOL_UNROLL
        base = (group // groups) * (128 * BAG) + (group % groups) * POOL_UNROLL
        for step in range(POOL_UNROLL):
            rows = [wide_table[pl.ds(ids[base + (place * 128 + step)], 1), :] for place in range(BAG)]
            summed[pl.ds(first + step, 1), :] = (
                (rows[0] + rows[1]) + (rows[2] + rows[3])
            ) + ((rows[4] + rows[5]) + (rows[6] + rows[7]))

    low = summed[...].astype(BF16)
    pooled[...] = low
    factor = proj[0]
    none = jnp.zeros_like(factor)
    both = jnp.concatenate(
        [jnp.concatenate([factor, none], axis=1), jnp.concatenate([none, factor], axis=1)], axis=0
    )
    for block in range(POOL_CHUNK // SAMPLES):
        start = block * SAMPLES
        pair = jnp.concatenate(
            [low[start : start + HALF], low[start + HALF : start + SAMPLES]], axis=1
        )
        sent[block] = dot(pair, both, 1, 1).astype(BF16)


def pool(at, ids, table, proj):
    blocks = POOL_CHUNK // SAMPLES
    return pl.pallas_call(
        pool_kernel,
        grid_spec=pltpu.PrefetchScalarGridSpec(
            num_scalar_prefetch=1,
            grid=(TOKENS // POOL_CHUNK,),
            in_specs=[
                pl.BlockSpec((POOL_CHUNK * BAG,), lambda i, at: (i,), memory_space=pltpu.SMEM),
                pl.BlockSpec((ROWS, EMB), lambda i, at: (0, 0)),
                pl.BlockSpec((1, PROJ, EMB), lambda i, at: (at[AT_BATCH], 0, 0)),
            ],
            out_specs=[
                pl.BlockSpec((POOL_CHUNK, EMB), lambda i, at: (i, 0)),
                pl.BlockSpec((blocks, HALF, EMB), lambda i, at: (i, 0, 0)),
            ],
            scratch_shapes=[pltpu.VMEM((ROWS + 8, EMB), F32), pltpu.VMEM((POOL_CHUNK, EMB), F32)],
        ),
        out_shape=[
            jax.ShapeDtypeStruct((TOKENS, EMB), BF16),
            jax.ShapeDtypeStruct((FIELD_TABLES, HALF, EMB), BF16),
        ],
        compiler_params=params(),
        cost_estimate=cost(100 * MIB),
    )(at, ids, table, proj)


def assemble_kernel(at, *refs):
    parts, whole = refs[:-1], refs[-1]
    for shift, part in enumerate(parts):
        place = lax.rem(at[AT_Y] + Y_SIZE - shift, Y_SIZE)
        whole[pl.ds(pl.multiple_of(place * QUARTER, QUARTER), QUARTER), :] = part[...]


def assemble(at, parts):
    return pl.pallas_call(
        assemble_kernel,
        grid_spec=pltpu.PrefetchScalarGridSpec(
            num_scalar_prefetch=1,
            grid=(1,),
            in_specs=[whole_spec(QUARTER, RANK)] * Y_SIZE,
            out_specs=whole_spec(2 * SAMPLES, RANK),
        ),
        out_shape=jax.ShapeDtypeStruct((2 * SAMPLES, RANK), BF16),
        compiler_params=params(),
        cost_estimate=cost(MIB),
    )(at, *parts)


def write_quarters(at, total, parts):
    for shift, part in enumerate(parts):
        place = lax.rem(at[AT_Y] + shift, Y_SIZE)
        part[...] = total[pl.ds(pl.multiple_of(place * QUARTER, QUARTER), QUARTER), :].astype(BF16)


def weight(ref):
    return ref[...].reshape(RANK, FEATURE_BLOCK)


def first_kernel(at, recv, cot, v0, u1, pair, bias_out, q0, q1, q2, q3, total):
    step = pl.program_id(0)
    columns = []
    for place in range(FEATURE_BLOCK // EMB):
        left, right = recv[2 * place], recv[2 * place + 1]
        top = jnp.concatenate([left[:, :PROJ], right[:, :PROJ]], axis=1)
        bottom = jnp.concatenate([left[:, PROJ:], right[:, PROJ:]], axis=1)
        columns.append(jnp.concatenate([top, bottom], axis=0))
    x0 = jnp.concatenate(columns, axis=1)
    hg = (cot[...].astype(F32) * x0.astype(F32)).astype(BF16)
    pair[0] = hg
    pair[1] = x0
    bias_out[...] = jnp.sum(hg.astype(F32), axis=0, keepdims=True)
    rank = dot(x0, weight(v0), 1, 1)
    rank_grad = dot(hg, weight(u1), 1, 1)

    @pl.when(step == 0)
    def _():
        total[:SAMPLES, :] = rank
        total[SAMPLES:, :] = rank_grad

    @pl.when(step > 0)
    def _():
        total[:SAMPLES, :] += rank
        total[SAMPLES:, :] += rank_grad

    @pl.when(step == pl.num_programs(0) - 1)
    def _():
        write_quarters(at, total, (q0, q1, q2, q3))


def feature_spec(rows):
    return pl.BlockSpec((rows, FEATURE_BLOCK), lambda j, at: (0, j))


def weight_spec(which):
    return pl.BlockSpec(
        (FIELD_TABLES, 1, SHARE, FEATURE_BLOCK), lambda j, at: (0, which, 0, j)
    )


def whole_spec(*shape):
    return pl.BlockSpec(shape, lambda j, at: (0,) * len(shape))


def pair_spec(which=None):
    if which is None:
        return pl.BlockSpec((2, SAMPLES, FEATURE_BLOCK), lambda j, at: (0, 0, j))
    return pl.BlockSpec((None, SAMPLES, FEATURE_BLOCK), lambda j, at: (which, 0, j))


QUARTER_SPECS = [whole_spec(QUARTER, RANK)] * Y_SIZE
QUARTER_SHAPES = [jax.ShapeDtypeStruct((QUARTER, RANK), BF16)] * Y_SIZE
FEATURE_STEPS = FEATURES // FEATURE_BLOCK
TABLES_STEP = FEATURE_BLOCK // PROJ


def first(at, recv, cot, weights):
    return pl.pallas_call(
        first_kernel,
        grid_spec=pltpu.PrefetchScalarGridSpec(
            num_scalar_prefetch=1,
            grid=(FEATURE_STEPS,),
            in_specs=[
                pl.BlockSpec((TABLES_STEP, HALF, EMB), lambda j, at: (j, 0, 0)),
                feature_spec(SAMPLES),
                weight_spec(V0),
                weight_spec(U1),
            ],
            out_specs=[pair_spec(), feature_spec(1)] + QUARTER_SPECS,
            scratch_shapes=[pltpu.VMEM((2 * SAMPLES, RANK), F32)],
        ),
        out_shape=[
            jax.ShapeDtypeStruct((2, SAMPLES, FEATURES), BF16),
            jax.ShapeDtypeStruct((1, FEATURES), F32),
        ]
        + QUARTER_SHAPES,
        compiler_params=params(),
        cost_estimate=cost(8 * MIB),
    )(at, recv, cot, weights, weights)


def second_kernel(at, ranks, x0_ref, cot, u0_ref, v1_ref, bias, pair, base_out, bias_out, q0, q1, q2, q3, total):
    step = pl.program_id(0)
    u0, v1 = weight(u0_ref), weight(v1_ref)
    x0 = x0_ref[...].astype(F32)
    hidden = dot(ranks[:SAMPLES, :], u0, 1, 0) + bias[0:1, :]
    upstream = cot[...].astype(F32) + dot(ranks[SAMPLES:, :], v1, 1, 0)
    x1 = (x0 * hidden + x0).astype(BF16)
    hg = (upstream * x0).astype(BF16)
    pair[0] = hg
    pair[1] = x1
    base_out[...] = upstream + upstream * hidden
    bias_out[...] = jnp.sum(hg.astype(F32), axis=0, keepdims=True)
    rank = dot(x1, v1, 1, 1)
    rank_grad = dot(hg, u0, 1, 1)

    @pl.when(step == 0)
    def _():
        total[:SAMPLES, :] = rank
        total[SAMPLES:, :] = rank_grad

    @pl.when(step > 0)
    def _():
        total[:SAMPLES, :] += rank
        total[SAMPLES:, :] += rank_grad

    @pl.when(step == pl.num_programs(0) - 1)
    def _():
        write_quarters(at, total, (q0, q1, q2, q3))


def second(at, ranks, pair, cot, weights, bias):
    return pl.pallas_call(
        second_kernel,
        grid_spec=pltpu.PrefetchScalarGridSpec(
            num_scalar_prefetch=1,
            grid=(FEATURE_STEPS,),
            in_specs=[
                whole_spec(2 * SAMPLES, RANK),
                pair_spec(1),
                feature_spec(SAMPLES),
                weight_spec(U0),
                weight_spec(V1),
                feature_spec(2),
            ],
            out_specs=[
                pair_spec(),
                feature_spec(SAMPLES),
                feature_spec(1),
            ]
            + QUARTER_SPECS,
            scratch_shapes=[pltpu.VMEM((2 * SAMPLES, RANK), F32)],
        ),
        out_shape=[
            jax.ShapeDtypeStruct((2, SAMPLES, FEATURES), BF16),
            jax.ShapeDtypeStruct((SAMPLES, FEATURES), F32),
            jax.ShapeDtypeStruct((1, FEATURES), F32),
        ]
        + QUARTER_SHAPES,
        compiler_params=params(),
        cost_estimate=cost(10 * MIB),
    )(at, ranks, pair, cot, weights, weights, bias)


def third_kernel(at, ranks, x0_ref, x1_ref, cot, base, u1_ref, v0_ref, bias, sum0, sum1, crossed, back):
    hidden = dot(ranks[:SAMPLES, :], weight(u1_ref), 1, 0) + bias[1:2, :]
    crossed[...] = (x0_ref[...].astype(F32) * hidden + x1_ref[...].astype(F32)).astype(BF16)
    grad = base[...] + dot(ranks[SAMPLES:, :], weight(v0_ref), 1, 0) + cot[...].astype(F32) * hidden
    grad = grad.astype(BF16)
    for table in range(TABLES_STEP):
        columns = slice(table * PROJ, (table + 1) * PROJ)
        back[table, :HALF, :] = jnp.concatenate([grad[:HALF, columns], grad[HALF:, columns]], axis=1)
        row = jnp.concatenate([sum0[:, columns], sum1[:, columns]], axis=1)
        first_row = lax.broadcasted_iota(jnp.int32, (16, EMB), 0) == 0
        back[table, HALF:, :] = jnp.where(first_row, row, 0.0).astype(BF16)


def third(at, ranks, pair_0, pair_1, cot, base, weights, bias, sum0, sum1):
    return pl.pallas_call(
        third_kernel,
        grid_spec=pltpu.PrefetchScalarGridSpec(
            num_scalar_prefetch=1,
            grid=(FEATURE_STEPS,),
            in_specs=[whole_spec(2 * SAMPLES, RANK), pair_spec(1), pair_spec(1)]
            + [feature_spec(SAMPLES)] * 2
            + [weight_spec(U1), weight_spec(V0), feature_spec(2), feature_spec(1), feature_spec(1)],
            out_specs=[
                feature_spec(SAMPLES),
                pl.BlockSpec((TABLES_STEP, BACK_ROWS, EMB), lambda j, at: (j, 0, 0)),
            ],
        ),
        out_shape=[
            jax.ShapeDtypeStruct((SAMPLES, FEATURES), BF16),
            jax.ShapeDtypeStruct((FIELD_TABLES, BACK_ROWS, EMB), BF16),
        ],
        compiler_params=params(),
        cost_estimate=cost(MIB),
    )(at, ranks, pair_0, pair_1, cot, base, weights, weights, bias, sum0, sum1)


def terms_kernel(at, ranks, other_ranks, pair, other_pair, out, sides):
    @pl.when(pl.program_id(0) == 0)
    def _():
        is_first = at[AT_CORE] == 0
        for which in range(2):
            part = slice(which * SAMPLES, (which + 1) * SAMPLES)
            rows = jnp.concatenate([ranks[part, :], other_ranks[part, :]], axis=0).astype(F32)
            turned = rows.T.reshape(RANK // (CORES * SHARE), CORES, SHARE, 2 * SAMPLES)
            mine = jnp.where(is_first, turned[:, 0], turned[:, 1])
            sides[which] = mine.reshape(RANK // CORES, 2 * SAMPLES).astype(BF16)

    for which in range(2):
        side = jnp.concatenate([pair[which], other_pair[which]], axis=0)
        term = dot(sides[which], side, 1, 0).astype(BF16)
        out[:, :, which] = term.reshape(X_SIZE, Z_SIZE, SHARE, FEATURE_BLOCK)


GRAD_SHAPE = (X_SIZE, Z_SIZE, 2, SHARE, FEATURES)


def terms(at, ranks, other_ranks, pair, other_pair):
    return pl.pallas_call(
        terms_kernel,
        grid_spec=pltpu.PrefetchScalarGridSpec(
            num_scalar_prefetch=1,
            grid=(FEATURE_STEPS,),
            in_specs=[whole_spec(2 * SAMPLES, RANK)] * 2 + [pair_spec()] * 2,
            out_specs=pl.BlockSpec(GRAD_SHAPE[:-1] + (FEATURE_BLOCK,), lambda j, at: (0, 0, 0, 0, j)),
            scratch_shapes=[pltpu.VMEM((2, RANK // CORES, 2 * SAMPLES), BF16)],
        ),
        out_shape=jax.ShapeDtypeStruct(GRAD_SHAPE, BF16),
        compiler_params=params(),
        cost_estimate=cost(6 * MIB),
    )(at, ranks, other_ranks, pair, other_pair)


def z_sum_kernel(early, late, grad_u, grad_v):
    def total(blocks, which):
        a, b, c, d = (blocks[place, which].astype(F32) for place in range(Z_SIZE))
        return (a + b) + (c + d)

    grad_u[0] = total(early, 0)
    grad_v[1] = total(early, 1)
    grad_u[1] = total(late, 0)
    grad_v[0] = total(late, 1)


def z_sum(early, late):
    return pl.pallas_call(
        z_sum_kernel,
        out_shape=[jax.ShapeDtypeStruct((2, SHARE, FEATURES), F32)] * 2,
        compiler_params=params(),
        cost_estimate=cost(2 * MIB),
    )(early, late)


def last_kernel(at, back, pooled, proj, grad_pooled, grad_proj, grad_bias):
    step = pl.program_id(0)
    factor = masked_projection(proj, at[AT_WIDTH])
    none = jnp.zeros_like(factor)
    both = jnp.concatenate(
        [jnp.concatenate([factor, none], axis=1), jnp.concatenate([none, factor], axis=1)], axis=0
    )
    total = jnp.zeros((PROJ, EMB), F32)
    bias = jnp.zeros((1, EMB), F32)
    for block in range(back.shape[0]):
        grads = back[block, :HALF, :]
        start = block * SAMPLES
        out = dot(grads, both, 1, 0).astype(BF16)
        grad_pooled[start : start + HALF, :] = out[:, :EMB]
        grad_pooled[start + HALF : start + SAMPLES, :] = out[:, EMB:]
        upper = dot(grads, pooled[start : start + HALF, :], 0, 0)
        lower = dot(grads, pooled[start + HALF : start + SAMPLES, :], 0, 0)
        total += upper[:PROJ] + lower[PROJ:]
        bias += back[block, HALF:, :].astype(F32)[:1]

    @pl.when(step == 0)
    def _():
        grad_proj[...] = total
        grad_bias[...] = bias

    @pl.when(step > 0)
    def _():
        grad_proj[...] += total
        grad_bias[...] += bias


def last(at, back, pooled, proj):
    blocks = 8
    return pl.pallas_call(
        last_kernel,
        grid_spec=pltpu.PrefetchScalarGridSpec(
            num_scalar_prefetch=1,
            grid=(FIELD_TABLES // blocks,),
            in_specs=[
                pl.BlockSpec((blocks, BACK_ROWS, EMB), lambda i, at: (i, 0, 0)),
                pl.BlockSpec((blocks * SAMPLES, EMB), lambda i, at: (i, 0)),
                pl.BlockSpec((1, PROJ, EMB), lambda i, at: (at[AT_BATCH], 0, 0)),
            ],
            out_specs=[
                pl.BlockSpec((blocks * SAMPLES, EMB), lambda i, at: (i, 0)),
                whole_spec(PROJ, EMB),
                whole_spec(1, EMB),
            ],
        ),
        out_shape=[
            jax.ShapeDtypeStruct((TOKENS, EMB), BF16),
            jax.ShapeDtypeStruct((PROJ, EMB), F32),
            jax.ShapeDtypeStruct((1, EMB), F32),
        ],
        compiler_params=params(),
        cost_estimate=cost(5 * MIB),
    )(at, back, pooled, proj)


def batch_moves(move):
    pairs = []
    for source in range(X_SIZE * Z_SIZE * CORES):
        x, z, core = source // (Z_SIZE * CORES), source // CORES % Z_SIZE, source % CORES
        x, z, core = move(x, z, core)
        pairs.append((source, (x * Z_SIZE + z) * CORES + core))
    return pairs


def field_moves(move):
    pairs = []
    for source in range(Y_SIZE * HALVES):
        y, half = move(source // HALVES, source % HALVES)
        pairs.append((source, y * HALVES + half))
    return pairs


CORE_SWAP = batch_moves(lambda x, z, core: (x, z, 1 - core))
X_GROUPS = [
    [(x * Z_SIZE + z) * CORES + core for x in range(X_SIZE)] for z in range(Z_SIZE) for core in range(CORES)
]
Z_GROUPS = [
    [(x * Z_SIZE + z) * CORES + core for z in range(Z_SIZE)] for x in range(X_SIZE) for core in range(CORES)
]
Y_MOVES = [field_moves(lambda y, half, s=s: ((y + s) % Y_SIZE, half)) for s in range(Y_SIZE)]
HALF_SWAP = field_moves(lambda y, half: (y, 1 - half))


def exchange(parts, axis, moves):
    return [parts[0]] + [lax.ppermute(parts[s], axis, moves[s]) for s in range(1, len(parts))]


def scatter_sum(blocks, groups):
    return lax.psum_scatter(
        blocks, "batch", scatter_dimension=0, tiled=True, axis_index_groups=groups
    )


def low_sum(parts):
    wide = [part.astype(F32) for part in parts]
    total = wide[0]
    for part in wide[1:]:
        total = total + part
    return total.astype(BF16)


def to_all(blocks, axis, groups=None):
    return lax.all_to_all(
        blocks, axis, split_axis=0, concat_axis=0, tiled=True, axis_index_groups=groups
    )


def in_hbm(value):
    return pltpu.with_memory_space_constraint(value, pltpu.HBM)


def after(value, earlier):
    return lax.optimization_barrier((value, earlier))[0]


def core_swap(value):
    return lax.ppermute(value, "batch", CORE_SWAP)


def both_halves(partial):
    return low_sum([partial, lax.ppermute(partial, "field", HALF_SWAP)])


def on_device(
    emb_tables, bag_ids, bag_lengths, table_widths, projection, cross_u, cross_v, cross_bias, cotangent
):
    batch = lax.axis_index("batch")
    field = lax.axis_index("field")
    at = jnp.stack(
        [batch, batch // (Z_SIZE * CORES), batch // CORES % Z_SIZE, batch % CORES, field // HALVES, table_widths[0]]
    ).astype(jnp.int32)
    shard = jnp.concatenate([cross_u, cross_v], axis=0)
    weights = lax.all_gather(shard, "batch", axis=0, tiled=True)
    weights = in_hbm(weights.reshape(FIELD_TABLES, 4, SHARE, FEATURES))
    proj = jnp.transpose(projection, (0, 2, 1))

    places = lax.broadcasted_iota(jnp.int32, (BAG, TOKENS), 0)
    ids = jnp.where(places < bag_lengths, bag_ids[0].T, ROWS)
    ids = ids.reshape(BAG, TOKENS // 128, 128).transpose(1, 0, 2).reshape(-1)
    pooled, sent = pool(at, ids, in_hbm(emb_tables[0]), proj)
    recv = to_all(sent, "batch")

    pair_0, sum1, *parts = first(at, recv, cotangent, weights)
    other_0 = core_swap(pair_0)
    parts = exchange(parts, "field", Y_MOVES)
    partial = low_sum([after(parts[0], other_0)] + parts[1:])
    ranks = assemble(at, exchange([both_halves(partial)] * Y_SIZE, "field", Y_MOVES))
    other_ranks = core_swap(ranks)

    pair_1, base, sum0, *parts = second(at, ranks, pair_0, cotangent, weights, cross_bias)
    blocks = terms(at, ranks, other_ranks, pair_1, core_swap(pair_1))
    early = scatter_sum(blocks, X_GROUPS)[0]
    parts = exchange(parts, "field", Y_MOVES)
    partial = low_sum([after(parts[0], blocks)] + parts[1:])
    ranks = assemble(at, exchange([both_halves(partial)] * Y_SIZE, "field", Y_MOVES))

    blocks = terms(at, ranks, core_swap(ranks), pair_0, other_0)
    crossed, back = third(
        at, after(ranks, blocks), pair_0, pair_1, cotangent, base, weights, cross_bias, sum0, sum1
    )
    early = to_all(early, "batch", Z_GROUPS)
    returned = to_all(after(back, early), "batch")
    late = scatter_sum(blocks, X_GROUPS)[0]
    late = to_all(after(late, returned), "batch", Z_GROUPS)
    grad_u, grad_v = z_sum(early, late)
    grad_pooled, grad_proj, grad_bias = last(at, returned, pooled, proj)
    return (
        crossed,
        grad_u,
        grad_v,
        grad_bias.reshape(2, PROJ),
        grad_proj.T[None],
        grad_pooled[None],
    )


def solution(mesh):
    return jax.shard_map(
        on_device,
        mesh=mesh,
        in_specs=(
            P(("field", "batch"), None, None),
            P(("field", "batch"), None, None),
            P(("field", "batch"), None),
            P(("field", "batch")),
            P("field", None, None),
            P(None, "batch", "field"),
            P(None, "batch", "field"),
            P(None, "field"),
            P("batch", "field"),
        ),
        out_specs=(
            P("batch", "field"),
            P(None, "batch", "field"),
            P(None, "batch", "field"),
            P(None, ("field", "batch")),
            P(("field", "batch"), None, None),
            P(("field", "batch"), None, None),
        ),
        check_vma=False,
    )
```

time: 271 us -> 257 us (0.948)
  Pallas kernels: 95.3 us -> 71.7 us
  waiting for transfers between devices: 59.4 us -> 69 us
  starting transfers between devices: 52.9 us -> 46.8 us
  local copies, waits for them, and re-layouts: 8.65 us -> 13.7 us
    ppermute x24 -> x12, waiting for transfers between devices: 52.2 us -> 17.6 us  [exchange(): lax.ppermute(parts[s], axis, moves[s])]
    all_to_all x1 -> x3, waiting for transfers between devices: 0.01 us -> 31.7 us  [to_all(): lax.all_to_all(blocks, axis, split_axis=0, concat_axis=0, tiled=True, axi...]
    ppermute x24 -> x12, starting transfers between devices: 32 us -> 14.6 us  [exchange(): lax.ppermute(parts[s], axis, moves[s])]
    pallas_call x4 -> x2, Pallas kernels: 9.87 us -> 1.15 us  [assemble(): pl.pallas_call(assemble_kernel, grid_spec=pltpu.PrefetchScalarGridSpec(nu...]
    all_to_all x1 -> x3, starting transfers between devices: 8.05 us -> 14.8 us  [to_all(): lax.all_to_all(blocks, axis, split_axis=0, concat_axis=0, tiled=True, axi...]
    reduce_scatter x0 -> x2, waiting for transfers between devices: none -> 6.03 us  [scatter_sum(): lax.psum_scatter(blocks, 'batch', scatter_dimension=0, tiled=True, axis_i...]
    pallas_call x2, Pallas kernels: 11.4 us -> 5.88 us  [terms(): pl.pallas_call(terms_kernel, grid_spec=pltpu.PrefetchScalarGridSpec(num_s...]
    unnamed x20 -> x30, local copies, waits for them, and re-layouts: 7.41 us -> 12.5 us
  transfers between devices with their start and end apart: 30 -> 24, of which waited for: 14 -> 18; matrix products, arithmetic and copies ran while one was open for 1% -> 1% of each run, Pallas kernels for 29% -> 22%
where the time goes in v2:
time: 257 us
  Pallas kernels  71.7 us (28%)
  waiting for transfers between devices  69 us (27%)
  starting transfers between devices  46.8 us (18%)
  blocking collectives  37.2 us (14%)
  between operations  14.7 us (6%)
  local copies, waits for them, and re-layouts  13.7 us (5%)
  other arithmetic  3.52 us (1%)
    pallas_call x1, Pallas kernels, pool(): pl.pallas_call(pool_kernel, grid_spec=pltpu.PrefetchScalarGridSpec(num_sc...  44 us
    all_to_all x1, blocking collectives, to_all(): lax.all_to_all(blocks, axis, split_axis=0, concat_axis=0, tiled=True, axi...  37.2 us
    all_to_all x3, waiting for transfers between devices, to_all(): lax.all_to_all(blocks, axis, split_axis=0, concat_axis=0, tiled=True, axi...  31.7 us
    ppermute x12, waiting for transfers between devices, exchange(): lax.ppermute(parts[s], axis, moves[s])  17.6 us
    all_to_all x3, starting transfers between devices, to_all(): lax.all_to_all(blocks, axis, split_axis=0, concat_axis=0, tiled=True, axi...  14.8 us
    ppermute x12, starting transfers between devices, exchange(): lax.ppermute(parts[s], axis, moves[s])  14.6 us
    unnamed x30, local copies, waits for them, and re-layouts  12.5 us
    ppermute x2, starting transfers between devices, both_halves(): return low_sum([partial, lax.ppermute(partial, 'field', HALF_SWAP)])  10 us
  transfers between devices with their start and end apart: 24, of which 18 were waited for; matrix products, arithmetic and copies ran while one was open for 1% of the time, Pallas kernels for 22%

profile of v2, /device:TPU:1, one launch (start us, length us, event | category | flops | bytes accessed | tf_op | source)
XLA Modules:
  0.0 256.7 jit_solution(5963329389529483903)
XLA Ops:
  7.2 1.7 pad_maximum_fusion
  9.7 0.1 stack.23.at
  9.8 1.0 fusion.ids
  10.8 44.0 %shard_map.136 = (bf16[6144,128]{1,0:T(8,128)(2,1)S(1)}, bf16[32,96,128]{2,1,0:T(8,128)(2,1)S(1)}) custom-call(s32[6]{0:T(128)S(1)} %stack.23.at, s32[49152]{0:T(1024)S(1)} %fusion.ids, bf16[8192,128]{1,0:T(8,128)(2,1)} %bitcast.35, bf16[32,64,128]{2,1,0:T(8,128)(2,1)S(1)} %bitcast.27), custom_call_target="tpu_custom_call" | custom-call | bytes 104857600 | tf_op jit(solution)/shard_map/pallas_call | solution.py:93
  54.8 1.2 copy-done.9
  56.0 37.2 %all_to_all.20.recv = bf16[32,96,128]{2,1,0:T(8,128)(2,1)S(1)} all-to-all(bf16[32,96,128]{2,1,0:T(8,128)(2,1)S(1)} %get-tuple-element.33), channel_id=1, replica_groups=mesh['batch'=32,'field'=8] {'batch'}, dimensions={0} | all-to-all | bytes 1572864 | tf_op jit(solution)/shard_map/all_to_all | solution.py:493
  93.2 3.6 %all-gather.2.cloned.1.call-done = bf16[128,16,2048]{2,1,0:T(8,128)(2,1)} async-done(((bf16[4,16,2048]{2,1,0:T(8,128)(2,1)}), bf16[128,16,2048]{2,1,0:T(8,128)(2,1)}) %all-gather.2.cloned.1.call-update) | async-done | bytes 8388624 | tf_op jit(solution)/shard_map/all_gather | solution.py:523
  96.8 5.0 %shard_map.137 = (bf16[2,192,2048]{2,1,0:T(8,128)(2,1)S(1)}, f32[1,2048]{1,0:T(1,128)S(1)}, bf16[96,512]{1,0:T(8,128)(2,1)S(1)}, bf16[96,512]{1,0:T(8,128)(2,1)S...) custom-call(s32[6]{0:T(128)S(1)} %stack.23.at, bf16[32,96,128]{2,1,0:T(8,128)(2,1)S(1)} %all_to_all.20.recv, ...), custom_call_target="tpu_custom_call" | custom-call | bytes 8388608 | tf_op jit(solution)/shard_map/pallas_call | solution.py:208
  101.8 0.3 collective-permute-start
  102.2 1.3 collective-permute-start.1
  103.4 2.4 collective-permute-start.2
  105.8 1.1 collective-permute-start.3
  106.9 1.2 copy-done.11
  108.1 2.5 collective-permute-done.2
  110.6 4.8 %collective-permute-start.4 = (bf16[96,512]{1,0:T(8,128)(2,1)S(1)}, bf16[96,512]{1,0:T(8,128)(2,1)S(1)}, u32[]{:S(2)}, u32[]{:S(2)}) collective-permute-start(bf16[96,512]{1,0:T(8,128)(2,1)S(1)} %add_convert_fusion.3), channel_id=1, source_target_pairs={{0,1},{1,0},{2,3},{3,2},{4,5},{5,4},{6,7},{7,6},{8,9},{9,8},{10,11... | collective-permute-start | bytes 294920 | tf_op jit(solution)/shard_map/ppermute | solution.py:511
  115.5 2.7 %collective-permute-done.4 = bf16[96,512]{1,0:T(8,128)(2,1)S(1)} collective-permute-done((bf16[96,512]{1,0:T(8,128)(2,1)S(1)}, bf16[96,512]{1,0:T(8,128)(2,1)S(1)}, u32[]{:S(2)}, u32[]{:S(2)}) %collective-permute-start.4) | collective-permute-done | bytes 98336 | tf_op jit(solution)/shard_map/ppermute | solution.py:511
  118.2 1.8 collective-permute-start.7
  120.0 0.9 collective-permute-start.6
  121.0 0.2 collective-permute-start.5
  121.2 0.6 collective-permute-done.7.refs_3_
  121.8 3.3 %collective-permute-done.6.refs_2_ = bf16[96,512]{1,0:T(8,128)(2,1)S(1)} collective-permute-done((bf16[96,512]{1,0:T(8,128)(2,1)S(1)}, bf16[96,512]{1,0:T(8,128)(2,1)S(1)}, u32[]{:S(2)}, u32[]{:S(2)}) %collective-permute-start.6) | collective-permute-done | bytes 98336 | tf_op jit(solution)/shard_map/ppermute | solution.py:475
  125.1 1.0 collective-permute-done.5.refs_1_
  126.1 0.6 shard_map.138.ranks
  126.7 5.8 %shard_map.139 = (bf16[2,192,2048]{2,1,0:T(8,128)(2,1)S(1)}, f32[192,2048]{1,0:T(8,128)S(1)}, f32[1,2048]{1,0:T(1,128)S(1)}, bf16[96,512]{1,0:T(8,128)(2,1)S(1)}...) custom-call(s32[6]{0:T(128)S(1)} %stack.23.at, ...), custom_call_target="tpu_custom_call" | custom-call | bytes 10485760 | tf_op jit(solution)/shard_map/pallas_call | solution.py:263
  132.5 1.2 copy-done.7
  133.7 3.9 %collective-permute-start.9 = (bf16[2,192,2048]{2,1,0:T(8,128)(2,1)S(1)}, bf16[2,192,2048]{2,1,0:T(8,128)(2,1)S(1)}, u32[]{:S(2)}, u32[]{:S(2)}) collective-permute-start(bf16[2,192,2048]{2,1,0:T(8,128)(2,1)S(1)} %get-tuple-element.41.pair.x1_ref), channel_id=1, source_target_pairs={{0,8},{8,0},{16,24},{24,16},{32,40},{40,32},{48,56},{56,48},{64,72... | collective-permute-start | bytes 4718600 | tf_op jit(solution)/shard_map/ppermute | solution.py:507
  137.6 3.6 %collective-permute-done.8.other_ranks = bf16[384,512]{1,0:T(8,128)(2,1)S(1)} collective-permute-done((bf16[384,512]{1,0:T(8,128)(2,1)S(1)}, bf16[384,512]{1,0:T(8,128)(2,1)S(1)}, u32[]{:S(2)}, u32[]{:S(2)}) %collective-permute-start.8) | collective-permute-done | bytes 393248 | tf_op jit(solution)/shard_map/ppermute | solution.py:507
  141.2 2.9 %shard_map.140 = bf16[4,4,2,16,2048]{4,3,2,1,0:T(8,128)(2,1)S(1)} custom-call(s32[6]{0:T(128)S(1)} %stack.23.at, bf16[384,512]{1,0:T(8,128)(2,1)S(1)} %shard_map.138.ranks, bf16[384,512]{1,0:T(8,128)(2,1)S(1)} %collective-permute-done.8.other_ranks, bf16[2,192,2048]{2,1,0:T(8,128)(2,1)S(1)} %get-tuple-element.41.pair.x1_ref, ...), custom_call_target="tpu_custom_call" | custom-call | bytes 6291456 | tf_op jit(solution)/shard_map/pallas_call | solution.py:352
  144.2 1.4 copy-done
  145.5 1.1 copy-done.3
  146.8 0.1 collective-permute-start.10
  146.8 1.5 collective-permute-start.11
  148.3 1.5 collective-permute-start.12
  149.8 4.6 %collective-permute-done.10 = bf16[96,512]{1,0:T(8,128)(2,1)S(1)} collective-permute-done((bf16[96,512]{1,0:T(8,128)(2,1)S(1)}, bf16[96,512]{1,0:T(8,128)(2,1)S(1)}, u32[]{:S(2)}, u32[]{:S(2)}) %collective-permute-start.10) | collective-permute-done | bytes 98336 | tf_op jit(solution)/shard_map/ppermute | solution.py:475
  154.4 0.1 collective-permute-done.12
  154.5 5.2 %collective-permute-start.13 = (bf16[96,512]{1,0:T(8,128)(2,1)S(1)}, bf16[96,512]{1,0:T(8,128)(2,1)S(1)}, u32[]{:S(2)}, u32[]{:S(2)}) collective-permute-start(bf16[96,512]{1,0:T(8,128)(2,1)S(1)} %add_convert_fusion.1), channel_id=1, source_target_pairs={{0,1},{1,0},{2,3},{3,2},{4,5},{5,4},{6,7},{7,6},{8,9},{9,8},{10,11... | collective-permute-start | bytes 294920 | tf_op jit(solution)/shard_map/ppermute | solution.py:511
  159.8 2.3 collective-permute-done.13
  162.1 3.2 %collective-permute-start.16 = (bf16[96,512]{1,0:T(8,128)(2,1)S(1)}, bf16[96,512]{1,0:T(8,128)(2,1)S(1)}, u32[]{:S(2)}, u32[]{:S(2)}) collective-permute-start(bf16[96,512]{1,0:T(8,128)(2,1)S(1)} %add_convert_fusion.refs_0_), channel_id=1, source_target_pairs={{0,6},{1,7},{2,0},{3,1},{4,2},{5,3},{6,4},{7,5},{8,14},{9,15},{10,... | collective-permute-start | bytes 294920 | tf_op jit(solution)/shard_map/ppermute | solution.py:475
  165.4 0.7 collective-permute-start.14
  166.0 1.9 collective-permute-done.16.refs_3_
  168.0 2.5 collective-permute-done.15.refs_2_
  170.4 1.1 collective-permute-done.14.refs_1_
  171.5 0.6 shard_map.141.ranks
  172.1 3.0 %collective-permute-start.17 = (bf16[384,512]{1,0:T(8,128)(2,1)S(1)}, bf16[384,512]{1,0:T(8,128)(2,1)S(1)}, u32[]{:S(2)}, u32[]{:S(2)}) collective-permute-start(bf16[384,512]{1,0:T(8,128)(2,1)S(1)} %shard_map.141.ranks), channel_id=1, source_target_pairs={{0,8},{8,0},{16,24},{24,16},{32,40},{40,32},{48,56},{56,48},{64,72... | collective-permute-start | bytes 1179656 | tf_op jit(solution)/shard_map/ppermute | solution.py:507
  175.1 1.3 collective-permute-done.17.other_ranks
  176.4 2.9 %shard_map.142 = bf16[4,4,2,16,2048]{4,3,2,1,0:T(8,128)(2,1)S(1)} custom-call(s32[6]{0:T(128)S(1)} %stack.23.at, bf16[384,512]{1,0:T(8,128)(2,1)S(1)} %shard_map.141.ranks, bf16[384,512]{1,0:T(8,128)(2,1)S(1)} %collective-permute-done.17.other_ranks, bf16[2,192,2048]{2,1,0:T(8,128)(2,1)S(1)} %get-tuple-element.35.x0_ref.pair, ...), custom_call_target="tpu_custom_call" | custom-call | bytes 6291456 | tf_op jit(solution)/shard_map/pallas_call | solution.py:352
  179.4 1.3 copy-done.1
  180.8 6.5 %all-to-all-start.1 = ((bf16[4,2,16,2048]{3,2,1,0:T(8,128)(2,1)}), bf16[4,2,16,2048]{3,2,1,0:T(8,128)(2,1)S(1)}, u32[]{:S(2)}, u32[]{:S(2)}) async-start(bf16[4,2,16,2048]{3,2,1,0:T(8,128)(2,1)} %bitcast.36), calls=%async_computation.2 | async-start | bytes 1048576 | tf_op jit(solution)/shard_map/all_to_all | solution.py:493
  187.2 1.4 copy-done.4
  188.6 1.4 copy-done.8
  190.1 5.6 %shard_map.143 = (bf16[192,2048]{1,0:T(8,128)(2,1)}, bf16[32,112,128]{2,1,0:T(8,128)(2,1)S(1)}) custom-call(s32[6]{0:T(128)S(1)} %stack.23.at, bf16[384,512]{1,0:T(8,128)(2,1)S(1)} %shard_map.141.ranks, bf16[2,192,2048]{2,1,0:T(8,128)(2,1)S(1)} %get-tuple-element.35.x0_ref.pair, bf16[2,192,2048]{2,1,0:T(8,128)(2,1)S(1)} %copy-done.4, ...), custom_call_target="tpu_custom_call" | custom-call | bytes 1048576 | tf_op jit(solution)/shard_map/pallas_call | solution.py:309
  195.6 0.9 copy-done.13
  196.6 4.8 %all-to-all-done.1.early = bf16[4,2,16,2048]{3,2,1,0:T(8,128)(2,1)S(1)} async-done(((bf16[4,2,16,2048]{3,2,1,0:T(8,128)(2,1)}), bf16[4,2,16,2048]{3,2,1,0:T(8,128)(2,1)S(1)}, u32[]{:S(2)}, u32[]{:S(2)}) %all-to-all-start.1) | async-done | bytes 524320 | tf_op jit(solution)/shard_map/all_to_all | solution.py:493
  201.4 4.9 %all-to-all-start.2 = ((bf16[32,112,128]{2,1,0:T(8,128)(2,1)}), bf16[32,112,128]{2,1,0:T(8,128)(2,1)S(1)}, u32[]{:S(2)}, u32[]{:S(2)}) async-start(bf16[32,112,128]{2,1,0:T(8,128)(2,1)} %copy-done.13), calls=%async_computation.4 | async-start | bytes 1835008 | tf_op jit(solution)/shard_map/all_to_all | solution.py:493
  206.3 6.0 %reduce-scatter.5.cloned.1.call-done = bf16[1,4,2,16,2048]{4,3,2,1,0:T(8,128)(2,1)} async-done(((bf16[4,4,2,16,2048]{4,3,2,1,0:T(8,128)(2,1)}), bf16[1,4,2,16,2048]{4,3,2,1,0:T(8,128)(2,1)}) %reduce-scatter.5.cloned.1.call-update) | async-done | bytes 524304 | tf_op jit(solution)/shard_map/reduce_scatter | solution.py:479
  212.3 19.2 %all-to-all-done.2.back = bf16[32,112,128]{2,1,0:T(8,128)(2,1)S(1)} async-done(((bf16[32,112,128]{2,1,0:T(8,128)(2,1)}), bf16[32,112,128]{2,1,0:T(8,128)(2,1)S(1)}, u32[]{:S(2)}, u32[]{:S(2)}) %all-to-all-start.2) | async-done | bytes 917536 | tf_op jit(solution)/shard_map/all_to_all | solution.py:493
  231.5 3.5 %all-to-all-start.3 = ((bf16[4,2,16,2048]{3,2,1,0:T(8,128)(2,1)}), bf16[4,2,16,2048]{3,2,1,0:T(8,128)(2,1)S(1)}, u32[]{:S(2)}, u32[]{:S(2)}) async-start(bf16[4,2,16,2048]{3,2,1,0:T(8,128)(2,1)} %bitcast.37), calls=%async_computation.5 | async-start | bytes 1048576 | tf_op jit(solution)/shard_map/all_to_all | solution.py:493
  235.0 1.4 copy-done.10
  236.4 3.4 %shard_map.145 = (bf16[6144,128]{1,0:T(8,128)(2,1)}, f32[64,128]{1,0:T(8,128)}, f32[1,128]{1,0:T(1,128)S(1)}) custom-call(s32[6]{0:T(128)S(1)} %stack.23.at, bf16[32,112,128]{2,1,0:T(8,128)(2,1)S(1)} %all-to-all-done.2.back, bf16[6144,128]{1,0:T(8,128)(2,1)S(1)} %copy-done.10, bf16[32,64,128]{2,1,0:T(8,128)(2,1)S(1)} %bitcast.28), custom_call_target="tpu_custom_call" | custom-call | bytes 5242880 | tf_op jit(solution)/shard_map/pallas_call | solution.py:420
  239.8 0.5 broadcast.8
  240.3 0.7 reduce.3
  240.9 0.6 reshape.27
  241.6 7.7 %all-to-all-done.3.late = bf16[4,2,16,2048]{3,2,1,0:T(8,128)(2,1)S(1)} async-done(((bf16[4,2,16,2048]{3,2,1,0:T(8,128)(2,1)}), bf16[4,2,16,2048]{3,2,1,0:T(8,128)(2,1)S(1)}, u32[]{:S(2)}, u32[]{:S(2)}) %all-to-all-start.3) | async-done | bytes 524320 | tf_op jit(solution)/shard_map/all_to_all | solution.py:493
  249.3 0.9 shard_map.144
  (38 shorter events, 0.4 us)
Async XLA Ops:
  7.2 3.6 %copy-start.5 = (bf16[32,128,64]{1,2,0:T(8,128)(2,1)S(1)}, bf16[32,128,64]{1,2,0:T(8,128)(2,1)}, u32[]{:S(2)}) copy-start(bf16[32,128,64]{1,2,0:T(8,128)(2,1)} %param.13) | copy-start | bytes 1572868
  7.2 89.6 %all-gather.2.cloned.1.call-start = ((), (), s32[]{:S(2)}) async-start(), calls=%async_computation.6 | async-start | bytes 8650752 | tf_op jit(solution)/shard_map/all_gather | solution.py:523
  9.0 171.8 %reduce-scatter.3.cloned.1.call-start = ((), (), s32[]{:S(2)}) async-start(), calls=%async_computation.7 | async-start | bytes 2621440 | tf_op jit(solution)/shard_map/reduce_scatter | solution.py:479
  10.8 86.0 %copy-start.2 = (bf16[192,2048]{1,0:T(8,128)(2,1)S(1)}, bf16[192,2048]{1,0:T(8,128)(2,1)}, u32[]{:S(2)}) copy-start(bf16[192,2048]{1,0:T(8,128)(2,1)} %cot.5) | copy-start | bytes 2359300
  54.8 1.2 copy-start.9
  101.8 24.8 %copy-start.14 = (f32[2,2048]{1,0:T(2,128)S(1)}, f32[2,2048]{1,0:T(2,128)}, u32[]{:S(2)}) copy-start(f32[2,2048]{1,0:T(2,128)} %bias.3) | copy-start | bytes 49156
  101.8 5.1 %collective-permute-start = (bf16[2,192,2048]{2,1,0:T(8,128)(2,1)S(1)}, bf16[2,192,2048]{2,1,0:T(8,128)(2,1)S(1)}, u32[]{:S(2)}, u32[]{:S(2)}) collective-permute-start(bf16[2,192,2048]{2,1,0:T(8,128)(2,1)S(1)} %get-tuple-element.35.x0_ref.pair), channel_id=1, source_target_pairs={{0,8},{8,0},{16,24},{24,16},{32,40},{40,32},{48,56},{56,48},{64,72... | collective-permute-start | bytes 4718600 | tf_op jit(solution)/shard_map/ppermute | solution.py:507
  102.2 5.9 %collective-permute-start.1 = (bf16[96,512]{1,0:T(8,128)(2,1)S(1)}, bf16[96,512]{1,0:T(8,128)(2,1)S(1)}, u32[]{:S(2)}, u32[]{:S(2)}) collective-permute-start(bf16[96,512]{1,0:T(8,128)(2,1)S(1)} %get-tuple-element.37), channel_id=1, source_target_pairs={{0,2},{1,3},{2,4},{3,5},{4,6},{5,7},{6,0},{7,1},{8,10},{9,11},{10,... | collective-permute-start | bytes 294920 | tf_op jit(solution)/shard_map/ppermute | solution.py:475
  103.4 7.2 %collective-permute-start.2 = (bf16[96,512]{1,0:T(8,128)(2,1)S(1)}, bf16[96,512]{1,0:T(8,128)(2,1)S(1)}, u32[]{:S(2)}, u32[]{:S(2)}) collective-permute-start(bf16[96,512]{1,0:T(8,128)(2,1)S(1)} %get-tuple-element.38), channel_id=1, source_target_pairs={{0,4},{1,5},{2,6},{3,7},{4,0},{5,1},{6,2},{7,3},{8,12},{9,13},{10,... | collective-permute-start | bytes 294920 | tf_op jit(solution)/shard_map/ppermute | solution.py:475
  105.8 4.8 %collective-permute-start.3 = (bf16[96,512]{1,0:T(8,128)(2,1)S(1)}, bf16[96,512]{1,0:T(8,128)(2,1)S(1)}, u32[]{:S(2)}, u32[]{:S(2)}) collective-permute-start(bf16[96,512]{1,0:T(8,128)(2,1)S(1)} %get-tuple-element.39), channel_id=1, source_target_pairs={{0,6},{1,7},{2,0},{3,1},{4,2},{5,3},{6,4},{7,5},{8,14},{9,15},{10,... | collective-permute-start | bytes 294920 | tf_op jit(solution)/shard_map/ppermute | solution.py:475
  106.9 1.2 copy-start.11
  110.6 7.6 %collective-permute-start.4 = (bf16[96,512]{1,0:T(8,128)(2,1)S(1)}, bf16[96,512]{1,0:T(8,128)(2,1)S(1)}, u32[]{:S(2)}, u32[]{:S(2)}) collective-permute-start(bf16[96,512]{1,0:T(8,128)(2,1)S(1)} %add_convert_fusion.3), channel_id=1, source_target_pairs={{0,1},{1,0},{2,3},{3,2},{4,5},{5,4},{6,7},{7,6},{8,9},{9,8},{10,11... | collective-permute-start | bytes 294920 | tf_op jit(solution)/shard_map/ppermute | solution.py:511
  118.2 3.5 %collective-permute-start.7 = (bf16[96,512]{1,0:T(8,128)(2,1)S(1)}, bf16[96,512]{1,0:T(8,128)(2,1)S(1)}, u32[]{:S(2)}, u32[]{:S(2)}) collective-permute-start(bf16[96,512]{1,0:T(8,128)(2,1)S(1)} %add_convert_fusion.2.refs_0_), channel_id=1, source_target_pairs={{0,6},{1,7},{2,0},{3,1},{4,2},{5,3},{6,4},{7,5},{8,14},{9,15},{10,... | collective-permute-start | bytes 294920 | tf_op jit(solution)/shard_map/ppermute | solution.py:475
  120.0 5.0 %collective-permute-start.6 = (bf16[96,512]{1,0:T(8,128)(2,1)S(1)}, bf16[96,512]{1,0:T(8,128)(2,1)S(1)}, u32[]{:S(2)}, u32[]{:S(2)}) collective-permute-start(bf16[96,512]{1,0:T(8,128)(2,1)S(1)} %add_convert_fusion.2.refs_0_), channel_id=1, source_target_pairs={{0,4},{1,5},{2,6},{3,7},{4,0},{5,1},{6,2},{7,3},{8,12},{9,13},{10,... | collective-permute-start | bytes 294920 | tf_op jit(solution)/shard_map/ppermute | solution.py:475
  121.0 5.1 %collective-permute-start.5 = (bf16[96,512]{1,0:T(8,128)(2,1)S(1)}, bf16[96,512]{1,0:T(8,128)(2,1)S(1)}, u32[]{:S(2)}, u32[]{:S(2)}) collective-permute-start(bf16[96,512]{1,0:T(8,128)(2,1)S(1)} %add_convert_fusion.2.refs_0_), channel_id=1, source_target_pairs={{0,2},{1,3},{2,4},{3,5},{4,6},{5,7},{6,0},{7,1},{8,10},{9,11},{10,... | collective-permute-start | bytes 294920 | tf_op jit(solution)/shard_map/ppermute | solution.py:475
  132.5 1.2 copy-start.7
  133.7 7.5 %collective-permute-start.9 = (bf16[2,192,2048]{2,1,0:T(8,128)(2,1)S(1)}, bf16[2,192,2048]{2,1,0:T(8,128)(2,1)S(1)}, u32[]{:S(2)}, u32[]{:S(2)}) collective-permute-start(bf16[2,192,2048]{2,1,0:T(8,128)(2,1)S(1)} %get-tuple-element.41.pair.x1_ref), channel_id=1, source_target_pairs={{0,8},{8,0},{16,24},{24,16},{32,40},{40,32},{48,56},{56,48},{64,72... | collective-permute-start | bytes 4718600 | tf_op jit(solution)/shard_map/ppermute | solution.py:507
  137.6 3.6 %collective-permute-start.8 = (bf16[384,512]{1,0:T(8,128)(2,1)S(1)}, bf16[384,512]{1,0:T(8,128)(2,1)S(1)}, u32[]{:S(2)}, u32[]{:S(2)}) collective-permute-start(bf16[384,512]{1,0:T(8,128)(2,1)S(1)} %shard_map.138.ranks), channel_id=1, source_target_pairs={{0,8},{8,0},{16,24},{24,16},{32,40},{40,32},{48,56},{56,48},{64,72... | collective-permute-start | bytes 1179656 | tf_op jit(solution)/shard_map/ppermute | solution.py:507
  144.1 1.4 copy-start
  145.5 1.1 copy-start.3
  146.7 65.6 %reduce-scatter.5.cloned.1.call-start = ((), (), s32[]{:S(2)}) async-start(), calls=%async_computation.8 | async-start | bytes 2621440 | tf_op jit(solution)/shard_map/reduce_scatter | solution.py:479
  146.7 29.7 %copy-start.12 = (bf16[2,192,2048]{2,1,0:T(8,128)(2,1)S(1)}, bf16[2,192,2048]{2,1,0:T(8,128)(2,1)}, u32[]{:S(2)}) copy-start(bf16[2,192,2048]{2,1,0:T(8,128)(2,1)} %copy-done.11) | copy-start | bytes 4718596
  146.8 7.6 %collective-permute-start.10 = (bf16[96,512]{1,0:T(8,128)(2,1)S(1)}, bf16[96,512]{1,0:T(8,128)(2,1)S(1)}, u32[]{:S(2)}, u32[]{:S(2)}) collective-permute-start(bf16[96,512]{1,0:T(8,128)(2,1)S(1)} %get-tuple-element.43), channel_id=1, source_target_pairs={{0,2},{1,3},{2,4},{3,5},{4,6},{5,7},{6,0},{7,1},{8,10},{9,11},{10,... | collective-permute-start | bytes 294920 | tf_op jit(solution)/shard_map/ppermute | solution.py:475
  146.8 7.5 %collective-permute-start.11 = (bf16[96,512]{1,0:T(8,128)(2,1)S(1)}, bf16[96,512]{1,0:T(8,128)(2,1)S(1)}, u32[]{:S(2)}, u32[]{:S(2)}) collective-permute-start(bf16[96,512]{1,0:T(8,128)(2,1)S(1)} %get-tuple-element.44), channel_id=1, source_target_pairs={{0,4},{1,5},{2,6},{3,7},{4,0},{5,1},{6,2},{7,3},{8,12},{9,13},{10,... | collective-permute-start | bytes 294920 | tf_op jit(solution)/shard_map/ppermute | solution.py:475
  148.3 6.2 %collective-permute-start.12 = (bf16[96,512]{1,0:T(8,128)(2,1)S(1)}, bf16[96,512]{1,0:T(8,128)(2,1)S(1)}, u32[]{:S(2)}, u32[]{:S(2)}) collective-permute-start(bf16[96,512]{1,0:T(8,128)(2,1)S(1)} %get-tuple-element.45), channel_id=1, source_target_pairs={{0,6},{1,7},{2,0},{3,1},{4,2},{5,3},{6,4},{7,5},{8,14},{9,15},{10,... | collective-permute-start | bytes 294920 | tf_op jit(solution)/shard_map/ppermute | solution.py:475
  154.5 7.5 %collective-permute-start.13 = (bf16[96,512]{1,0:T(8,128)(2,1)S(1)}, bf16[96,512]{1,0:T(8,128)(2,1)S(1)}, u32[]{:S(2)}, u32[]{:S(2)}) collective-permute-start(bf16[96,512]{1,0:T(8,128)(2,1)S(1)} %add_convert_fusion.1), channel_id=1, source_target_pairs={{0,1},{1,0},{2,3},{3,2},{4,5},{5,4},{6,7},{7,6},{8,9},{9,8},{10,11... | collective-permute-start | bytes 294920 | tf_op jit(solution)/shard_map/ppermute | solution.py:511
  162.1 5.8 %collective-permute-start.16 = (bf16[96,512]{1,0:T(8,128)(2,1)S(1)}, bf16[96,512]{1,0:T(8,128)(2,1)S(1)}, u32[]{:S(2)}, u32[]{:S(2)}) collective-permute-start(bf16[96,512]{1,0:T(8,128)(2,1)S(1)} %add_convert_fusion.refs_0_), channel_id=1, source_target_pairs={{0,6},{1,7},{2,0},{3,1},{4,2},{5,3},{6,4},{7,5},{8,14},{9,15},{10,... | collective-permute-start | bytes 294920 | tf_op jit(solution)/shard_map/ppermute | solution.py:475
  165.4 5.1 %collective-permute-start.15 = (bf16[96,512]{1,0:T(8,128)(2,1)S(1)}, bf16[96,512]{1,0:T(8,128)(2,1)S(1)}, u32[]{:S(2)}, u32[]{:S(2)}) collective-permute-start(bf16[96,512]{1,0:T(8,128)(2,1)S(1)} %add_convert_fusion.refs_0_), channel_id=1, source_target_pairs={{0,4},{1,5},{2,6},{3,7},{4,0},{5,1},{6,2},{7,3},{8,12},{9,13},{10,... | collective-permute-start | bytes 294920 | tf_op jit(solution)/shard_map/ppermute | solution.py:475
  165.4 6.1 %collective-permute-start.14 = (bf16[96,512]{1,0:T(8,128)(2,1)S(1)}, bf16[96,512]{1,0:T(8,128)(2,1)S(1)}, u32[]{:S(2)}, u32[]{:S(2)}) collective-permute-start(bf16[96,512]{1,0:T(8,128)(2,1)S(1)} %add_convert_fusion.refs_0_), channel_id=1, source_target_pairs={{0,2},{1,3},{2,4},{3,5},{4,6},{5,7},{6,0},{7,1},{8,10},{9,11},{10,... | collective-permute-start | bytes 294920 | tf_op jit(solution)/shard_map/ppermute | solution.py:475
  172.1 4.4 %collective-permute-start.17 = (bf16[384,512]{1,0:T(8,128)(2,1)S(1)}, bf16[384,512]{1,0:T(8,128)(2,1)S(1)}, u32[]{:S(2)}, u32[]{:S(2)}) collective-permute-start(bf16[384,512]{1,0:T(8,128)(2,1)S(1)} %shard_map.141.ranks), channel_id=1, source_target_pairs={{0,8},{8,0},{16,24},{24,16},{32,40},{40,32},{48,56},{56,48},{64,72... | collective-permute-start | bytes 1179656 | tf_op jit(solution)/shard_map/ppermute | solution.py:507
  179.4 1.3 copy-start.1
  180.8 20.6 %all-to-all-start.1 = ((bf16[4,2,16,2048]{3,2,1,0:T(8,128)(2,1)}), bf16[4,2,16,2048]{3,2,1,0:T(8,128)(2,1)S(1)}, u32[]{:S(2)}, u32[]{:S(2)}) async-start(bf16[4,2,16,2048]{3,2,1,0:T(8,128)(2,1)} %bitcast.36), calls=%async_computation.2 | async-start | bytes 1048576 | tf_op jit(solution)/shard_map/all_to_all | solution.py:493
  187.2 1.4 copy-start.4
  188.6 1.4 copy-start.8
  195.6 0.9 copy-start.13
  196.6 38.4 %copy-start.6 = (bf16[32,128,64]{1,2,0:T(8,128)(2,1)S(1)}, bf16[32,128,64]{1,2,0:T(8,128)(2,1)}, u32[]{:S(2)}) copy-start(bf16[32,128,64]{1,2,0:T(8,128)(2,1)} %param.13) | copy-start | bytes 1572868
  201.4 30.1 %all-to-all-start.2 = ((bf16[32,112,128]{2,1,0:T(8,128)(2,1)}), bf16[32,112,128]{2,1,0:T(8,128)(2,1)S(1)}, u32[]{:S(2)}, u32[]{:S(2)}) async-start(bf16[32,112,128]{2,1,0:T(8,128)(2,1)} %copy-done.13), calls=%async_computation.4 | async-start | bytes 1835008 | tf_op jit(solution)/shard_map/all_to_all | solution.py:493
  231.5 17.8 %all-to-all-start.3 = ((bf16[4,2,16,2048]{3,2,1,0:T(8,128)(2,1)}), bf16[4,2,16,2048]{3,2,1,0:T(8,128)(2,1)S(1)}, u32[]{:S(2)}, u32[]{:S(2)}) async-start(bf16[4,2,16,2048]{3,2,1,0:T(8,128)(2,1)} %bitcast.37), calls=%async_computation.5 | async-start | bytes 1048576 | tf_op jit(solution)/shard_map/all_to_all | solution.py:493
  235.0 1.4 copy-start.10
Sparse Core Ops, SparseCore 0:
  10.4 86.2 all-gather.1
  146.8 29.0 reduce-scatter.2
  180.9 31.3 reduce-scatter.4

commit v3 on v2

--- a/solution.py
+++ b/solution.py
@@ -147,8 +147,7 @@
     return ref[...].reshape(RANK, FEATURE_BLOCK)
 
 
-def first_kernel(at, recv, cot, v0, u1, pair, bias_out, q0, q1, q2, q3, total):
-    step = pl.program_id(0)
+def unpack_kernel(recv, cot, pair, bias_out):
     columns = []
     for place in range(FEATURE_BLOCK // EMB):
         left, right = recv[2 * place], recv[2 * place + 1]
@@ -160,8 +159,33 @@
     pair[0] = hg
     pair[1] = x0
     bias_out[...] = jnp.sum(hg.astype(F32), axis=0, keepdims=True)
-    rank = dot(x0, weight(v0), 1, 1)
-    rank_grad = dot(hg, weight(u1), 1, 1)
+
+
+def unpack(recv, cot):
+    return pl.pallas_call(
+        unpack_kernel,
+        grid=(FEATURE_STEPS,),
+        in_specs=[
+            pl.BlockSpec((TABLES_STEP, HALF, EMB), lambda j: (j, 0, 0)),
+            pl.BlockSpec((SAMPLES, FEATURE_BLOCK), lambda j: (0, j)),
+        ],
+        out_specs=[
+            pl.BlockSpec((2, SAMPLES, FEATURE_BLOCK), lambda j: (0, 0, j)),
+            pl.BlockSpec((1, FEATURE_BLOCK), lambda j: (0, j)),
+        ],
+        out_shape=[
+            jax.ShapeDtypeStruct((2, SAMPLES, FEATURES), BF16),
+            jax.ShapeDtypeStruct((1, FEATURES), F32),
+        ],
+        compiler_params=params(),
+        cost_estimate=cost(4 * MIB),
+    )(recv, cot)
+
+
+def first_kernel(at, pair, v0, u1, q0, q1, q2, q3, total):
+    step = pl.program_id(0)
+    rank = dot(pair[1], weight(v0), 1, 1)
+    rank_grad = dot(pair[0], weight(u1), 1, 1)
 
     @pl.when(step == 0)
     def _():
@@ -204,29 +228,20 @@
 TABLES_STEP = FEATURE_BLOCK // PROJ
 
 
-def first(at, recv, cot, weights):
+def first(at, pair, weights):
     return pl.pallas_call(
         first_kernel,
         grid_spec=pltpu.PrefetchScalarGridSpec(
             num_scalar_prefetch=1,
             grid=(FEATURE_STEPS,),
-            in_specs=[
-                pl.BlockSpec((TABLES_STEP, HALF, EMB), lambda j, at: (j, 0, 0)),
-                feature_spec(SAMPLES),
-                weight_spec(V0),
-                weight_spec(U1),
-            ],
-            out_specs=[pair_spec(), feature_spec(1)] + QUARTER_SPECS,
+            in_specs=[pair_spec(), weight_spec(V0), weight_spec(U1)],
+            out_specs=QUARTER_SPECS,
             scratch_shapes=[pltpu.VMEM((2 * SAMPLES, RANK), F32)],
         ),
-        out_shape=[
-            jax.ShapeDtypeStruct((2, SAMPLES, FEATURES), BF16),
-            jax.ShapeDtypeStruct((1, FEATURES), F32),
-        ]
-        + QUARTER_SHAPES,
+        out_shape=QUARTER_SHAPES,
         compiler_params=params(),
         cost_estimate=cost(8 * MIB),
-    )(at, recv, cot, weights, weights)
+    )(at, pair, weights, weights)
 
 
 def second_kernel(at, ranks, x0_ref, cot, u0_ref, v1_ref, bias, pair, base_out, bias_out, q0, q1, q2, q3, total):
@@ -364,9 +379,31 @@
     )(at, ranks, other_ranks, pair, other_pair)
 
 
-def z_sum_kernel(early, late, grad_u, grad_v):
+def z_split_kernel(at, blocks, *outs):
+    for shift, out in enumerate(outs):
+        out[...] = blocks[lax.rem(at[AT_Z] + shift, Z_SIZE)]
+
+
+def z_split(at, blocks):
+    return pl.pallas_call(
+        z_split_kernel,
+        grid_spec=pltpu.PrefetchScalarGridSpec(
+            num_scalar_prefetch=1,
+            grid=(1,),
+            in_specs=[whole_spec(*GRAD_SHAPE[1:])],
+            out_specs=[whole_spec(2, SHARE, FEATURES)] * Z_SIZE,
+        ),
+        out_shape=[jax.ShapeDtypeStruct((2, SHARE, FEATURES), BF16)] * Z_SIZE,
+        compiler_params=params(),
+        cost_estimate=cost(MIB),
+    )(at, blocks)
+
+
+def z_sum_kernel(*refs):
+    early, late, (grad_u, grad_v) = refs[:Z_SIZE], refs[Z_SIZE : 2 * Z_SIZE], refs[2 * Z_SIZE :]
+
     def total(blocks, which):
-        a, b, c, d = (blocks[place, which].astype(F32) for place in range(Z_SIZE))
+        a, b, c, d = (block[which].astype(F32) for block in blocks)
         return (a + b) + (c + d)
 
     grad_u[0] = total(early, 0)
@@ -381,7 +418,7 @@
         out_shape=[jax.ShapeDtypeStruct((2, SHARE, FEATURES), F32)] * 2,
         compiler_params=params(),
         cost_estimate=cost(2 * MIB),
-    )(early, late)
+    )(*early, *late)
 
 
 def last_kernel(at, back, pooled, proj, grad_pooled, grad_proj, grad_bias):
@@ -404,6 +441,8 @@
         total += upper[:PROJ] + lower[PROJ:]
         bias += back[block, HALF:, :].astype(F32)[:1]
 
+    bias = jnp.concatenate([bias[:, :PROJ], bias[:, PROJ:]], axis=0)
+
     @pl.when(step == 0)
     def _():
         grad_proj[...] = total
@@ -430,13 +469,13 @@
             out_specs=[
                 pl.BlockSpec((blocks * SAMPLES, EMB), lambda i, at: (i, 0)),
                 whole_spec(PROJ, EMB),
-                whole_spec(1, EMB),
+                whole_spec(2, PROJ),
             ],
         ),
         out_shape=[
             jax.ShapeDtypeStruct((TOKENS, EMB), BF16),
             jax.ShapeDtypeStruct((PROJ, EMB), F32),
-            jax.ShapeDtypeStruct((1, EMB), F32),
+            jax.ShapeDtypeStruct((2, PROJ), F32),
         ],
         compiler_params=params(),
         cost_estimate=cost(5 * MIB),
@@ -461,11 +500,9 @@
 
 
 CORE_SWAP = batch_moves(lambda x, z, core: (x, z, 1 - core))
+Z_MOVES = [batch_moves(lambda x, z, core, s=s: (x, (z + s) % Z_SIZE, core)) for s in range(Z_SIZE)]
 X_GROUPS = [
     [(x * Z_SIZE + z) * CORES + core for x in range(X_SIZE)] for z in range(Z_SIZE) for core in range(CORES)
-]
-Z_GROUPS = [
-    [(x * Z_SIZE + z) * CORES + core for z in range(Z_SIZE)] for x in range(X_SIZE) for core in range(CORES)
 ]
 Y_MOVES = [field_moves(lambda y, half, s=s: ((y + s) % Y_SIZE, half)) for s in range(Y_SIZE)]
 HALF_SWAP = field_moves(lambda y, half: (y, 1 - half))
@@ -489,10 +526,8 @@
     return total.astype(BF16)
 
 
-def to_all(blocks, axis, groups=None):
-    return lax.all_to_all(
-        blocks, axis, split_axis=0, concat_axis=0, tiled=True, axis_index_groups=groups
-    )
+def to_all(blocks):
+    return lax.all_to_all(blocks, "batch", split_axis=0, concat_axis=0, tiled=True)
 
 
 def in_hbm(value):
@@ -528,9 +563,10 @@
     ids = jnp.where(places < bag_lengths, bag_ids[0].T, ROWS)
     ids = ids.reshape(BAG, TOKENS // 128, 128).transpose(1, 0, 2).reshape(-1)
     pooled, sent = pool(at, ids, in_hbm(emb_tables[0]), proj)
-    recv = to_all(sent, "batch")
-
-    pair_0, sum1, *parts = first(at, recv, cotangent, weights)
+    recv = to_all(sent)
+
+    pair_0, sum1 = unpack(recv, cotangent)
+    parts = first(at, pair_0, weights)
     other_0 = core_swap(pair_0)
     parts = exchange(parts, "field", Y_MOVES)
     partial = low_sum([after(parts[0], other_0)] + parts[1:])
@@ -546,19 +582,28 @@
 
     blocks = terms(at, ranks, core_swap(ranks), pair_0, other_0)
     crossed, back = third(
-        at, after(ranks, blocks), pair_0, pair_1, cotangent, base, weights, cross_bias, sum0, sum1
-    )
-    early = to_all(early, "batch", Z_GROUPS)
-    returned = to_all(after(back, early), "batch")
-    late = scatter_sum(blocks, X_GROUPS)[0]
-    late = to_all(after(late, returned), "batch", Z_GROUPS)
-    grad_u, grad_v = z_sum(early, late)
-    grad_pooled, grad_proj, grad_bias = last(at, returned, pooled, proj)
+        at,
+        after(ranks, blocks),
+        in_hbm(pair_0),
+        in_hbm(pair_1),
+        in_hbm(cotangent),
+        in_hbm(base),
+        weights,
+        cross_bias,
+        sum0,
+        sum1,
+    )
+    early = exchange(z_split(at, early), "batch", Z_MOVES)
+    returned = to_all(after(back, early[1:]))
+    late = exchange(z_split(at, scatter_sum(blocks, X_GROUPS)[0]), "batch", Z_MOVES)
+    returned = after(returned, late[0])
+    grad_pooled, grad_proj, grad_bias = last(at, returned, in_hbm(pooled), proj)
+    grad_u, grad_v = z_sum(early, [after(late[0], grad_proj)] + late[1:])
     return (
         crossed,
         grad_u,
         grad_v,
-        grad_bias.reshape(2, PROJ),
+        grad_bias,
         grad_proj.T[None],
         grad_pooled[None],
     )

time: 257 us -> 250 us (0.973)
  waiting for transfers between devices: 69 us -> 60.8 us
  Pallas kernels: 71.7 us -> 77.3 us
  local copies, waits for them, and re-layouts: 13.7 us -> 8.35 us
    all_to_all x3 -> x1, waiting for transfers between devices: 31.7 us -> 11.3 us  [to_all(): lax.all_to_all(blocks, 'batch', split_axis=0, concat_axis=0, tiled=True)]
    ppermute x12 -> x18, starting transfers between devices: 14.6 us -> 24 us  [exchange(): lax.ppermute(parts[s], axis, moves[s])]
    reduce_scatter x2, waiting for transfers between devices: 6.03 us -> 13.1 us  [scatter_sum(): lax.psum_scatter(blocks, 'batch', scatter_dimension=0, tiled=True, axis_i...]
    all_to_all x3 -> x1, starting transfers between devices: 14.8 us -> 7.72 us  [to_all(): lax.all_to_all(blocks, 'batch', split_axis=0, concat_axis=0, tiled=True)]
    unnamed x30 -> x22, local copies, waits for them, and re-layouts: 12.5 us -> 8.26 us
    ppermute x12 -> x18, waiting for transfers between devices: 17.6 us -> 20.6 us  [exchange(): lax.ppermute(parts[s], axis, moves[s])]
  transfers between devices with their start and end apart: 24 -> 28, of which waited for: 18 -> 18; matrix products, arithmetic and copies ran while one was open for 1% -> 0% of each run, Pallas kernels for 22% -> 27%
where the time goes in v3:
time: 250 us
  Pallas kernels  77.3 us (31%)
  waiting for transfers between devices  60.8 us (24%)
  starting transfers between devices  48.3 us (19%)
  blocking collectives  37.2 us (15%)
  between operations  14.7 us (6%)
  local copies, waits for them, and re-layouts  8.35 us (3%)
  other arithmetic  2.86 us (1%)
    pallas_call x1, Pallas kernels, pool(): pl.pallas_call(pool_kernel, grid_spec=pltpu.PrefetchScalarGridSpec(num_sc...  44 us
    all_to_all x1, blocking collectives, to_all(): lax.all_to_all(blocks, 'batch', split_axis=0, concat_axis=0, tiled=True)  37.2 us
    ppermute x18, starting transfers between devices, exchange(): lax.ppermute(parts[s], axis, moves[s])  24 us
    ppermute x18, waiting for transfers between devices, exchange(): lax.ppermute(parts[s], axis, moves[s])  20.6 us
    reduce_scatter x2, waiting for transfers between devices, scatter_sum(): lax.psum_scatter(blocks, 'batch', scatter_dimension=0, tiled=True, axis_i...  13.1 us
    all_to_all x1, waiting for transfers between devices, to_all(): lax.all_to_all(blocks, 'batch', split_axis=0, concat_axis=0, tiled=True)  11.3 us
    ppermute x2, starting transfers between devices, both_halves(): return low_sum([partial, lax.ppermute(partial, 'field', HALF_SWAP)])  8.32 us
    unnamed x22, local copies, waits for them, and re-layouts  8.26 us
  transfers between devices with their start and end apart: 28, of which 18 were waited for; matrix products, arithmetic and copies ran while one was open for 0% of the time, Pallas kernels for 27%

profile of v3, /device:TPU:1, one launch (start us, length us, event | category | flops | bytes accessed | tf_op | source)
XLA Modules:
  0.0 249.6 jit_solution(14218046814292253787)
XLA Ops:
  7.2 1.7 pad_maximum_fusion
  9.7 0.1 stack.23.at
  9.8 1.0 fusion.ids
  10.8 44.0 %shard_map.136 = (bf16[6144,128]{1,0:T(8,128)(2,1)S(1)}, bf16[32,96,128]{2,1,0:T(8,128)(2,1)S(1)}) custom-call(s32[6]{0:T(128)S(1)} %stack.23.at, s32[49152]{0:T(1024)S(1)} %fusion.ids, bf16[8192,128]{1,0:T(8,128)(2,1)} %bitcast.37, bf16[32,64,128]{2,1,0:T(8,128)(2,1)S(1)} %bitcast.27), custom_call_target="tpu_custom_call" | custom-call | bytes 104857600 | tf_op jit(solution)/shard_map/pallas_call | solution.py:93
  54.8 1.1 copy-done.7
  55.9 37.2 %all_to_all.10.recv = bf16[32,96,128]{2,1,0:T(8,128)(2,1)S(1)} all-to-all(bf16[32,96,128]{2,1,0:T(8,128)(2,1)S(1)} %get-tuple-element.42), channel_id=1, replica_groups=mesh['batch'=32,'field'=8] {'batch'}, dimensions={0} | all-to-all | bytes 1572864 | tf_op jit(solution)/shard_map/all_to_all | solution.py:530
  93.1 0.9 shard_map.137
  94.0 0.1 collective-permute-start
  94.1 3.9 %all-gather.2.cloned.1.call-done = bf16[128,16,2048]{2,1,0:T(8,128)(2,1)} async-done(((bf16[4,16,2048]{2,1,0:T(8,128)(2,1)}), bf16[128,16,2048]{2,1,0:T(8,128)(2,1)}) %all-gather.2.cloned.1.call-update) | async-done | bytes 8388624 | tf_op jit(solution)/shard_map/all_gather | solution.py:558
  98.0 4.9 %shard_map.138 = (bf16[96,512]{1,0:T(8,128)(2,1)S(1)}, bf16[96,512]{1,0:T(8,128)(2,1)S(1)}, bf16[96,512]{1,0:T(8,128)(2,1)S(1)}, bf16[96,512]{1,0:T(8,128)(2,1)S(1)}) custom-call(s32[6]{0:T(128)S(1)} %stack.23.at, bf16[2,192,2048]{2,1,0:T(8,128)(2,1)S(1)} %get-tuple-element.43.pair.x0_ref, bf16[32,4,16,2048]{3,2,1,0:T(8,128)(2,1)} %bitcast.31, ...), custom_call_target="tpu_custom_call" | custom-call | bytes 8388608 | tf_op jit(solution)/shard_map/pallas_call | solution.py:232
  102.9 1.3 collective-permute-start.1
  104.3 2.4 collective-permute-start.2
  106.7 1.1 collective-permute-start.3
  107.8 0.6 collective-permute-done.1
  108.4 3.1 %collective-permute-done.2 = bf16[96,512]{1,0:T(8,128)(2,1)S(1)} collective-permute-done((bf16[96,512]{1,0:T(8,128)(2,1)S(1)}, bf16[96,512]{1,0:T(8,128)(2,1)S(1)}, u32[]{:S(2)}, u32[]{:S(2)}) %collective-permute-start.2) | collective-permute-done | bytes 98336 | tf_op jit(solution)/shard_map/ppermute | solution.py:512
  111.6 4.2 %collective-permute-start.4 = (bf16[96,512]{1,0:T(8,128)(2,1)S(1)}, bf16[96,512]{1,0:T(8,128)(2,1)S(1)}, u32[]{:S(2)}, u32[]{:S(2)}) collective-permute-start(bf16[96,512]{1,0:T(8,128)(2,1)S(1)} %add_convert_fusion.3), channel_id=1, source_target_pairs={{0,1},{1,0},{2,3},{3,2},{4,5},{5,4},{6,7},{7,6},{8,9},{9,8},{10,11... | collective-permute-start | bytes 294920 | tf_op jit(solution)/shard_map/ppermute | solution.py:546
  115.8 3.3 %collective-permute-done.4 = bf16[96,512]{1,0:T(8,128)(2,1)S(1)} collective-permute-done((bf16[96,512]{1,0:T(8,128)(2,1)S(1)}, bf16[96,512]{1,0:T(8,128)(2,1)S(1)}, u32[]{:S(2)}, u32[]{:S(2)}) %collective-permute-start.4) | collective-permute-done | bytes 98336 | tf_op jit(solution)/shard_map/ppermute | solution.py:546
  119.2 1.6 collective-permute-start.7
  120.8 0.7 collective-permute-start.6
  121.5 0.6 collective-permute-start.5
  122.1 0.6 collective-permute-done.7.refs_3_
  122.7 3.1 %collective-permute-done.6.refs_2_ = bf16[96,512]{1,0:T(8,128)(2,1)S(1)} collective-permute-done((bf16[96,512]{1,0:T(8,128)(2,1)S(1)}, bf16[96,512]{1,0:T(8,128)(2,1)S(1)}, u32[]{:S(2)}, u32[]{:S(2)}) %collective-permute-start.6) | collective-permute-done | bytes 98336 | tf_op jit(solution)/shard_map/ppermute | solution.py:512
  125.9 1.0 collective-permute-done.5.refs_1_
  126.8 0.6 shard_map.139.ranks
  127.4 5.8 %shard_map.140 = (bf16[2,192,2048]{2,1,0:T(8,128)(2,1)S(1)}, f32[192,2048]{1,0:T(8,128)S(1)}, f32[1,2048]{1,0:T(1,128)S(1)}, bf16[96,512]{1,0:T(8,128)(2,1)S(1)}...) custom-call(s32[6]{0:T(128)S(1)} %stack.23.at, ...), custom_call_target="tpu_custom_call" | custom-call | bytes 10485760 | tf_op jit(solution)/shard_map/pallas_call | solution.py:278
  133.3 1.2 copy-done.6
  134.4 5.0 %collective-permute-start.9 = (bf16[2,192,2048]{2,1,0:T(8,128)(2,1)S(1)}, bf16[2,192,2048]{2,1,0:T(8,128)(2,1)S(1)}, u32[]{:S(2)}, u32[]{:S(2)}) collective-permute-start(bf16[2,192,2048]{2,1,0:T(8,128)(2,1)S(1)} %get-tuple-element.50.pair.x1_ref), channel_id=1, source_target_pairs={{0,8},{8,0},{16,24},{24,16},{32,40},{40,32},{48,56},{56,48},{64,72... | collective-permute-start | bytes 4718600 | tf_op jit(solution)/shard_map/ppermute | solution.py:542
  139.4 3.6 %collective-permute-done.8.other_ranks = bf16[384,512]{1,0:T(8,128)(2,1)S(1)} collective-permute-done((bf16[384,512]{1,0:T(8,128)(2,1)S(1)}, bf16[384,512]{1,0:T(8,128)(2,1)S(1)}, u32[]{:S(2)}, u32[]{:S(2)}) %collective-permute-start.8) | collective-permute-done | bytes 393248 | tf_op jit(solution)/shard_map/ppermute | solution.py:542
  143.0 2.9 %shard_map.141 = bf16[4,4,2,16,2048]{4,3,2,1,0:T(8,128)(2,1)S(1)} custom-call(s32[6]{0:T(128)S(1)} %stack.23.at, bf16[384,512]{1,0:T(8,128)(2,1)S(1)} %shard_map.139.ranks, bf16[384,512]{1,0:T(8,128)(2,1)S(1)} %collective-permute-done.8.other_ranks, bf16[2,192,2048]{2,1,0:T(8,128)(2,1)S(1)} %get-tuple-element.50.pair.x1_ref, ...), custom_call_target="tpu_custom_call" | custom-call | bytes 6291456 | tf_op jit(solution)/shard_map/pallas_call | solution.py:367
  146.0 1.4 copy-done.1
  147.4 1.1 copy-done.4
  148.7 1.5 collective-permute-start.11
  150.1 1.3 collective-permute-start.12
  151.4 4.8 %collective-permute-done.10 = bf16[96,512]{1,0:T(8,128)(2,1)S(1)} collective-permute-done((bf16[96,512]{1,0:T(8,128)(2,1)S(1)}, bf16[96,512]{1,0:T(8,128)(2,1)S(1)}, u32[]{:S(2)}, u32[]{:S(2)}) %collective-permute-start.10) | collective-permute-done | bytes 98336 | tf_op jit(solution)/shard_map/ppermute | solution.py:512
  156.2 0.1 collective-permute-done.12
  156.4 4.1 %collective-permute-start.13 = (bf16[96,512]{1,0:T(8,128)(2,1)S(1)}, bf16[96,512]{1,0:T(8,128)(2,1)S(1)}, u32[]{:S(2)}, u32[]{:S(2)}) collective-permute-start(bf16[96,512]{1,0:T(8,128)(2,1)S(1)} %add_convert_fusion.1), channel_id=1, source_target_pairs={{0,1},{1,0},{2,3},{3,2},{4,5},{5,4},{6,7},{7,6},{8,9},{9,8},{10,11... | collective-permute-start | bytes 294920 | tf_op jit(solution)/shard_map/ppermute | solution.py:546
  160.5 3.5 %collective-permute-done.13 = bf16[96,512]{1,0:T(8,128)(2,1)S(1)} collective-permute-done((bf16[96,512]{1,0:T(8,128)(2,1)S(1)}, bf16[96,512]{1,0:T(8,128)(2,1)S(1)}, u32[]{:S(2)}, u32[]{:S(2)}) %collective-permute-start.13) | collective-permute-done | bytes 98336 | tf_op jit(solution)/shard_map/ppermute | solution.py:546
  164.0 3.0 %collective-permute-start.16 = (bf16[96,512]{1,0:T(8,128)(2,1)S(1)}, bf16[96,512]{1,0:T(8,128)(2,1)S(1)}, u32[]{:S(2)}, u32[]{:S(2)}) collective-permute-start(bf16[96,512]{1,0:T(8,128)(2,1)S(1)} %add_convert_fusion.refs_0_), channel_id=1, source_target_pairs={{0,6},{1,7},{2,0},{3,1},{4,2},{5,3},{6,4},{7,5},{8,14},{9,15},{10,... | collective-permute-start | bytes 294920 | tf_op jit(solution)/shard_map/ppermute | solution.py:512
  167.0 0.7 collective-permute-start.14
  167.7 1.9 collective-permute-done.16.refs_3_
  169.6 2.5 collective-permute-done.15.refs_2_
  172.0 1.1 collective-permute-done.14.refs_1_
  173.1 0.6 shard_map.142.ranks
  173.7 3.2 %collective-permute-start.17 = (bf16[384,512]{1,0:T(8,128)(2,1)S(1)}, bf16[384,512]{1,0:T(8,128)(2,1)S(1)}, u32[]{:S(2)}, u32[]{:S(2)}) collective-permute-start(bf16[384,512]{1,0:T(8,128)(2,1)S(1)} %shard_map.142.ranks), channel_id=1, source_target_pairs={{0,8},{8,0},{16,24},{24,16},{32,40},{40,32},{48,56},{56,48},{64,72... | collective-permute-start | bytes 1179656 | tf_op jit(solution)/shard_map/ppermute | solution.py:542
  176.9 1.3 collective-permute-done.17.other_ranks
  178.2 4.3 %shard_map.143 = bf16[4,4,2,16,2048]{4,3,2,1,0:T(8,128)(2,1)S(1)} custom-call(s32[6]{0:T(128)S(1)} %stack.23.at, bf16[384,512]{1,0:T(8,128)(2,1)S(1)} %shard_map.142.ranks, bf16[384,512]{1,0:T(8,128)(2,1)S(1)} %collective-permute-done.17.other_ranks, bf16[2,192,2048]{2,1,0:T(8,128)(2,1)S(1)} %get-tuple-element.43.pair.x0_ref, ...), custom_call_target="tpu_custom_call" | custom-call | bytes 6291456 | tf_op jit(solution)/shard_map/pallas_call | solution.py:367
  182.6 1.3 copy-done.2
  183.9 1.0 copy-done.8
  185.0 0.6 shard_map.145
  185.6 1.2 collective-permute-start.18
  186.8 1.3 collective-permute-start.19
  188.0 2.3 collective-permute-start.20
  190.3 6.4 %shard_map.144 = (bf16[192,2048]{1,0:T(8,128)(2,1)}, bf16[32,112,128]{2,1,0:T(8,128)(2,1)}) custom-call(s32[6]{0:T(128)S(1)} %stack.23.at, bf16[384,512]{1,0:T(8,128)(2,1)S(1)} %shard_map.142.ranks, bf16[2,192,2048]{2,1,0:T(8,128)(2,1)} %copy-done, bf16[2,192,2048]{2,1,0:T(8,128)(2,1)} %copy-done.4, bf16[192,2048]{1,0:T(8,128)(2,1)} %cot.5, ...), custom_call_target="tpu_custom_call" | custom-call | bytes 1048576 | tf_op jit(solution)/shard_map/pallas_call | solution.py:324
  196.7 1.9 collective-permute-done.19.refs_2_
  198.6 7.7 %all-to-all-start.1 = ((bf16[32,112,128]{2,1,0:T(8,128)(2,1)}), bf16[32,112,128]{2,1,0:T(8,128)(2,1)S(1)}, u32[]{:S(2)}, u32[]{:S(2)}) async-start(bf16[32,112,128]{2,1,0:T(8,128)(2,1)} %get-tuple-element.66), calls=%async_computation.3 | async-start | bytes 1835008 | tf_op jit(solution)/shard_map/all_to_all | solution.py:530
  206.3 13.1 %reduce-scatter.5.cloned.1.call-done = bf16[1,4,2,16,2048]{4,3,2,1,0:T(8,128)(2,1)} async-done(((bf16[4,4,2,16,2048]{4,3,2,1,0:T(8,128)(2,1)}), bf16[1,4,2,16,2048]{4,3,2,1,0:T(8,128)(2,1)}) %reduce-scatter.5.cloned.1.call-update) | async-done | bytes 524304 | tf_op jit(solution)/shard_map/reduce_scatter | solution.py:516
  219.4 1.0 copy-done.9
  220.5 0.6 shard_map.146
  221.0 1.0 collective-permute-start.21
  222.1 3.6 %collective-permute-start.22 = (bf16[2,16,2048]{2,1,0:T(8,128)(2,1)S(1)}, bf16[2,16,2048]{2,1,0:T(8,128)(2,1)S(1)}, u32[]{:S(2)}, u32[]{:S(2)}) collective-permute-start(bf16[2,16,2048]{2,1,0:T(8,128)(2,1)S(1)} %get-tuple-element.72), channel_id=1, source_target_pairs={{0,32},{8,40},{16,48},{24,56},{32,0},{40,8},{48,16},{56,24},{64,96... | collective-permute-start | bytes 393224 | tf_op jit(solution)/shard_map/ppermute | solution.py:512
  225.7 0.2 collective-permute-start.23
  225.9 11.3 %all-to-all-done.1.back = bf16[32,112,128]{2,1,0:T(8,128)(2,1)S(1)} async-done(((bf16[32,112,128]{2,1,0:T(8,128)(2,1)}), bf16[32,112,128]{2,1,0:T(8,128)(2,1)S(1)}, u32[]{:S(2)}, u32[]{:S(2)}) %all-to-all-start.1) | async-done | bytes 917536 | tf_op jit(solution)/shard_map/all_to_all | solution.py:530
  237.2 4.9 %shard_map.147 = (bf16[6144,128]{1,0:T(8,128)(2,1)}, f32[64,128]{1,0:T(8,128)}, f32[2,64]{1,0:T(2,128)}) custom-call(s32[6]{0:T(128)S(1)} %stack.23.at, bf16[32,112,128]{2,1,0:T(8,128)(2,1)S(1)} %all-to-all-done.1.back, bf16[6144,128]{1,0:T(8,128)(2,1)} %copy-done.7, bf16[32,64,128]{2,1,0:T(8,128)(2,1)S(1)} %bitcast.28), custom_call_target="tpu_custom_call" | custom-call | bytes 5242880 | tf_op jit(solution)/shard_map/pallas_call | solution.py:459
  242.1 0.9 shard_map.148
  (38 shorter events, 0.5 us)
Async XLA Ops:
  7.2 3.6 %copy-start.5 = (bf16[32,128,64]{1,2,0:T(8,128)(2,1)S(1)}, bf16[32,128,64]{1,2,0:T(8,128)(2,1)}, u32[]{:S(2)}) copy-start(bf16[32,128,64]{1,2,0:T(8,128)(2,1)} %param.13) | copy-start | bytes 1572868
  7.2 90.8 %all-gather.2.cloned.1.call-start = ((), (), s32[]{:S(2)}) async-start(), calls=%async_computation.4 | async-start | bytes 8650752 | tf_op jit(solution)/shard_map/all_gather | solution.py:558
  9.0 174.9 %reduce-scatter.3.cloned.1.call-start = ((), (), s32[]{:S(2)}) async-start(), calls=%async_computation.5 | async-start | bytes 2621440 | tf_op jit(solution)/shard_map/reduce_scatter | solution.py:516
  10.8 82.4 %copy-start.3 = (bf16[192,2048]{1,0:T(8,128)(2,1)S(1)}, bf16[192,2048]{1,0:T(8,128)(2,1)}, u32[]{:S(2)}) copy-start(bf16[192,2048]{1,0:T(8,128)(2,1)} %cot.5) | copy-start | bytes 2359300
  54.8 1.1 copy-start.7
  94.0 84.2 %copy-start = (bf16[2,192,2048]{2,1,0:T(8,128)(2,1)}, bf16[2,192,2048]{2,1,0:T(8,128)(2,1)S(1)}, u32[]{:S(2)}) copy-start(bf16[2,192,2048]{2,1,0:T(8,128)(2,1)S(1)} %get-tuple-element.43.pair.x0_ref) | copy-start | bytes 4718596
  94.0 13.8 %collective-permute-start = (bf16[2,192,2048]{2,1,0:T(8,128)(2,1)S(1)}, bf16[2,192,2048]{2,1,0:T(8,128)(2,1)}, u32[]{:S(2)}, u32[]{:S(2)}) collective-permute-start(bf16[2,192,2048]{2,1,0:T(8,128)(2,1)S(1)} %get-tuple-element.43.pair.x0_ref), channel_id=1, source_target_pairs={{0,8},{8,0},{16,24},{24,16},{32,40},{40,32},{48,56},{56,48},{64,72... | collective-permute-start | bytes 4718600 | tf_op jit(solution)/shard_map/ppermute | solution.py:542
  102.9 24.5 %copy-start.10 = (f32[2,2048]{1,0:T(2,128)S(1)}, f32[2,2048]{1,0:T(2,128)}, u32[]{:S(2)}) copy-start(f32[2,2048]{1,0:T(2,128)} %bias.3) | copy-start | bytes 49156
  102.9 5.4 %collective-permute-start.1 = (bf16[96,512]{1,0:T(8,128)(2,1)S(1)}, bf16[96,512]{1,0:T(8,128)(2,1)S(1)}, u32[]{:S(2)}, u32[]{:S(2)}) collective-permute-start(bf16[96,512]{1,0:T(8,128)(2,1)S(1)} %get-tuple-element.46), channel_id=1, source_target_pairs={{0,2},{1,3},{2,4},{3,5},{4,6},{5,7},{6,0},{7,1},{8,10},{9,11},{10,... | collective-permute-start | bytes 294920 | tf_op jit(solution)/shard_map/ppermute | solution.py:512
  104.3 7.2 %collective-permute-start.2 = (bf16[96,512]{1,0:T(8,128)(2,1)S(1)}, bf16[96,512]{1,0:T(8,128)(2,1)S(1)}, u32[]{:S(2)}, u32[]{:S(2)}) collective-permute-start(bf16[96,512]{1,0:T(8,128)(2,1)S(1)} %get-tuple-element.47), channel_id=1, source_target_pairs={{0,4},{1,5},{2,6},{3,7},{4,0},{5,1},{6,2},{7,3},{8,12},{9,13},{10,... | collective-permute-start | bytes 294920 | tf_op jit(solution)/shard_map/ppermute | solution.py:512
  106.7 4.8 %collective-permute-start.3 = (bf16[96,512]{1,0:T(8,128)(2,1)S(1)}, bf16[96,512]{1,0:T(8,128)(2,1)S(1)}, u32[]{:S(2)}, u32[]{:S(2)}) collective-permute-start(bf16[96,512]{1,0:T(8,128)(2,1)S(1)} %get-tuple-element.48), channel_id=1, source_target_pairs={{0,6},{1,7},{2,0},{3,1},{4,2},{5,3},{6,4},{7,5},{8,14},{9,15},{10,... | collective-permute-start | bytes 294920 | tf_op jit(solution)/shard_map/ppermute | solution.py:512
  111.6 7.6 %collective-permute-start.4 = (bf16[96,512]{1,0:T(8,128)(2,1)S(1)}, bf16[96,512]{1,0:T(8,128)(2,1)S(1)}, u32[]{:S(2)}, u32[]{:S(2)}) collective-permute-start(bf16[96,512]{1,0:T(8,128)(2,1)S(1)} %add_convert_fusion.3), channel_id=1, source_target_pairs={{0,1},{1,0},{2,3},{3,2},{4,5},{5,4},{6,7},{7,6},{8,9},{9,8},{10,11... | collective-permute-start | bytes 294920 | tf_op jit(solution)/shard_map/ppermute | solution.py:546
  119.2 3.5 %collective-permute-start.7 = (bf16[96,512]{1,0:T(8,128)(2,1)S(1)}, bf16[96,512]{1,0:T(8,128)(2,1)S(1)}, u32[]{:S(2)}, u32[]{:S(2)}) collective-permute-start(bf16[96,512]{1,0:T(8,128)(2,1)S(1)} %add_convert_fusion.2.refs_0_), channel_id=1, source_target_pairs={{0,6},{1,7},{2,0},{3,1},{4,2},{5,3},{6,4},{7,5},{8,14},{9,15},{10,... | collective-permute-start | bytes 294920 | tf_op jit(solution)/shard_map/ppermute | solution.py:512
  120.8 5.0 %collective-permute-start.6 = (bf16[96,512]{1,0:T(8,128)(2,1)S(1)}, bf16[96,512]{1,0:T(8,128)(2,1)S(1)}, u32[]{:S(2)}, u32[]{:S(2)}) collective-permute-start(bf16[96,512]{1,0:T(8,128)(2,1)S(1)} %add_convert_fusion.2.refs_0_), channel_id=1, source_target_pairs={{0,4},{1,5},{2,6},{3,7},{4,0},{5,1},{6,2},{7,3},{8,12},{9,13},{10,... | collective-permute-start | bytes 294920 | tf_op jit(solution)/shard_map/ppermute | solution.py:512
  121.5 5.3 %collective-permute-start.5 = (bf16[96,512]{1,0:T(8,128)(2,1)S(1)}, bf16[96,512]{1,0:T(8,128)(2,1)S(1)}, u32[]{:S(2)}, u32[]{:S(2)}) collective-permute-start(bf16[96,512]{1,0:T(8,128)(2,1)S(1)} %add_convert_fusion.2.refs_0_), channel_id=1, source_target_pairs={{0,2},{1,3},{2,4},{3,5},{4,6},{5,7},{6,0},{7,1},{8,10},{9,11},{10,... | collective-permute-start | bytes 294920 | tf_op jit(solution)/shard_map/ppermute | solution.py:512
  133.3 1.2 copy-start.6
  134.4 8.6 %collective-permute-start.9 = (bf16[2,192,2048]{2,1,0:T(8,128)(2,1)S(1)}, bf16[2,192,2048]{2,1,0:T(8,128)(2,1)S(1)}, u32[]{:S(2)}, u32[]{:S(2)}) collective-permute-start(bf16[2,192,2048]{2,1,0:T(8,128)(2,1)S(1)} %get-tuple-element.50.pair.x1_ref), channel_id=1, source_target_pairs={{0,8},{8,0},{16,24},{24,16},{32,40},{40,32},{48,56},{56,48},{64,72... | collective-permute-start | bytes 4718600 | tf_op jit(solution)/shard_map/ppermute | solution.py:542
  139.4 3.6 %collective-permute-start.8 = (bf16[384,512]{1,0:T(8,128)(2,1)S(1)}, bf16[384,512]{1,0:T(8,128)(2,1)S(1)}, u32[]{:S(2)}, u32[]{:S(2)}) collective-permute-start(bf16[384,512]{1,0:T(8,128)(2,1)S(1)} %shard_map.139.ranks), channel_id=1, source_target_pairs={{0,8},{8,0},{16,24},{24,16},{32,40},{40,32},{48,56},{56,48},{64,72... | collective-permute-start | bytes 1179656 | tf_op jit(solution)/shard_map/ppermute | solution.py:542
  146.0 1.4 copy-start.1
  147.4 1.1 copy-start.4
  148.5 70.9 %reduce-scatter.5.cloned.1.call-start = ((), (), s32[]{:S(2)}) async-start(), calls=%async_computation.6 | async-start | bytes 2621440 | tf_op jit(solution)/shard_map/reduce_scatter | solution.py:516
  148.6 7.6 %collective-permute-start.10 = (bf16[96,512]{1,0:T(8,128)(2,1)S(1)}, bf16[96,512]{1,0:T(8,128)(2,1)S(1)}, u32[]{:S(2)}, u32[]{:S(2)}) collective-permute-start(bf16[96,512]{1,0:T(8,128)(2,1)S(1)} %get-tuple-element.52), channel_id=1, source_target_pairs={{0,2},{1,3},{2,4},{3,5},{4,6},{5,7},{6,0},{7,1},{8,10},{9,11},{10,... | collective-permute-start | bytes 294920 | tf_op jit(solution)/shard_map/ppermute | solution.py:512
  148.7 7.5 %collective-permute-start.11 = (bf16[96,512]{1,0:T(8,128)(2,1)S(1)}, bf16[96,512]{1,0:T(8,128)(2,1)S(1)}, u32[]{:S(2)}, u32[]{:S(2)}) collective-permute-start(bf16[96,512]{1,0:T(8,128)(2,1)S(1)} %get-tuple-element.53), channel_id=1, source_target_pairs={{0,4},{1,5},{2,6},{3,7},{4,0},{5,1},{6,2},{7,3},{8,12},{9,13},{10,... | collective-permute-start | bytes 294920 | tf_op jit(solution)/shard_map/ppermute | solution.py:512
  150.1 6.2 %collective-permute-start.12 = (bf16[96,512]{1,0:T(8,128)(2,1)S(1)}, bf16[96,512]{1,0:T(8,128)(2,1)S(1)}, u32[]{:S(2)}, u32[]{:S(2)}) collective-permute-start(bf16[96,512]{1,0:T(8,128)(2,1)S(1)} %get-tuple-element.54), channel_id=1, source_target_pairs={{0,6},{1,7},{2,0},{3,1},{4,2},{5,3},{6,4},{7,5},{8,14},{9,15},{10,... | collective-permute-start | bytes 294920 | tf_op jit(solution)/shard_map/ppermute | solution.py:512
  156.4 7.6 %collective-permute-start.13 = (bf16[96,512]{1,0:T(8,128)(2,1)S(1)}, bf16[96,512]{1,0:T(8,128)(2,1)S(1)}, u32[]{:S(2)}, u32[]{:S(2)}) collective-permute-start(bf16[96,512]{1,0:T(8,128)(2,1)S(1)} %add_convert_fusion.1), channel_id=1, source_target_pairs={{0,1},{1,0},{2,3},{3,2},{4,5},{5,4},{6,7},{7,6},{8,9},{9,8},{10,11... | collective-permute-start | bytes 294920 | tf_op jit(solution)/shard_map/ppermute | solution.py:546
  164.0 5.6 %collective-permute-start.16 = (bf16[96,512]{1,0:T(8,128)(2,1)S(1)}, bf16[96,512]{1,0:T(8,128)(2,1)S(1)}, u32[]{:S(2)}, u32[]{:S(2)}) collective-permute-start(bf16[96,512]{1,0:T(8,128)(2,1)S(1)} %add_convert_fusion.refs_0_), channel_id=1, source_target_pairs={{0,6},{1,7},{2,0},{3,1},{4,2},{5,3},{6,4},{7,5},{8,14},{9,15},{10,... | collective-permute-start | bytes 294920 | tf_op jit(solution)/shard_map/ppermute | solution.py:512
  167.0 5.1 %collective-permute-start.15 = (bf16[96,512]{1,0:T(8,128)(2,1)S(1)}, bf16[96,512]{1,0:T(8,128)(2,1)S(1)}, u32[]{:S(2)}, u32[]{:S(2)}) collective-permute-start(bf16[96,512]{1,0:T(8,128)(2,1)S(1)} %add_convert_fusion.refs_0_), channel_id=1, source_target_pairs={{0,4},{1,5},{2,6},{3,7},{4,0},{5,1},{6,2},{7,3},{8,12},{9,13},{10,... | collective-permute-start | bytes 294920 | tf_op jit(solution)/shard_map/ppermute | solution.py:512
  167.0 6.1 %collective-permute-start.14 = (bf16[96,512]{1,0:T(8,128)(2,1)S(1)}, bf16[96,512]{1,0:T(8,128)(2,1)S(1)}, u32[]{:S(2)}, u32[]{:S(2)}) collective-permute-start(bf16[96,512]{1,0:T(8,128)(2,1)S(1)} %add_convert_fusion.refs_0_), channel_id=1, source_target_pairs={{0,2},{1,3},{2,4},{3,5},{4,6},{5,7},{6,0},{7,1},{8,10},{9,11},{10,... | collective-permute-start | bytes 294920 | tf_op jit(solution)/shard_map/ppermute | solution.py:512
  173.7 4.5 %collective-permute-start.17 = (bf16[384,512]{1,0:T(8,128)(2,1)S(1)}, bf16[384,512]{1,0:T(8,128)(2,1)S(1)}, u32[]{:S(2)}, u32[]{:S(2)}) collective-permute-start(bf16[384,512]{1,0:T(8,128)(2,1)S(1)} %shard_map.142.ranks), channel_id=1, source_target_pairs={{0,8},{8,0},{16,24},{24,16},{32,40},{40,32},{48,56},{56,48},{64,72... | collective-permute-start | bytes 1179656 | tf_op jit(solution)/shard_map/ppermute | solution.py:542
  182.5 1.3 copy-start.2
  183.9 1.0 copy-start.8
  185.6 11.1 %collective-permute-start.18 = (bf16[2,16,2048]{2,1,0:T(8,128)(2,1)S(1)}, bf16[2,16,2048]{2,1,0:T(8,128)(2,1)S(1)}, u32[]{:S(2)}, u32[]{:S(2)}) collective-permute-start(bf16[2,16,2048]{2,1,0:T(8,128)(2,1)S(1)} %get-tuple-element.61), channel_id=1, source_target_pairs={{0,16},{8,24},{16,32},{24,40},{32,48},{40,56},{48,0},{56,8},{64,80... | collective-permute-start | bytes 393224 | tf_op jit(solution)/shard_map/ppermute | solution.py:512
  186.8 11.8 %collective-permute-start.19 = (bf16[2,16,2048]{2,1,0:T(8,128)(2,1)S(1)}, bf16[2,16,2048]{2,1,0:T(8,128)(2,1)S(1)}, u32[]{:S(2)}, u32[]{:S(2)}) collective-permute-start(bf16[2,16,2048]{2,1,0:T(8,128)(2,1)S(1)} %get-tuple-element.62), channel_id=1, source_target_pairs={{0,32},{8,40},{16,48},{24,56},{32,0},{40,8},{48,16},{56,24},{64,96... | collective-permute-start | bytes 393224 | tf_op jit(solution)/shard_map/ppermute | solution.py:512
  188.0 10.5 %collective-permute-start.20 = (bf16[2,16,2048]{2,1,0:T(8,128)(2,1)S(1)}, bf16[2,16,2048]{2,1,0:T(8,128)(2,1)S(1)}, u32[]{:S(2)}, u32[]{:S(2)}) collective-permute-start(bf16[2,16,2048]{2,1,0:T(8,128)(2,1)S(1)} %get-tuple-element.63), channel_id=1, source_target_pairs={{0,48},{8,56},{16,0},{24,8},{32,16},{40,24},{48,32},{56,40},{64,11... | collective-permute-start | bytes 393224 | tf_op jit(solution)/shard_map/ppermute | solution.py:512
  198.6 38.6 %all-to-all-start.1 = ((bf16[32,112,128]{2,1,0:T(8,128)(2,1)}), bf16[32,112,128]{2,1,0:T(8,128)(2,1)S(1)}, u32[]{:S(2)}, u32[]{:S(2)}) async-start(bf16[32,112,128]{2,1,0:T(8,128)(2,1)} %get-tuple-element.66), calls=%async_computation.3 | async-start | bytes 1835008 | tf_op jit(solution)/shard_map/all_to_all | solution.py:530
  219.4 1.0 copy-start.9
  221.0 21.1 %collective-permute-start.21 = (bf16[2,16,2048]{2,1,0:T(8,128)(2,1)S(1)}, bf16[2,16,2048]{2,1,0:T(8,128)(2,1)S(1)}, u32[]{:S(2)}, u32[]{:S(2)}) collective-permute-start(bf16[2,16,2048]{2,1,0:T(8,128)(2,1)S(1)} %get-tuple-element.71), channel_id=1, source_target_pairs={{0,16},{8,24},{16,32},{24,40},{32,48},{40,56},{48,0},{56,8},{64,80... | collective-permute-start | bytes 393224 | tf_op jit(solution)/shard_map/ppermute | solution.py:512
  222.1 20.0 %collective-permute-start.22 = (bf16[2,16,2048]{2,1,0:T(8,128)(2,1)S(1)}, bf16[2,16,2048]{2,1,0:T(8,128)(2,1)S(1)}, u32[]{:S(2)}, u32[]{:S(2)}) collective-permute-start(bf16[2,16,2048]{2,1,0:T(8,128)(2,1)S(1)} %get-tuple-element.72), channel_id=1, source_target_pairs={{0,32},{8,40},{16,48},{24,56},{32,0},{40,8},{48,16},{56,24},{64,96... | collective-permute-start | bytes 393224 | tf_op jit(solution)/shard_map/ppermute | solution.py:512
  225.7 16.4 %collective-permute-start.23 = (bf16[2,16,2048]{2,1,0:T(8,128)(2,1)S(1)}, bf16[2,16,2048]{2,1,0:T(8,128)(2,1)S(1)}, u32[]{:S(2)}, u32[]{:S(2)}) collective-permute-start(bf16[2,16,2048]{2,1,0:T(8,128)(2,1)S(1)} %get-tuple-element.73), channel_id=1, source_target_pairs={{0,48},{8,56},{16,0},{24,8},{32,16},{40,24},{48,32},{56,40},{64,11... | collective-permute-start | bytes 393224 | tf_op jit(solution)/shard_map/ppermute | solution.py:512
Sparse Core Ops, SparseCore 0:
  10.4 87.5 all-gather.1
  148.7 27.7 reduce-scatter.2
  184.0 35.3 reduce-scatter.4

commit v4 on v3

--- a/solution.py
+++ b/solution.py
@@ -21,7 +21,7 @@
 SHARE = RANK // FIELD_TABLES
 TOKENS = SAMPLES * FIELD_TABLES
 BACK_ROWS = HALF + 16
-FEATURE_BLOCK = 512
+FEATURE_BLOCK = 1024
 POOL_CHUNK = 1536
 POOL_UNROLL = 64
 QUARTER = 2 * SAMPLES // Y_SIZE
@@ -428,19 +428,17 @@
     both = jnp.concatenate(
         [jnp.concatenate([factor, none], axis=1), jnp.concatenate([none, factor], axis=1)], axis=0
     )
-    total = jnp.zeros((PROJ, EMB), F32)
-    bias = jnp.zeros((1, EMB), F32)
-    for block in range(back.shape[0]):
-        grads = back[block, :HALF, :]
-        start = block * SAMPLES
-        out = dot(grads, both, 1, 0).astype(BF16)
-        grad_pooled[start : start + HALF, :] = out[:, :EMB]
-        grad_pooled[start + HALF : start + SAMPLES, :] = out[:, EMB:]
-        upper = dot(grads, pooled[start : start + HALF, :], 0, 0)
-        lower = dot(grads, pooled[start + HALF : start + SAMPLES, :], 0, 0)
-        total += upper[:PROJ] + lower[PROJ:]
-        bias += back[block, HALF:, :].astype(F32)[:1]
-
+    blocks = back.shape[0]
+    grads = back[:, :HALF, :].reshape(blocks * HALF, EMB)
+    out = dot(grads, both, 1, 0).astype(BF16)
+    halves = [out[:, :EMB].reshape(blocks, HALF, EMB), out[:, EMB:].reshape(blocks, HALF, EMB)]
+    grad_pooled[...] = jnp.concatenate(halves, axis=1).reshape(blocks * SAMPLES, EMB)
+    bags = pooled[...].reshape(blocks, SAMPLES, EMB)
+    upper = bags[:, :HALF].reshape(blocks * HALF, EMB)
+    lower = bags[:, HALF:].reshape(blocks * HALF, EMB)
+    products = dot(grads, jnp.concatenate([upper, lower], axis=1), 0, 0)
+    total = products[:PROJ, :EMB] + products[PROJ:, EMB:]
+    bias = jnp.sum(back[:, HALF:, :].astype(F32), axis=0)[:1]
     bias = jnp.concatenate([bias[:, :PROJ], bias[:, PROJ:]], axis=0)
 
     @pl.when(step == 0)

time: 250 us -> 247 us (0.988)
  Pallas kernels: 77.3 us -> 74 us
  transfers between devices with their start and end apart: 28 -> 28, of which waited for: 18 -> 18; matrix products, arithmetic and copies ran while one was open for 0% -> 0% of each run, Pallas kernels for 27% -> 26%
where the time goes in v4:
time: 247 us
  Pallas kernels  74 us (30%)
  waiting for transfers between devices  60.9 us (25%)
  starting transfers between devices  48.9 us (20%)
  blocking collectives  37.2 us (15%)
  between operations  14.7 us (6%)
  local copies, waits for them, and re-layouts  8.35 us (3%)
  other arithmetic  2.86 us (1%)
    pallas_call x1, Pallas kernels, pool(): pl.pallas_call(pool_kernel, grid_spec=pltpu.PrefetchScalarGridSpec(num_sc...  44 us
    all_to_all x1, blocking collectives, to_all(): lax.all_to_all(blocks, 'batch', split_axis=0, concat_axis=0, tiled=True)  37.2 us
    ppermute x18, starting transfers between devices, exchange(): lax.ppermute(parts[s], axis, moves[s])  24.3 us
    ppermute x18, waiting for transfers between devices, exchange(): lax.ppermute(parts[s], axis, moves[s])  20.7 us
    reduce_scatter x2, waiting for transfers between devices, scatter_sum(): lax.psum_scatter(blocks, 'batch', scatter_dimension=0, tiled=True, axis_i...  13.1 us
    all_to_all x1, waiting for transfers between devices, to_all(): lax.all_to_all(blocks, 'batch', split_axis=0, concat_axis=0, tiled=True)  11.3 us
    ppermute x4, starting transfers between devices, core_swap(): return lax.ppermute(value, 'batch', CORE_SWAP)  8.46 us
    ppermute x2, starting transfers between devices, both_halves(): return low_sum([partial, lax.ppermute(partial, 'field', HALF_SWAP)])  8.28 us
  transfers between devices with their start and end apart: 28, of which 18 were waited for; matrix products, arithmetic and copies ran while one was open for 0% of the time, Pallas kernels for 26%

profile of v4, /device:TPU:1, one launch (start us, length us, event | category | flops | bytes accessed | tf_op | source)
XLA Modules:
  0.0 246.9 jit_solution(13706399092279209500)
XLA Ops:
  7.2 1.7 pad_maximum_fusion
  9.7 0.1 stack.23.at
  9.8 1.0 fusion.ids
  10.8 44.0 %shard_map.136 = (bf16[6144,128]{1,0:T(8,128)(2,1)S(1)}, bf16[32,96,128]{2,1,0:T(8,128)(2,1)S(1)}) custom-call(s32[6]{0:T(128)S(1)} %stack.23.at, s32[49152]{0:T(1024)S(1)} %fusion.ids, bf16[8192,128]{1,0:T(8,128)(2,1)} %bitcast.37, bf16[32,64,128]{2,1,0:T(8,128)(2,1)S(1)} %bitcast.27), custom_call_target="tpu_custom_call" | custom-call | bytes 104857600 | tf_op jit(solution)/shard_map/pallas_call | solution.py:93
  54.8 1.1 copy-done.7
  55.9 37.2 %all_to_all.10.recv = bf16[32,96,128]{2,1,0:T(8,128)(2,1)S(1)} all-to-all(bf16[32,96,128]{2,1,0:T(8,128)(2,1)S(1)} %get-tuple-element.42), channel_id=1, replica_groups=mesh['batch'=32,'field'=8] {'batch'}, dimensions={0} | all-to-all | bytes 1572864 | tf_op jit(solution)/shard_map/all_to_all | solution.py:528
  93.1 0.7 shard_map.137
  93.9 0.1 collective-permute-start
  94.0 3.9 %all-gather.2.cloned.1.call-done = bf16[128,16,2048]{2,1,0:T(8,128)(2,1)} async-done(((bf16[4,16,2048]{2,1,0:T(8,128)(2,1)}), bf16[128,16,2048]{2,1,0:T(8,128)(2,1)}) %all-gather.2.cloned.1.call-update) | async-done | bytes 8388624 | tf_op jit(solution)/shard_map/all_gather | solution.py:556
  97.9 4.0 %shard_map.138 = (bf16[96,512]{1,0:T(8,128)(2,1)S(1)}, bf16[96,512]{1,0:T(8,128)(2,1)S(1)}, bf16[96,512]{1,0:T(8,128)(2,1)S(1)}, bf16[96,512]{1,0:T(8,128)(2,1)S(1)}) custom-call(s32[6]{0:T(128)S(1)} %stack.23.at, bf16[2,192,2048]{2,1,0:T(8,128)(2,1)S(1)} %get-tuple-element.43.pair.x0_ref, bf16[32,4,16,2048]{3,2,1,0:T(8,128)(2,1)} %bitcast.31, ...), custom_call_target="tpu_custom_call" | custom-call | bytes 8388608 | tf_op jit(solution)/shard_map/pallas_call | solution.py:232
  101.9 1.3 collective-permute-start.1
  103.2 2.5 %collective-permute-start.2 = (bf16[96,512]{1,0:T(8,128)(2,1)S(1)}, bf16[96,512]{1,0:T(8,128)(2,1)S(1)}, u32[]{:S(2)}, u32[]{:S(2)}) collective-permute-start(bf16[96,512]{1,0:T(8,128)(2,1)S(1)} %get-tuple-element.47), channel_id=1, source_target_pairs={{0,4},{1,5},{2,6},{3,7},{4,0},{5,1},{6,2},{7,3},{8,12},{9,13},{10,... | collective-permute-start | bytes 294920 | tf_op jit(solution)/shard_map/ppermute | solution.py:510
  105.8 1.1 collective-permute-start.3
  106.9 0.5 collective-permute-done.1
  107.4 3.2 %collective-permute-done.2 = bf16[96,512]{1,0:T(8,128)(2,1)S(1)} collective-permute-done((bf16[96,512]{1,0:T(8,128)(2,1)S(1)}, bf16[96,512]{1,0:T(8,128)(2,1)S(1)}, u32[]{:S(2)}, u32[]{:S(2)}) %collective-permute-start.2) | collective-permute-done | bytes 98336 | tf_op jit(solution)/shard_map/ppermute | solution.py:510
  110.6 4.3 %collective-permute-start.4 = (bf16[96,512]{1,0:T(8,128)(2,1)S(1)}, bf16[96,512]{1,0:T(8,128)(2,1)S(1)}, u32[]{:S(2)}, u32[]{:S(2)}) collective-permute-start(bf16[96,512]{1,0:T(8,128)(2,1)S(1)} %add_convert_fusion.3), channel_id=1, source_target_pairs={{0,1},{1,0},{2,3},{3,2},{4,5},{5,4},{6,7},{7,6},{8,9},{9,8},{10,11... | collective-permute-start | bytes 294920 | tf_op jit(solution)/shard_map/ppermute | solution.py:544
  114.9 3.3 %collective-permute-done.4 = bf16[96,512]{1,0:T(8,128)(2,1)S(1)} collective-permute-done((bf16[96,512]{1,0:T(8,128)(2,1)S(1)}, bf16[96,512]{1,0:T(8,128)(2,1)S(1)}, u32[]{:S(2)}, u32[]{:S(2)}) %collective-permute-start.4) | collective-permute-done | bytes 98336 | tf_op jit(solution)/shard_map/ppermute | solution.py:544
  118.2 1.2 collective-permute-start.7
  119.5 1.0 collective-permute-start.6
  120.4 0.8 collective-permute-start.5
  121.2 0.6 collective-permute-done.7.refs_3_
  121.8 2.7 %collective-permute-done.6.refs_2_ = bf16[96,512]{1,0:T(8,128)(2,1)S(1)} collective-permute-done((bf16[96,512]{1,0:T(8,128)(2,1)S(1)}, bf16[96,512]{1,0:T(8,128)(2,1)S(1)}, u32[]{:S(2)}, u32[]{:S(2)}) %collective-permute-start.6) | collective-permute-done | bytes 98336 | tf_op jit(solution)/shard_map/ppermute | solution.py:510
  124.5 1.0 collective-permute-done.5.refs_1_
  125.5 0.6 shard_map.139.ranks
  126.1 5.3 %shard_map.140 = (bf16[2,192,2048]{2,1,0:T(8,128)(2,1)S(1)}, f32[192,2048]{1,0:T(8,128)S(1)}, f32[1,2048]{1,0:T(1,128)S(1)}, bf16[96,512]{1,0:T(8,128)(2,1)S(1)}...) custom-call(s32[6]{0:T(128)S(1)} %stack.23.at, ...), custom_call_target="tpu_custom_call" | custom-call | bytes 10485760 | tf_op jit(solution)/shard_map/pallas_call | solution.py:278
  131.4 1.2 copy-done.6
  132.6 5.3 %collective-permute-start.9 = (bf16[2,192,2048]{2,1,0:T(8,128)(2,1)S(1)}, bf16[2,192,2048]{2,1,0:T(8,128)(2,1)S(1)}, u32[]{:S(2)}, u32[]{:S(2)}) collective-permute-start(bf16[2,192,2048]{2,1,0:T(8,128)(2,1)S(1)} %get-tuple-element.50.pair.x1_ref), channel_id=1, source_target_pairs={{0,8},{8,0},{16,24},{24,16},{32,40},{40,32},{48,56},{56,48},{64,72... | collective-permute-start | bytes 4718600 | tf_op jit(solution)/shard_map/ppermute | solution.py:540
  137.9 3.6 %collective-permute-done.8.other_ranks = bf16[384,512]{1,0:T(8,128)(2,1)S(1)} collective-permute-done((bf16[384,512]{1,0:T(8,128)(2,1)S(1)}, bf16[384,512]{1,0:T(8,128)(2,1)S(1)}, u32[]{:S(2)}, u32[]{:S(2)}) %collective-permute-start.8) | collective-permute-done | bytes 393248 | tf_op jit(solution)/shard_map/ppermute | solution.py:540
  141.5 2.6 %shard_map.141 = bf16[4,4,2,16,2048]{4,3,2,1,0:T(8,128)(2,1)S(1)} custom-call(s32[6]{0:T(128)S(1)} %stack.23.at, bf16[384,512]{1,0:T(8,128)(2,1)S(1)} %shard_map.139.ranks, bf16[384,512]{1,0:T(8,128)(2,1)S(1)} %collective-permute-done.8.other_ranks, bf16[2,192,2048]{2,1,0:T(8,128)(2,1)S(1)} %get-tuple-element.50.pair.x1_ref, ...), custom_call_target="tpu_custom_call" | custom-call | bytes 6291456 | tf_op jit(solution)/shard_map/pallas_call | solution.py:367
  144.1 1.4 copy-done.1
  145.5 1.1 copy-done.4
  146.8 0.3 collective-permute-start.10
  147.0 1.4 collective-permute-start.11
  148.5 1.3 collective-permute-start.12
  149.8 4.8 %collective-permute-done.10 = bf16[96,512]{1,0:T(8,128)(2,1)S(1)} collective-permute-done((bf16[96,512]{1,0:T(8,128)(2,1)S(1)}, bf16[96,512]{1,0:T(8,128)(2,1)S(1)}, u32[]{:S(2)}, u32[]{:S(2)}) %collective-permute-start.10) | collective-permute-done | bytes 98336 | tf_op jit(solution)/shard_map/ppermute | solution.py:510
  154.6 0.1 collective-permute-done.12
  154.7 4.0 %collective-permute-start.13 = (bf16[96,512]{1,0:T(8,128)(2,1)S(1)}, bf16[96,512]{1,0:T(8,128)(2,1)S(1)}, u32[]{:S(2)}, u32[]{:S(2)}) collective-permute-start(bf16[96,512]{1,0:T(8,128)(2,1)S(1)} %add_convert_fusion.1), channel_id=1, source_target_pairs={{0,1},{1,0},{2,3},{3,2},{4,5},{5,4},{6,7},{7,6},{8,9},{9,8},{10,11... | collective-permute-start | bytes 294920 | tf_op jit(solution)/shard_map/ppermute | solution.py:544
  158.8 3.5 %collective-permute-done.13 = bf16[96,512]{1,0:T(8,128)(2,1)S(1)} collective-permute-done((bf16[96,512]{1,0:T(8,128)(2,1)S(1)}, bf16[96,512]{1,0:T(8,128)(2,1)S(1)}, u32[]{:S(2)}, u32[]{:S(2)}) %collective-permute-start.13) | collective-permute-done | bytes 98336 | tf_op jit(solution)/shard_map/ppermute | solution.py:544
  162.3 3.1 %collective-permute-start.16 = (bf16[96,512]{1,0:T(8,128)(2,1)S(1)}, bf16[96,512]{1,0:T(8,128)(2,1)S(1)}, u32[]{:S(2)}, u32[]{:S(2)}) collective-permute-start(bf16[96,512]{1,0:T(8,128)(2,1)S(1)} %add_convert_fusion.refs_0_), channel_id=1, source_target_pairs={{0,6},{1,7},{2,0},{3,1},{4,2},{5,3},{6,4},{7,5},{8,14},{9,15},{10,... | collective-permute-start | bytes 294920 | tf_op jit(solution)/shard_map/ppermute | solution.py:510
  165.4 0.7 collective-permute-start.14
  166.1 1.9 collective-permute-done.16.refs_3_
  168.0 2.5 collective-permute-done.15.refs_2_
  170.5 1.1 collective-permute-done.14.refs_1_
  171.6 0.6 shard_map.142.ranks
  172.1 3.1 %collective-permute-start.17 = (bf16[384,512]{1,0:T(8,128)(2,1)S(1)}, bf16[384,512]{1,0:T(8,128)(2,1)S(1)}, u32[]{:S(2)}, u32[]{:S(2)}) collective-permute-start(bf16[384,512]{1,0:T(8,128)(2,1)S(1)} %shard_map.142.ranks), channel_id=1, source_target_pairs={{0,8},{8,0},{16,24},{24,16},{32,40},{40,32},{48,56},{56,48},{64,72... | collective-permute-start | bytes 1179656 | tf_op jit(solution)/shard_map/ppermute | solution.py:540
  175.2 1.3 collective-permute-done.17.other_ranks
  176.6 3.6 %shard_map.143 = bf16[4,4,2,16,2048]{4,3,2,1,0:T(8,128)(2,1)S(1)} custom-call(s32[6]{0:T(128)S(1)} %stack.23.at, bf16[384,512]{1,0:T(8,128)(2,1)S(1)} %shard_map.142.ranks, bf16[384,512]{1,0:T(8,128)(2,1)S(1)} %collective-permute-done.17.other_ranks, bf16[2,192,2048]{2,1,0:T(8,128)(2,1)S(1)} %get-tuple-element.43.pair.x0_ref, ...), custom_call_target="tpu_custom_call" | custom-call | bytes 6291456 | tf_op jit(solution)/shard_map/pallas_call | solution.py:367
  180.1 1.3 copy-done.2
  181.5 1.0 copy-done.8
  182.5 0.6 shard_map.145
  183.1 2.6 %collective-permute-start.18 = (bf16[2,16,2048]{2,1,0:T(8,128)(2,1)S(1)}, bf16[2,16,2048]{2,1,0:T(8,128)(2,1)S(1)}, u32[]{:S(2)}, u32[]{:S(2)}) collective-permute-start(bf16[2,16,2048]{2,1,0:T(8,128)(2,1)S(1)} %get-tuple-element.61), channel_id=1, source_target_pairs={{0,16},{8,24},{16,32},{24,40},{32,48},{40,56},{48,0},{56,8},{64,80... | collective-permute-start | bytes 393224 | tf_op jit(solution)/shard_map/ppermute | solution.py:510
  185.7 2.2 collective-permute-start.20
  187.9 5.9 %shard_map.144 = (bf16[192,2048]{1,0:T(8,128)(2,1)}, bf16[32,112,128]{2,1,0:T(8,128)(2,1)}) custom-call(s32[6]{0:T(128)S(1)} %stack.23.at, bf16[384,512]{1,0:T(8,128)(2,1)S(1)} %shard_map.142.ranks, bf16[2,192,2048]{2,1,0:T(8,128)(2,1)} %copy-done, bf16[2,192,2048]{2,1,0:T(8,128)(2,1)} %copy-done.4, bf16[192,2048]{1,0:T(8,128)(2,1)} %cot.5, ...), custom_call_target="tpu_custom_call" | custom-call | bytes 1048576 | tf_op jit(solution)/shard_map/pallas_call | solution.py:324
  193.8 2.3 collective-permute-done.19.refs_2_
  196.2 7.8 %all-to-all-start.1 = ((bf16[32,112,128]{2,1,0:T(8,128)(2,1)}), bf16[32,112,128]{2,1,0:T(8,128)(2,1)S(1)}, u32[]{:S(2)}, u32[]{:S(2)}) async-start(bf16[32,112,128]{2,1,0:T(8,128)(2,1)} %get-tuple-element.66), calls=%async_computation.3 | async-start | bytes 1835008 | tf_op jit(solution)/shard_map/all_to_all | solution.py:528
  203.9 13.1 %reduce-scatter.5.cloned.1.call-done = bf16[1,4,2,16,2048]{4,3,2,1,0:T(8,128)(2,1)} async-done(((bf16[4,4,2,16,2048]{4,3,2,1,0:T(8,128)(2,1)}), bf16[1,4,2,16,2048]{4,3,2,1,0:T(8,128)(2,1)}) %reduce-scatter.5.cloned.1.call-update) | async-done | bytes 524304 | tf_op jit(solution)/shard_map/reduce_scatter | solution.py:514
  217.0 1.0 copy-done.9
  218.1 0.6 shard_map.146
  218.7 1.0 collective-permute-start.21
  219.7 3.7 %collective-permute-start.22 = (bf16[2,16,2048]{2,1,0:T(8,128)(2,1)S(1)}, bf16[2,16,2048]{2,1,0:T(8,128)(2,1)S(1)}, u32[]{:S(2)}, u32[]{:S(2)}) collective-permute-start(bf16[2,16,2048]{2,1,0:T(8,128)(2,1)S(1)} %get-tuple-element.72), channel_id=1, source_target_pairs={{0,32},{8,40},{16,48},{24,56},{32,0},{40,8},{48,16},{56,24},{64,96... | collective-permute-start | bytes 393224 | tf_op jit(solution)/shard_map/ppermute | solution.py:510
  223.4 0.1 collective-permute-start.23
  223.5 11.3 %all-to-all-done.1.back = bf16[32,112,128]{2,1,0:T(8,128)(2,1)S(1)} async-done(((bf16[32,112,128]{2,1,0:T(8,128)(2,1)}), bf16[32,112,128]{2,1,0:T(8,128)(2,1)S(1)}, u32[]{:S(2)}, u32[]{:S(2)}) %all-to-all-start.1) | async-done | bytes 917536 | tf_op jit(solution)/shard_map/all_to_all | solution.py:528
  234.8 4.7 %shard_map.147 = (bf16[6144,128]{1,0:T(8,128)(2,1)}, f32[64,128]{1,0:T(8,128)}, f32[2,64]{1,0:T(2,128)}) custom-call(s32[6]{0:T(128)S(1)} %stack.23.at, bf16[32,112,128]{2,1,0:T(8,128)(2,1)S(1)} %all-to-all-done.1.back, bf16[6144,128]{1,0:T(8,128)(2,1)} %copy-done.7, bf16[32,64,128]{2,1,0:T(8,128)(2,1)S(1)} %bitcast.28), custom_call_target="tpu_custom_call" | custom-call | bytes 5242880 | tf_op jit(solution)/shard_map/pallas_call | solution.py:457
  239.5 0.9 shard_map.148
  (38 shorter events, 0.4 us)
Async XLA Ops:
  7.2 3.6 %copy-start.5 = (bf16[32,128,64]{1,2,0:T(8,128)(2,1)S(1)}, bf16[32,128,64]{1,2,0:T(8,128)(2,1)}, u32[]{:S(2)}) copy-start(bf16[32,128,64]{1,2,0:T(8,128)(2,1)} %param.13) | copy-start | bytes 1572868
  7.2 90.7 %all-gather.2.cloned.1.call-start = ((), (), s32[]{:S(2)}) async-start(), calls=%async_computation.4 | async-start | bytes 8650752 | tf_op jit(solution)/shard_map/all_gather | solution.py:556
  9.0 172.5 %reduce-scatter.3.cloned.1.call-start = ((), (), s32[]{:S(2)}) async-start(), calls=%async_computation.5 | async-start | bytes 2621440 | tf_op jit(solution)/shard_map/reduce_scatter | solution.py:514
  10.8 82.4 %copy-start.3 = (bf16[192,2048]{1,0:T(8,128)(2,1)S(1)}, bf16[192,2048]{1,0:T(8,128)(2,1)}, u32[]{:S(2)}) copy-start(bf16[192,2048]{1,0:T(8,128)(2,1)} %cot.5) | copy-start | bytes 2359300
  54.8 1.1 copy-start.7
  93.9 82.7 %copy-start = (bf16[2,192,2048]{2,1,0:T(8,128)(2,1)}, bf16[2,192,2048]{2,1,0:T(8,128)(2,1)S(1)}, u32[]{:S(2)}) copy-start(bf16[2,192,2048]{2,1,0:T(8,128)(2,1)S(1)} %get-tuple-element.43.pair.x0_ref) | copy-start | bytes 4718596
  93.9 13.0 %collective-permute-start = (bf16[2,192,2048]{2,1,0:T(8,128)(2,1)S(1)}, bf16[2,192,2048]{2,1,0:T(8,128)(2,1)}, u32[]{:S(2)}, u32[]{:S(2)}) collective-permute-start(bf16[2,192,2048]{2,1,0:T(8,128)(2,1)S(1)} %get-tuple-element.43.pair.x0_ref), channel_id=1, source_target_pairs={{0,8},{8,0},{16,24},{24,16},{32,40},{40,32},{48,56},{56,48},{64,72... | collective-permute-start | bytes 4718600 | tf_op jit(solution)/shard_map/ppermute | solution.py:540
  101.9 24.2 %copy-start.10 = (f32[2,2048]{1,0:T(2,128)S(1)}, f32[2,2048]{1,0:T(2,128)}, u32[]{:S(2)}) copy-start(f32[2,2048]{1,0:T(2,128)} %bias.3) | copy-start | bytes 49156
  101.9 5.5 %collective-permute-start.1 = (bf16[96,512]{1,0:T(8,128)(2,1)S(1)}, bf16[96,512]{1,0:T(8,128)(2,1)S(1)}, u32[]{:S(2)}, u32[]{:S(2)}) collective-permute-start(bf16[96,512]{1,0:T(8,128)(2,1)S(1)} %get-tuple-element.46), channel_id=1, source_target_pairs={{0,2},{1,3},{2,4},{3,5},{4,6},{5,7},{6,0},{7,1},{8,10},{9,11},{10,... | collective-permute-start | bytes 294920 | tf_op jit(solution)/shard_map/ppermute | solution.py:510
  103.2 7.3 %collective-permute-start.2 = (bf16[96,512]{1,0:T(8,128)(2,1)S(1)}, bf16[96,512]{1,0:T(8,128)(2,1)S(1)}, u32[]{:S(2)}, u32[]{:S(2)}) collective-permute-start(bf16[96,512]{1,0:T(8,128)(2,1)S(1)} %get-tuple-element.47), channel_id=1, source_target_pairs={{0,4},{1,5},{2,6},{3,7},{4,0},{5,1},{6,2},{7,3},{8,12},{9,13},{10,... | collective-permute-start | bytes 294920 | tf_op jit(solution)/shard_map/ppermute | solution.py:510
  105.8 4.8 %collective-permute-start.3 = (bf16[96,512]{1,0:T(8,128)(2,1)S(1)}, bf16[96,512]{1,0:T(8,128)(2,1)S(1)}, u32[]{:S(2)}, u32[]{:S(2)}) collective-permute-start(bf16[96,512]{1,0:T(8,128)(2,1)S(1)} %get-tuple-element.48), channel_id=1, source_target_pairs={{0,6},{1,7},{2,0},{3,1},{4,2},{5,3},{6,4},{7,5},{8,14},{9,15},{10,... | collective-permute-start | bytes 294920 | tf_op jit(solution)/shard_map/ppermute | solution.py:510
  110.6 7.6 %collective-permute-start.4 = (bf16[96,512]{1,0:T(8,128)(2,1)S(1)}, bf16[96,512]{1,0:T(8,128)(2,1)S(1)}, u32[]{:S(2)}, u32[]{:S(2)}) collective-permute-start(bf16[96,512]{1,0:T(8,128)(2,1)S(1)} %add_convert_fusion.3), channel_id=1, source_target_pairs={{0,1},{1,0},{2,3},{3,2},{4,5},{5,4},{6,7},{7,6},{8,9},{9,8},{10,11... | collective-permute-start | bytes 294920 | tf_op jit(solution)/shard_map/ppermute | solution.py:544
  118.2 3.5 %collective-permute-start.7 = (bf16[96,512]{1,0:T(8,128)(2,1)S(1)}, bf16[96,512]{1,0:T(8,128)(2,1)S(1)}, u32[]{:S(2)}, u32[]{:S(2)}) collective-permute-start(bf16[96,512]{1,0:T(8,128)(2,1)S(1)} %add_convert_fusion.2.refs_0_), channel_id=1, source_target_pairs={{0,6},{1,7},{2,0},{3,1},{4,2},{5,3},{6,4},{7,5},{8,14},{9,15},{10,... | collective-permute-start | bytes 294920 | tf_op jit(solution)/shard_map/ppermute | solution.py:510
  119.5 5.0 %collective-permute-start.6 = (bf16[96,512]{1,0:T(8,128)(2,1)S(1)}, bf16[96,512]{1,0:T(8,128)(2,1)S(1)}, u32[]{:S(2)}, u32[]{:S(2)}) collective-permute-start(bf16[96,512]{1,0:T(8,128)(2,1)S(1)} %add_convert_fusion.2.refs_0_), channel_id=1, source_target_pairs={{0,4},{1,5},{2,6},{3,7},{4,0},{5,1},{6,2},{7,3},{8,12},{9,13},{10,... | collective-permute-start | bytes 294920 | tf_op jit(solution)/shard_map/ppermute | solution.py:510
  120.4 5.0 %collective-permute-start.5 = (bf16[96,512]{1,0:T(8,128)(2,1)S(1)}, bf16[96,512]{1,0:T(8,128)(2,1)S(1)}, u32[]{:S(2)}, u32[]{:S(2)}) collective-permute-start(bf16[96,512]{1,0:T(8,128)(2,1)S(1)} %add_convert_fusion.2.refs_0_), channel_id=1, source_target_pairs={{0,2},{1,3},{2,4},{3,5},{4,6},{5,7},{6,0},{7,1},{8,10},{9,11},{10,... | collective-permute-start | bytes 294920 | tf_op jit(solution)/shard_map/ppermute | solution.py:510
  131.4 1.2 copy-start.6
  132.6 8.9 %collective-permute-start.9 = (bf16[2,192,2048]{2,1,0:T(8,128)(2,1)S(1)}, bf16[2,192,2048]{2,1,0:T(8,128)(2,1)S(1)}, u32[]{:S(2)}, u32[]{:S(2)}) collective-permute-start(bf16[2,192,2048]{2,1,0:T(8,128)(2,1)S(1)} %get-tuple-element.50.pair.x1_ref), channel_id=1, source_target_pairs={{0,8},{8,0},{16,24},{24,16},{32,40},{40,32},{48,56},{56,48},{64,72... | collective-permute-start | bytes 4718600 | tf_op jit(solution)/shard_map/ppermute | solution.py:540
  137.9 3.6 %collective-permute-start.8 = (bf16[384,512]{1,0:T(8,128)(2,1)S(1)}, bf16[384,512]{1,0:T(8,128)(2,1)S(1)}, u32[]{:S(2)}, u32[]{:S(2)}) collective-permute-start(bf16[384,512]{1,0:T(8,128)(2,1)S(1)} %shard_map.139.ranks), channel_id=1, source_target_pairs={{0,8},{8,0},{16,24},{24,16},{32,40},{40,32},{48,56},{56,48},{64,72... | collective-permute-start | bytes 1179656 | tf_op jit(solution)/shard_map/ppermute | solution.py:540
  144.1 1.4 copy-start.1
  145.5 1.1 copy-start.4
  146.7 70.3 %reduce-scatter.5.cloned.1.call-start = ((), (), s32[]{:S(2)}) async-start(), calls=%async_computation.6 | async-start | bytes 2621440 | tf_op jit(solution)/shard_map/reduce_scatter | solution.py:514
  146.8 7.8 %collective-permute-start.10 = (bf16[96,512]{1,0:T(8,128)(2,1)S(1)}, bf16[96,512]{1,0:T(8,128)(2,1)S(1)}, u32[]{:S(2)}, u32[]{:S(2)}) collective-permute-start(bf16[96,512]{1,0:T(8,128)(2,1)S(1)} %get-tuple-element.52), channel_id=1, source_target_pairs={{0,2},{1,3},{2,4},{3,5},{4,6},{5,7},{6,0},{7,1},{8,10},{9,11},{10,... | collective-permute-start | bytes 294920 | tf_op jit(solution)/shard_map/ppermute | solution.py:510
  147.0 7.6 %collective-permute-start.11 = (bf16[96,512]{1,0:T(8,128)(2,1)S(1)}, bf16[96,512]{1,0:T(8,128)(2,1)S(1)}, u32[]{:S(2)}, u32[]{:S(2)}) collective-permute-start(bf16[96,512]{1,0:T(8,128)(2,1)S(1)} %get-tuple-element.53), channel_id=1, source_target_pairs={{0,4},{1,5},{2,6},{3,7},{4,0},{5,1},{6,2},{7,3},{8,12},{9,13},{10,... | collective-permute-start | bytes 294920 | tf_op jit(solution)/shard_map/ppermute | solution.py:510
  148.5 6.2 %collective-permute-start.12 = (bf16[96,512]{1,0:T(8,128)(2,1)S(1)}, bf16[96,512]{1,0:T(8,128)(2,1)S(1)}, u32[]{:S(2)}, u32[]{:S(2)}) collective-permute-start(bf16[96,512]{1,0:T(8,128)(2,1)S(1)} %get-tuple-element.54), channel_id=1, source_target_pairs={{0,6},{1,7},{2,0},{3,1},{4,2},{5,3},{6,4},{7,5},{8,14},{9,15},{10,... | collective-permute-start | bytes 294920 | tf_op jit(solution)/shard_map/ppermute | solution.py:510
  154.7 7.6 %collective-permute-start.13 = (bf16[96,512]{1,0:T(8,128)(2,1)S(1)}, bf16[96,512]{1,0:T(8,128)(2,1)S(1)}, u32[]{:S(2)}, u32[]{:S(2)}) collective-permute-start(bf16[96,512]{1,0:T(8,128)(2,1)S(1)} %add_convert_fusion.1), channel_id=1, source_target_pairs={{0,1},{1,0},{2,3},{3,2},{4,5},{5,4},{6,7},{7,6},{8,9},{9,8},{10,11... | collective-permute-start | bytes 294920 | tf_op jit(solution)/shard_map/ppermute | solution.py:544
  162.3 5.7 %collective-permute-start.16 = (bf16[96,512]{1,0:T(8,128)(2,1)S(1)}, bf16[96,512]{1,0:T(8,128)(2,1)S(1)}, u32[]{:S(2)}, u32[]{:S(2)}) collective-permute-start(bf16[96,512]{1,0:T(8,128)(2,1)S(1)} %add_convert_fusion.refs_0_), channel_id=1, source_target_pairs={{0,6},{1,7},{2,0},{3,1},{4,2},{5,3},{6,4},{7,5},{8,14},{9,15},{10,... | collective-permute-start | bytes 294920 | tf_op jit(solution)/shard_map/ppermute | solution.py:510
  165.4 5.1 %collective-permute-start.15 = (bf16[96,512]{1,0:T(8,128)(2,1)S(1)}, bf16[96,512]{1,0:T(8,128)(2,1)S(1)}, u32[]{:S(2)}, u32[]{:S(2)}) collective-permute-start(bf16[96,512]{1,0:T(8,128)(2,1)S(1)} %add_convert_fusion.refs_0_), channel_id=1, source_target_pairs={{0,4},{1,5},{2,6},{3,7},{4,0},{5,1},{6,2},{7,3},{8,12},{9,13},{10,... | collective-permute-start | bytes 294920 | tf_op jit(solution)/shard_map/ppermute | solution.py:510
  165.4 6.1 %collective-permute-start.14 = (bf16[96,512]{1,0:T(8,128)(2,1)S(1)}, bf16[96,512]{1,0:T(8,128)(2,1)S(1)}, u32[]{:S(2)}, u32[]{:S(2)}) collective-permute-start(bf16[96,512]{1,0:T(8,128)(2,1)S(1)} %add_convert_fusion.refs_0_), channel_id=1, source_target_pairs={{0,2},{1,3},{2,4},{3,5},{4,6},{5,7},{6,0},{7,1},{8,10},{9,11},{10,... | collective-permute-start | bytes 294920 | tf_op jit(solution)/shard_map/ppermute | solution.py:510
  172.1 4.4 %collective-permute-start.17 = (bf16[384,512]{1,0:T(8,128)(2,1)S(1)}, bf16[384,512]{1,0:T(8,128)(2,1)S(1)}, u32[]{:S(2)}, u32[]{:S(2)}) collective-permute-start(bf16[384,512]{1,0:T(8,128)(2,1)S(1)} %shard_map.142.ranks), channel_id=1, source_target_pairs={{0,8},{8,0},{16,24},{24,16},{32,40},{40,32},{48,56},{56,48},{64,72... | collective-permute-start | bytes 1179656 | tf_op jit(solution)/shard_map/ppermute | solution.py:540
  180.1 1.3 copy-start.2
  181.5 1.0 copy-start.8
  183.1 10.7 %collective-permute-start.18 = (bf16[2,16,2048]{2,1,0:T(8,128)(2,1)S(1)}, bf16[2,16,2048]{2,1,0:T(8,128)(2,1)S(1)}, u32[]{:S(2)}, u32[]{:S(2)}) collective-permute-start(bf16[2,16,2048]{2,1,0:T(8,128)(2,1)S(1)} %get-tuple-element.61), channel_id=1, source_target_pairs={{0,16},{8,24},{16,32},{24,40},{32,48},{40,56},{48,0},{56,8},{64,80... | collective-permute-start | bytes 393224 | tf_op jit(solution)/shard_map/ppermute | solution.py:510
  185.7 10.4 %collective-permute-start.19 = (bf16[2,16,2048]{2,1,0:T(8,128)(2,1)S(1)}, bf16[2,16,2048]{2,1,0:T(8,128)(2,1)S(1)}, u32[]{:S(2)}, u32[]{:S(2)}) collective-permute-start(bf16[2,16,2048]{2,1,0:T(8,128)(2,1)S(1)} %get-tuple-element.62), channel_id=1, source_target_pairs={{0,32},{8,40},{16,48},{24,56},{32,0},{40,8},{48,16},{56,24},{64,96... | collective-permute-start | bytes 393224 | tf_op jit(solution)/shard_map/ppermute | solution.py:510
  185.7 10.4 %collective-permute-start.20 = (bf16[2,16,2048]{2,1,0:T(8,128)(2,1)S(1)}, bf16[2,16,2048]{2,1,0:T(8,128)(2,1)S(1)}, u32[]{:S(2)}, u32[]{:S(2)}) collective-permute-start(bf16[2,16,2048]{2,1,0:T(8,128)(2,1)S(1)} %get-tuple-element.63), channel_id=1, source_target_pairs={{0,48},{8,56},{16,0},{24,8},{32,16},{40,24},{48,32},{56,40},{64,11... | collective-permute-start | bytes 393224 | tf_op jit(solution)/shard_map/ppermute | solution.py:510
  196.2 38.7 %all-to-all-start.1 = ((bf16[32,112,128]{2,1,0:T(8,128)(2,1)}), bf16[32,112,128]{2,1,0:T(8,128)(2,1)S(1)}, u32[]{:S(2)}, u32[]{:S(2)}) async-start(bf16[32,112,128]{2,1,0:T(8,128)(2,1)} %get-tuple-element.66), calls=%async_computation.3 | async-start | bytes 1835008 | tf_op jit(solution)/shard_map/all_to_all | solution.py:528
  217.0 1.0 copy-start.9
  218.7 20.8 %collective-permute-start.21 = (bf16[2,16,2048]{2,1,0:T(8,128)(2,1)S(1)}, bf16[2,16,2048]{2,1,0:T(8,128)(2,1)S(1)}, u32[]{:S(2)}, u32[]{:S(2)}) collective-permute-start(bf16[2,16,2048]{2,1,0:T(8,128)(2,1)S(1)} %get-tuple-element.71), channel_id=1, source_target_pairs={{0,16},{8,24},{16,32},{24,40},{32,48},{40,56},{48,0},{56,8},{64,80... | collective-permute-start | bytes 393224 | tf_op jit(solution)/shard_map/ppermute | solution.py:510
  219.7 19.8 %collective-permute-start.22 = (bf16[2,16,2048]{2,1,0:T(8,128)(2,1)S(1)}, bf16[2,16,2048]{2,1,0:T(8,128)(2,1)S(1)}, u32[]{:S(2)}, u32[]{:S(2)}) collective-permute-start(bf16[2,16,2048]{2,1,0:T(8,128)(2,1)S(1)} %get-tuple-element.72), channel_id=1, source_target_pairs={{0,32},{8,40},{16,48},{24,56},{32,0},{40,8},{48,16},{56,24},{64,96... | collective-permute-start | bytes 393224 | tf_op jit(solution)/shard_map/ppermute | solution.py:510
  223.4 16.2 %collective-permute-start.23 = (bf16[2,16,2048]{2,1,0:T(8,128)(2,1)S(1)}, bf16[2,16,2048]{2,1,0:T(8,128)(2,1)S(1)}, u32[]{:S(2)}, u32[]{:S(2)}) collective-permute-start(bf16[2,16,2048]{2,1,0:T(8,128)(2,1)S(1)} %get-tuple-element.73), channel_id=1, source_target_pairs={{0,48},{8,56},{16,0},{24,8},{32,16},{40,24},{48,32},{56,40},{64,11... | collective-permute-start | bytes 393224 | tf_op jit(solution)/shard_map/ppermute | solution.py:510
Sparse Core Ops, SparseCore 0:
  10.4 87.3 all-gather.1
  146.8 27.7 reduce-scatter.2
  181.6 35.4 reduce-scatter.4
